TPU v7x, 32 devices: a whole 2x2x4 slice. The times are simulated.
32 devices in a mesh: dp: 4 (over y, x), sp: 8 (over z, core).
Axes of the slice: x: 2, y: 2, z: 4, core: 2. Of those that a mesh axis runs over, the one named last changes fastest.
Arguments:
- hidden_in: bfloat16 [8, 1024, 1536], P('dp', 'sp'), may hold values from -6 to 6
- w_zx: bfloat16 [1536, 6144], P(('dp', 'sp')), may hold values from -0.15625 to 0.15625
- w_bc: bfloat16 [1536, 256], P(('dp', 'sp')), may hold values from -0.15625 to 0.15625
- w_dt: bfloat16 [1536, 48], P(('dp', 'sp')), may hold values from -0.15625 to 0.15625
- norm_gain: bfloat16 [1536], P(('dp', 'sp')), may hold values from 0.5 to 1.5
- conv_bc_weight: bfloat16 [256, 4], P(('dp', 'sp')), may hold values from -3 to 3
- conv_bc_bias: bfloat16 [256], P(('dp', 'sp')), may hold values from -3 to 3
- conv_x_weight: bfloat16 [3072, 4], P('sp'), may hold values from -3 to 3
- conv_x_bias: bfloat16 [3072], P('sp'), may hold values from -3 to 3
- dt_bias: bfloat16 [48], P('sp'), may hold values from -5 to -2.296875
- a_log: bfloat16 [48], P('sp'), may hold values from 0 to 2.796875
- d_skip: bfloat16 [48], P('sp'), may hold values from 0.5 to 1.5
- gate_gain: bfloat16 [3072], P(('dp', 'sp')), may hold values from 0.5 to 1.5
- w_out: bfloat16 [3072, 1536], P(('dp', 'sp')), may hold values from -0.109375 to 0.109375
- cotangent: bfloat16 [8, 1024, 1536], P('dp', 'sp'), may hold values from -6 to 6
Outputs:
- hidden_out: bfloat16 [8, 1024, 1536], P('dp', 'sp')
- grad_hidden: bfloat16 [8, 1024, 1536], P('dp', 'sp')
- grad_w_zx: float32 [1536, 6144], P(('dp', 'sp'))
- grad_w_bc: float32 [1536, 256], P(('dp', 'sp'))
- grad_w_dt: float32 [1536, 48], P(('dp', 'sp'))
- grad_norm_gain: float32 [1536], P(('dp', 'sp'))
- grad_conv_bc_weight: float32 [256, 4], P(('dp', 'sp'))
- grad_conv_bc_bias: float32 [256], P(('dp', 'sp'))
- grad_conv_x_weight: float32 [3072, 4], P('sp')
- grad_conv_x_bias: float32 [3072], P('sp')
- grad_dt_bias: float32 [48], P('sp')
- grad_a_log: float32 [48], P('sp')
- grad_d_skip: float32 [48], P('sp')
- grad_gate_gain: float32 [3072], P(('dp', 'sp'))
- grad_w_out: float32 [3072, 1536], P(('dp', 'sp'))
All inputs are finite; a program needn't handle non-finite values.
Results may differ from a plain program's by a relative error of at most 0.009.
The roundings to bfloat16 on the way count: a program that leaves them out, or rounds other values in their place, can miss the bound.
Values may be sent and summed in bfloat16 or wider, within the bound.
A program may use at most 256 MiB of HBM per device.

v0:
```python
import jax
import jax.numpy as jnp
from jax import lax
from jax.sharding import PartitionSpec as P

H = 48
P_SIZE = 64
N = 128
SPAN = 256


EPS = 1e-05
HIGH = lax.Precision.HIGHEST


def rounded(value):
    return lax.optimization_barrier(value.astype(jnp.bfloat16)).astype(jnp.float32)


def contract_rows(left, right):
    return lax.dot_general(
        left, right, (((0,), (0,)), ((), ())), preferred_element_type=jnp.float32
    )


def contract_cols(left, right):
    return lax.dot_general(
        left, right, (((1,), (1,)), ((), ())), preferred_element_type=jnp.float32
    )


def norm_back(grad_out, unit, gain, scale):
    weighted = grad_out * gain
    return scale * (weighted - unit * jnp.mean(weighted * unit, axis=-1, keepdims=True))


def conv_silu(values, weight, bias):
    taps = weight.shape[1]
    length = values.shape[0]
    padded = jnp.pad(values, ((taps - 1, 0), (0, 0)))
    total = bias[None, :]
    for offset in range(taps):
        total = total + weight[:, offset][None, :] * padded[offset : offset + length, :]
    return jax.nn.silu(total)


def scan_heads(heads_x, steps, rates, bmat, cmat):
    length, heads, width = heads_x.shape
    count = length // SPAN
    states_n = bmat.shape[-1]
    x_blocks = heads_x.reshape(count, SPAN, heads, width)
    dt_blocks = steps.reshape(count, SPAN, heads)
    logs = dt_blocks * (-rates)[None, None, :]
    b_blocks = bmat.reshape(count, SPAN, states_n)
    c_blocks = cmat.reshape(count, SPAN, states_n)
    cumul = jnp.cumsum(logs, axis=1)
    cumul_heads = jnp.transpose(cumul, (0, 2, 1))
    dt_heads = jnp.transpose(dt_blocks, (0, 2, 1))
    differ = cumul_heads[:, :, :, None] - cumul_heads[:, :, None, :]
    causal = jnp.tril(jnp.ones((SPAN, SPAN), dtype=bool))
    decays = jnp.where(causal[None, None, :, :], jnp.exp(jnp.minimum(differ, 0.0)), 0.0)
    scores = jnp.einsum("cin,cjn->cij", c_blocks, b_blocks, precision=HIGH)
    weights = scores[:, None, :, :] * decays * dt_heads[:, :, None, :]
    inside = jnp.einsum("chij,cjhp->cihp", weights, x_blocks, precision=HIGH)
    to_end = jnp.exp(cumul[:, -1:, :] - cumul) * dt_blocks
    states = jnp.einsum("cjn,cjh,cjhp->chnp", b_blocks, to_end, x_blocks, precision=HIGH)
    factors = jnp.exp(cumul[:, -1, :])

    def advance(carry, pieces):
        state, factor = pieces
        return (carry * factor[:, None, None] + state, carry)

    start = jnp.zeros((heads, states_n, width), dtype=jnp.float32)
    _, entering = lax.scan(advance, start, (states, factors))
    across = jnp.einsum("cin,cih,chnp->cihp", c_blocks, jnp.exp(cumul), entering, precision=HIGH)
    return (inside + across).reshape(length, heads, width)


def convolve(x_input, bc_input, x_weight, x_bias, bc_weight, bc_bias):
    return (conv_silu(x_input, x_weight, x_bias), conv_silu(bc_input, bc_weight, bc_bias))


def mixer(x_conv, bc_conv, dt_input, step_bias, log_rates, skip_coef):
    length = x_conv.shape[0]
    heads_x = x_conv.reshape(length, -1, P_SIZE)
    steps = jax.nn.softplus(dt_input + step_bias[None, :])
    mixed = scan_heads(heads_x, steps, jnp.exp(log_rates), bc_conv[:, :N], bc_conv[:, N:])
    mixed = mixed + skip_coef[None, :, None] * heads_x
    return mixed.reshape(length, -1)


def column_sum(values):
    return jnp.sum(values, axis=0)


def on_device(
    hidden_in,
    w_zx,
    w_bc,
    w_dt,
    norm_gain,
    conv_bc_weight,
    conv_bc_bias,
    conv_x_weight,
    conv_x_bias,
    dt_bias,
    a_log,
    d_skip,
    gate_gain,
    w_out,
    cotangent,
):
    seqs, block, width = hidden_in.shape
    rows = seqs * block
    inner = H * P_SIZE
    zx_full, bc_full, dt_full, gain_full, bc_taps, bc_offsets = (
        lax.all_gather(w_zx, ("dp", "sp"), axis=0, tiled=True),
        lax.all_gather(w_bc, ("dp", "sp"), axis=0, tiled=True),
        lax.all_gather(w_dt, ("dp", "sp"), axis=0, tiled=True),
        lax.all_gather(norm_gain, ("dp", "sp"), axis=0, tiled=True),
        lax.all_gather(conv_bc_weight, ("dp", "sp"), axis=0, tiled=True),
        lax.all_gather(conv_bc_bias, ("dp", "sp"), axis=0, tiled=True),
    )
    hidden = hidden_in.reshape(rows, width).astype(jnp.float32)
    scale_in = lax.rsqrt(jnp.mean(hidden * hidden, axis=-1, keepdims=True) + EPS)
    unit_in = hidden * scale_in
    normed = (unit_in * gain_full.astype(jnp.float32)).astype(jnp.bfloat16)
    proj_zx = jnp.dot(normed, zx_full, preferred_element_type=jnp.float32)
    gate = proj_zx[:, :inner].astype(jnp.bfloat16)
    inner_x = proj_zx[:, inner:].astype(jnp.bfloat16)
    bc_proj = jnp.dot(normed, bc_full, preferred_element_type=jnp.float32).astype(jnp.bfloat16)
    dt_raw = jnp.dot(normed, dt_full, preferred_element_type=jnp.float32).astype(jnp.bfloat16)
    x_heads, dt_heads = (
        lax.all_to_all(
            inner_x.reshape(seqs, block, inner), "sp", split_axis=2, concat_axis=1, tiled=True
        ),
        lax.all_to_all(
            dt_raw.reshape(seqs, block, H), "sp", split_axis=2, concat_axis=1, tiled=True
        ),
    )
    bc_whole = lax.all_gather(bc_proj.reshape(seqs, block, 2 * N), "sp", axis=1, tiled=True)
    x_taps = conv_x_weight.astype(jnp.float32)
    x_offsets = conv_x_bias.astype(jnp.float32)
    bc_taps_f = bc_taps.astype(jnp.float32)
    bc_offsets_f = bc_offsets.astype(jnp.float32)
    step_bias = dt_bias.astype(jnp.float32)
    log_rates = a_log.astype(jnp.float32)
    skip_coef = d_skip.astype(jnp.float32)

    def forward_single(pieces):
        x_input, bc_input, dt_input = pieces
        x_conv, bc_conv = convolve(
            x_input.astype(jnp.float32),
            bc_input.astype(jnp.float32),
            x_taps,
            x_offsets,
            bc_taps_f,
            bc_offsets_f,
        )
        mixed = mixer(
            rounded(x_conv),
            rounded(bc_conv),
            dt_input.astype(jnp.float32),
            step_bias,
            log_rates,
            skip_coef,
        )
        return mixed.astype(jnp.bfloat16)

    mixed_heads = lax.map(forward_single, (x_heads, bc_whole, dt_heads))
    mixed_tok = lax.all_to_all(mixed_heads, "sp", split_axis=1, concat_axis=2, tiled=True)
    wout_full, ggain_full = (
        lax.all_gather(w_out, ("dp", "sp"), axis=0, tiled=True),
        lax.all_gather(gate_gain, ("dp", "sp"), axis=0, tiled=True),
    )
    mixed = mixed_tok.reshape(rows, inner).astype(jnp.float32)
    gate_f = gate.astype(jnp.float32)
    sigmoid_gate = jax.nn.sigmoid(gate_f)
    silu_gate = gate_f * sigmoid_gate
    gated_in = mixed * silu_gate
    scale_out = lax.rsqrt(jnp.mean(gated_in * gated_in, axis=-1, keepdims=True) + EPS)
    unit_out = gated_in * scale_out
    gated = (unit_out * ggain_full.astype(jnp.float32)).astype(jnp.bfloat16)
    output = hidden + jnp.dot(gated, wout_full, preferred_element_type=jnp.float32)
    hidden_out = output.astype(jnp.bfloat16).reshape(seqs, block, width)
    grad_out = cotangent.reshape(rows, width)
    d_gated = contract_cols(grad_out, wout_full)
    wout_terms = contract_rows(gated, grad_out)
    ggain_terms = jnp.sum(d_gated * unit_out, axis=0)
    d_gated_in = norm_back(d_gated, unit_out, ggain_full.astype(jnp.float32), scale_out)
    d_mixed = (d_gated_in * silu_gate).astype(jnp.bfloat16)
    d_gate = (d_gated_in * mixed * sigmoid_gate * (1.0 + gate_f * (1.0 - sigmoid_gate))).astype(
        jnp.bfloat16
    )
    grad_w_out, grad_gate_gain = (
        lax.psum_scatter(wout_terms, ("dp", "sp"), scatter_dimension=0, tiled=True),
        lax.psum_scatter(ggain_terms, ("dp", "sp"), scatter_dimension=0, tiled=True),
    )
    dy_heads = lax.all_to_all(
        d_mixed.reshape(seqs, block, inner), "sp", split_axis=2, concat_axis=1, tiled=True
    )

    def backward_single(pieces):
        x_input, bc_input, dt_input, dy_input = pieces
        conv_values, conv_pull = jax.vjp(
            convolve,
            x_input.astype(jnp.float32),
            bc_input.astype(jnp.float32),
            x_taps,
            x_offsets,
            bc_taps_f,
            bc_offsets_f,
        )
        _, mix_pull = jax.vjp(
            mixer,
            rounded(conv_values[0]),
            rounded(conv_values[1]),
            dt_input.astype(jnp.float32),
            step_bias,
            log_rates,
            skip_coef,
        )
        d_xconv, d_bcconv, d_dtin, g_bias, g_rates, g_skip = mix_pull(dy_input.astype(jnp.float32))
        d_xin, d_bcin, g_xtaps, g_xoff, g_bctaps, g_bcoff = conv_pull((d_xconv, d_bcconv))
        return (
            d_xin.astype(jnp.bfloat16),
            d_dtin.astype(jnp.bfloat16),
            d_bcin,
            (g_xtaps, g_xoff, g_bctaps, g_bcoff, g_bias, g_rates, g_skip),
        )

    dx_heads, ddt_heads, dbc_heads, param_terms = lax.map(
        backward_single, (x_heads, bc_whole, dt_heads, dy_heads)
    )
    g_xtaps, g_xoff, g_bctaps, g_bcoff, g_bias, g_rates, g_skip = jax.tree.map(
        column_sum, param_terms
    )
    dx_tok, ddt_tok = (
        lax.all_to_all(dx_heads, "sp", split_axis=1, concat_axis=2, tiled=True),
        lax.all_to_all(ddt_heads, "sp", split_axis=1, concat_axis=2, tiled=True),
    )
    dbc_tok = lax.psum_scatter(dbc_heads, "sp", scatter_dimension=1, tiled=True).astype(
        jnp.bfloat16
    )
    grad_conv_x_weight, grad_conv_x_bias, grad_dt_bias, grad_a_log, grad_d_skip = lax.psum(
        (g_xtaps, g_xoff, g_bias, g_rates, g_skip), "dp"
    )
    dx_rows = dx_tok.reshape(rows, inner)
    d_proj_zx = jnp.concatenate([d_gate, dx_rows], axis=1)
    d_proj_bc = dbc_tok.reshape(rows, 2 * N)
    d_proj_dt = ddt_tok.reshape(rows, H)
    d_normed = contract_cols(d_proj_zx, zx_full) + contract_cols(d_proj_bc, bc_full)
    d_normed = d_normed + contract_cols(d_proj_dt, dt_full)
    bc_terms = contract_rows(normed, d_proj_bc)
    dt_terms = contract_rows(normed, d_proj_dt)
    gain_terms = jnp.sum(d_normed * unit_in, axis=0)
    grad_input = grad_out.astype(jnp.float32) + norm_back(
        d_normed, unit_in, gain_full.astype(jnp.float32), scale_in
    )
    grad_hidden = grad_input.astype(jnp.bfloat16).reshape(seqs, block, width)
    first_terms = contract_rows(normed, d_proj_zx)
    summed_first, grad_w_bc, grad_w_dt, grad_norm_gain, grad_conv_bc_weight, grad_conv_bc_bias = (
        lax.psum_scatter(first_terms, ("dp", "sp"), scatter_dimension=0, tiled=True),
        lax.psum_scatter(bc_terms, ("dp", "sp"), scatter_dimension=0, tiled=True),
        lax.psum_scatter(dt_terms, ("dp", "sp"), scatter_dimension=0, tiled=True),
        lax.psum_scatter(gain_terms, ("dp", "sp"), scatter_dimension=0, tiled=True),
        lax.psum_scatter(g_bctaps, ("dp", "sp"), scatter_dimension=0, tiled=True),
        lax.psum_scatter(g_bcoff, ("dp", "sp"), scatter_dimension=0, tiled=True),
    )
    return (
        hidden_out,
        grad_hidden,
        summed_first,
        grad_w_bc,
        grad_w_dt,
        grad_norm_gain,
        grad_conv_bc_weight,
        grad_conv_bc_bias,
        grad_conv_x_weight,
        grad_conv_x_bias,
        grad_dt_bias,
        grad_a_log,
        grad_d_skip,
        grad_gate_gain,
        grad_w_out,
    )


def solution(mesh):
    return jax.shard_map(
        on_device,
        mesh=mesh,
        in_specs=(
            P("dp", "sp", None),
            P(("dp", "sp"), None),
            P(("dp", "sp"), None),
            P(("dp", "sp"), None),
            P(("dp", "sp")),
            P(("dp", "sp"), None),
            P(("dp", "sp")),
            P("sp", None),
            P("sp"),
            P("sp"),
            P("sp"),
            P("sp"),
            P(("dp", "sp")),
            P(("dp", "sp"), None),
            P("dp", "sp", None),
        ),
        out_specs=(
            P("dp", "sp", None),
            P("dp", "sp", None),
            P(("dp", "sp"), None),
            P(("dp", "sp"), None),
            P(("dp", "sp"), None),
            P(("dp", "sp")),
            P(("dp", "sp"), None),
            P(("dp", "sp")),
            P("sp", None),
            P("sp"),
            P("sp"),
            P("sp"),
            P("sp"),
            P(("dp", "sp")),
            P(("dp", "sp"), None),
        ),
        check_vma=False,
    )
```

profile of v0, /device:TPU:0, one launch (start us, length us, event | category | flops | bytes accessed | tf_op | source)
XLA Modules:
  0.0 1570.5 jit_solution(214375686654192271)
XLA Ops:
  11.3 43.0 %all-reduce.33 = (bf16[1536]{0:T(1024)(128)(2,1)S(1)}, bf16[256]{0:T(256)(128)(2,1)S(1)}, bf16[3072]{0:T(1024)(128)(2,1)}) all-reduce(bf16[1536]{0:T(1024)(128)(2,1)S(1)} %dynamic-update-slice, bf16[256]{0:T(256)(128)(2,1)S(1)} %dynamic-update-slice.1, bf16[3072]{0:T(1024)(128)(2,1)S(1)} %dynamic-update-slice.2), channel_id=1, replica_groups=mesh['dp'=4,'sp'=8] {'dp','sp'}, use_global_device_ids=true, to_apply=%add.24 | all-reduce | flops 4864 | bytes 19456
  54.3 44.3 %all_gather.33 = bf16[1536,48]{1,0:T(8,128)(2,1)S(1)} all-gather(bf16[48,48]{1,0:T(8,128)(2,1)} %param.28), channel_id=1, replica_groups=mesh['dp'=4,'sp'=8] {'dp','sp'}, dimensions={0}, use_global_device_ids=true | all-gather | bytes 152064 | tf_op jit(solution)/shard_map/all_gather | solution.py:119
  101.0 3.3 all-to-all-start.1
  104.3 37.8 %all-gather.5.cloned.1.call-done = bf16[1536,6144]{1,0:T(8,128)(2,1)} async-done(((bf16[48,6144]{1,0:T(8,128)(2,1)}), bf16[1536,6144]{1,0:T(8,128)(2,1)}) %all-gather.5.cloned.1.call-update) | async-done | bytes 18874384 | tf_op jit(solution)/shard_map/all_gather | solution.py:117
  142.1 11.6 convolution_convert_fusion
  155.4 2.9 copy.457
  158.3 3.7 all-to-all-start
  162.2 70.9 %all_gather.31 = bf16[1536,256]{1,0:T(8,128)(2,1)S(1)} all-gather(bf16[48,256]{1,0:T(8,128)(2,1)S(1)} %copy-done.114), channel_id=1, replica_groups=mesh['dp'=4,'sp'=8] {'dp','sp'}, dimensions={0}, use_global_device_ids=true | all-gather | bytes 811008 | tf_op jit(solution)/shard_map/all_gather | solution.py:118
  236.5 36.7 %all-gather = bf16[32,8,4]{1,2,0:T(4,128)(2,1)S(1)} all-gather(bf16[1,8,4]{1,2,0:T(4,128)(2,1)S(1)} %bitcast.618), channel_id=1, replica_groups=mesh['dp'=4,'sp'=8] {'dp','sp'}, dimensions={0}, use_global_device_ids=true | all-gather | bytes 2112 | tf_op jit(solution)/shard_map/all_gather | solution.py:121
  277.8 102.1 %while.133 = (s32[]{:T(128)}, bf16[2,1024,384]{1,2,0:T(8,128)(2,1)}, f32[384]{0:T(512)}, f32[384,4]{0,1:T(4,128)S(1)}, bf16[2,1024,384]{1,2,0:T(8,128)(2,1)S(1)}...) while((s32[]{:T(128)}, bf16[2,1024,384]{1,2,0:T(8,128)(2,1)}, ...), condition=%wide.region_6.7_spmd, body=%wide.region_1.6_spmd.sunk | while | flops 2504323072 | bytes 64241048 | solution.py:170
  280.8 7.2 reduce-window.70
  302.1 15.7 %while.137 = (s32[]{:T(128)}, f32[6,128,64]{2,1,0:T(8,128)S(1)}, f32[4,6,128,64]{2,3,1,0:T(8,128)}, f32[4,6]{1,0:T(4,128)}, f32[4,6,128,64]{2,3,1,0:T(8,128)}, /*index=5*/s32[]{:T(128)}, s32[]{:T(128)}) while((s32[]{:T(128)}, f32[6,128,64]{2,1,0:T(8,128)S(1)}, f32[4,6,128,64]{2,3,1,0:T(8,128)}, f32[4,6]{1,0:T(4,128)}, ...), condition=%wide.region_5.5_spmd.clone, body=%wide.region_4.4_spmd.clone.sunk | while | flops 147459 | bytes 2359475 | solution.py:74
  320.1 4.9 bitcast_add_fusion.9
  331.7 7.2 reduce-window.70
  353.0 15.7 %while.137 = (s32[]{:T(128)}, f32[6,128,64]{2,1,0:T(8,128)S(1)}, f32[4,6,128,64]{2,3,1,0:T(8,128)}, f32[4,6]{1,0:T(4,128)}, f32[4,6,128,64]{2,3,1,0:T(8,128)}, /*index=5*/s32[]{:T(128)}, s32[]{:T(128)}) while((s32[]{:T(128)}, f32[6,128,64]{2,1,0:T(8,128)S(1)}, f32[4,6,128,64]{2,3,1,0:T(8,128)}, f32[4,6]{1,0:T(4,128)}, ...), condition=%wide.region_5.5_spmd.clone, body=%wide.region_4.4_spmd.clone.sunk | while | flops 147459 | bytes 2359475 | solution.py:74
  371.0 4.9 bitcast_add_fusion.9
  379.9 5.0 copy.463
  384.9 3.7 all-to-all-start.2
  388.7 37.7 %all-to-all-done.2 = bf16[2,1024,384]{2,0,1:T(2,128)(2,1)S(1)} async-done(((bf16[2,1024,384]{2,0,1:T(2,128)(2,1)}), bf16[2,1024,384]{2,0,1:T(2,128)(2,1)S(1)}, u32[]{:S(2)}, u32[]{:S(2)}) %all-to-all-start.2) | async-done | bytes 1572896 | tf_op jit(solution)/shard_map/all_to_all | solution.py:171
  430.1 2.8 multiply_reduce_fusion.12
  432.9 8.2 multiply_reduce_fusion.10
  441.1 3.3 fusion.129
  444.4 2.9 copy.465
  447.2 3.6 all-to-all-start.3
  451.0 37.6 %all-to-all-done.3 = bf16[2,128,3072]{1,0,2:T(2,128)(2,1)S(1)} async-done(((bf16[2,128,3072]{1,0,2:T(2,128)(2,1)}), bf16[2,128,3072]{1,0,2:T(2,128)(2,1)S(1)}, u32[]{:S(2)}, u32[]{:S(2)}) %all-to-all-start.3) | async-done | bytes 1572896 | tf_op jit(solution)/shard_map/all_to_all | solution.py:199
  488.6 2.2 copy.466
  490.8 3.7 all_to_all.80
  495.9 264.7 %while.136 = (s32[]{:T(128)}, bf16[2,1024,384]{1,2,0:T(8,128)(2,1)}, bf16[2,1024,6]{1,2,0:T(8,128)(2,1)}, f32[2,1024,256]{2,1,0:T(8,128)}, f32[2,384,4]{1,2,0:T(...) while((s32[]{:T(128)}, bf16[2,1024,384]{1,2,0:T(8,128)(2,1)}, ...), condition=%wide.region_38.39_spmd, body=%wide.region_9.38_spmd.sunk | while | flops 5981070336 | bytes 223539184 | solution.py:232
  499.7 7.2 reduce-window.73
  516.9 2.7 multiply_convert_fusion.16
  526.2 5.3 while.138
  532.9 5.9 fusion.306
  542.1 8.7 while.139
  551.0 6.9 fusion.305
  560.9 4.2 bitcast_add_fusion.10
  565.1 6.3 fusion.300
  578.3 4.0 multiply_reduce_fusion.21
  585.2 30.2 %reduce-window.74 = f32[4,6,2,128]{3,2,1,0:T(2,128)S(1)} reduce-window(f32[4,6,2,128]{3,2,1,0:T(2,128)S(1)} %reshape.667, f32[]{:T(128)} %constant.242.clone.1..sunk.1), window={size=1x1x1x128 pad=0_0x0_0x0_0x0_127}, to_apply=%region_21.21 | reduce-window | flops 780288 | bytes 49156 | tf_op jit(solution)/shard_map/reduce-window.34
  628.3 7.2 reduce-window.73
  645.5 2.7 multiply_convert_fusion.16
  654.5 5.3 while.138
  661.2 5.9 fusion.306
  670.4 8.7 while.139
  679.3 6.9 fusion.305
  689.2 4.2 bitcast_add_fusion.10
  693.4 6.4 fusion.300
  706.6 4.0 multiply_reduce_fusion.21
  713.5 30.2 %reduce-window.74 = f32[4,6,2,128]{3,2,1,0:T(2,128)S(1)} reduce-window(f32[4,6,2,128]{3,2,1,0:T(2,128)S(1)} %reshape.667, f32[]{:T(128)} %constant.242.clone.1..sunk.1), window={size=1x1x1x128 pad=0_0x0_0x0_0x0_127}, to_apply=%region_21.21 | reduce-window | flops 780288 | bytes 49156 | tf_op jit(solution)/shard_map/reduce-window.34
  763.2 3.3 all-to-all-start.5
  766.9 5.6 all-to-all-done.5
  775.9 18.3 %reduce-scatter.7.cloned.1.call-done = f32[2,128,256]{2,1,0:T(8,128)} async-done(((f32[2,1024,256]{2,1,0:T(8,128)}), f32[2,128,256]{2,1,0:T(8,128)}) %reduce-scatter.7.cloned.1.call-update) | async-done | bytes 262160 | tf_op jit(solution)/shard_map/reduce_scatter | solution.py:242
  795.8 2.9 convolution_bitcast_fusion
  798.8 9.1 fusion.144
  808.0 5.0 copy.468
  813.0 42.6 %all_to_all.93 = bf16[2,1024,384]{2,0,1:T(2,128)(2,1)S(1)} all-to-all(bf16[2,1024,384]{2,0,1:T(2,128)(2,1)} %copy.468), channel_id=1, replica_groups=mesh['dp'=4,'sp'=8] {'sp'}, dimensions={1} | all-to-all | bytes 3145728 | tf_op jit(solution)/shard_map/all_to_all | solution.py:239
  858.8 14.9 fusion.132
  873.8 7.4 fusion.131
  886.2 11.7 all-reduce.32
  897.9 2.3 fusion.136
  902.4 10.9 multiply_reduce_fusion.13
  913.3 37.5 %all-reduce.31 = (f32[1536]{0:T(1024)S(1)}, f32[256,4]{0,1:T(4,128)S(1)}, f32[256]{0:T(256)S(1)}, f32[3072]{0:T(1024)S(1)}) all-reduce(f32[1536]{0:T(1024)S(1)} %get-tuple-element.1294, f32[256,4]{0,1:T(4,128)S(1)} %reduce_sum.485, f32[256]{0:T(256)S(1)} %reduce_sum.486, ...), channel_id=6, replica_groups=mesh['dp'=4,'sp'=8] {'dp','sp'}, use_global_device_ids=true, to_apply=%region_45.46.clone | all-reduce | flops 5888 | bytes 47104
  954.6 42.3 %reduce-scatter.11.cloned.1.call-done = f32[48,256]{1,0:T(8,128)} async-done(((f32[1536,256]{1,0:T(8,128)}), f32[48,256]{1,0:T(8,128)}) %reduce-scatter.11.cloned.1.call-update) | async-done | bytes 49168 | tf_op jit(solution)/shard_map/reduce_scatter | solution.py:264
  996.9 212.2 %reduce-scatter.15.cloned.1.call-done = f32[96,1536]{1,0:T(8,128)} async-done(((f32[3072,1536]{1,0:T(8,128)}), f32[96,1536]{1,0:T(8,128)}) %reduce-scatter.15.cloned.1.call-update) | async-done | bytes 589840 | tf_op jit(solution)/shard_map/reduce_scatter | solution.py:196
  1209.1 353.6 %reduce-scatter.9.cloned.1.call-done = f32[48,6144]{1,0:T(8,128)} async-done(((f32[1536,6144]{1,0:T(8,128)}), f32[48,6144]{1,0:T(8,128)}) %reduce-scatter.9.cloned.1.call-update) | async-done | bytes 1179664 | tf_op jit(solution)/shard_map/reduce_scatter | solution.py:263
  (952 shorter events, 237.4 us)
Async XLA Ops:
  8.0 90.6 %copy-start.36 = (bf16[2,128,1536]{2,1,0:T(8,128)(2,1)S(1)}, bf16[2,128,1536]{2,1,0:T(8,128)(2,1)}, u32[]{:S(2)}) copy-start(bf16[2,128,1536]{2,1,0:T(8,128)(2,1)} %param.25) | copy-start | bytes 2359300
  8.0 134.1 %all-gather.5.cloned.1.call-start = ((), (), s32[]{:S(2)}) async-start(), calls=%async_computation.11 | async-start | bytes 19464192 | tf_op jit(solution)/shard_map/all_gather | solution.py:117
  54.3 45.4 %copy-start.95 = (f32[1536]{0:T(1024)}, f32[1536]{0:T(1024)S(1)}, u32[]{:S(2)}) copy-start(f32[1536]{0:T(1024)S(1)} %convert_element_type.272) | copy-start | bytes 18436
  100.0 133.1 %copy-start.39 = (bf16[256,1536]{1,0:T(8,128)(2,1)}, bf16[256,1536]{1,0:T(8,128)(2,1)S(1)}, u32[]{:S(2)}) copy-start(bf16[256,1536]{1,0:T(8,128)(2,1)S(1)} %multiply_convert_fusion.7) | copy-start | bytes 2359300
  101.0 57.3 %all-to-all-start.1 = ((bf16[2,128,48]{1,0,2:T(2,128)(2,1)}), bf16[2,128,48]{1,0,2:T(2,128)(2,1)S(1)}, u32[]{:S(2)}, u32[]{:S(2)}) async-start(bf16[2,128,48]{1,0,2:T(2,128)(2,1)} %reshape.591), calls=%async_computation.1 | async-start | bytes 49152 | tf_op jit(solution)/shard_map/all_to_all | solution.py:137
  158.3 116.3 %all-to-all-start = ((bf16[2,128,3072]{1,0,2:T(2,128)(2,1)}), bf16[2,128,3072]{1,0,2:T(2,128)(2,1)S(1)}, u32[]{:S(2)}, u32[]{:S(2)}) async-start(bf16[2,128,3072]{1,0,2:T(2,128)(2,1)} %copy.457), calls=%async_computation | async-start | bytes 3145728 | tf_op jit(solution)/shard_map/all_to_all | solution.py:134
  162.0 72.7 %copy-start.139 = (bf16[6]{0:T(256)(128)(2,1)S(1)}, bf16[6]{0:T(256)(128)(2,1)}, u32[]{:S(2)}) copy-start(bf16[6]{0:T(256)(128)(2,1)} %param.34) | copy-start | bytes 40
  162.1 72.7 %copy-start.140 = (bf16[6]{0:T(256)(128)(2,1)S(1)}, bf16[6]{0:T(256)(128)(2,1)}, u32[]{:S(2)}) copy-start(bf16[6]{0:T(256)(128)(2,1)} %param.36) | copy-start | bytes 40
  162.1 73.2 %copy-start.131 = (bf16[384]{0:T(512)(128)(2,1)S(1)}, bf16[384]{0:T(512)(128)(2,1)}, u32[]{:S(2)}) copy-start(bf16[384]{0:T(512)(128)(2,1)} %param.33) | copy-start | bytes 2308
  162.1 73.8 %copy-start.126 = (bf16[384,4]{0,1:T(4,128)(2,1)S(1)}, bf16[384,4]{0,1:T(4,128)(2,1)}, u32[]{:S(2)}) copy-start(bf16[384,4]{0,1:T(4,128)(2,1)} %param.32) | copy-start | bytes 9220
  162.1 74.4 %copy-start.132 = (bf16[8,4]{0,1:T(4,128)(2,1)S(1)}, bf16[8,4]{0,1:T(4,128)(2,1)}, u32[]{:S(2)}) copy-start(bf16[8,4]{0,1:T(4,128)(2,1)} %param.30) | copy-start | bytes 196
  162.1 111.3 %copy-start.141 = (bf16[6]{0:T(256)(128)(2,1)S(1)}, bf16[6]{0:T(256)(128)(2,1)}, u32[]{:S(2)}) copy-start(bf16[6]{0:T(256)(128)(2,1)} %param.35) | copy-start | bytes 40
  162.1 114.3 %all-gather.7.cloned.1.call-start = ((), (), s32[]{:S(2)}) async-start(), calls=%async_computation.12 | async-start | bytes 1179648 | tf_op jit(solution)/shard_map/all_gather | solution.py:141
  234.1 198.7 %all-gather.9.cloned.1.call-start = ((), (), s32[]{:S(2)}) async-start(), calls=%async_computation.13 | async-start | bytes 9732096 | tf_op jit(solution)/shard_map/all_gather | solution.py:173
  384.9 41.5 %all-to-all-start.2 = ((bf16[2,1024,384]{2,0,1:T(2,128)(2,1)}), bf16[2,1024,384]{2,0,1:T(2,128)(2,1)S(1)}, u32[]{:S(2)}, u32[]{:S(2)}) async-start(bf16[2,1024,384]{2,0,1:T(2,128)(2,1)} %copy.463), calls=%async_computation.2 | async-start | bytes 3145728 | tf_op jit(solution)/shard_map/all_to_all | solution.py:171
  388.7 52.4 %copy-start.93 = (f32[3072]{0:T(1024)}, f32[3072]{0:T(1024)S(1)}, u32[]{:S(2)}) copy-start(f32[3072]{0:T(1024)S(1)} %convert_element_type.286) | copy-start | bytes 36868
  447.2 41.3 %all-to-all-start.3 = ((bf16[2,128,3072]{1,0,2:T(2,128)(2,1)}), bf16[2,128,3072]{1,0,2:T(2,128)(2,1)S(1)}, u32[]{:S(2)}, u32[]{:S(2)}) async-start(bf16[2,128,3072]{1,0,2:T(2,128)(2,1)} %copy.465), calls=%async_computation.3 | async-start | bytes 3145728 | tf_op jit(solution)/shard_map/all_to_all | solution.py:199
  450.8 343.3 %reduce-scatter.7.cloned.1.call-start = ((), (), s32[]{:S(2)}) async-start(), calls=%async_computation.14 | async-start | bytes 2359296 | tf_op jit(solution)/shard_map/reduce_scatter | solution.py:242
  496.1 11.3 copy-start.70
  496.1 13.5 copy-start.15
  497.5 15.5 copy-start.78
  497.5 15.5 copy-start.80
  497.5 15.5 copy-start.82
  497.5 15.5 copy-start.84
  498.9 14.2 copy-start.28
  583.4 32.4 %copy-start.100 = (f32[1,1,6]{2,1,0:T(1,128)S(1)}, f32[1,1,6]{2,1,0:T(1,128)}, u32[]{:S(2)}) copy-start(f32[1,1,6]{2,1,0:T(1,128)} %get-tuple-element.2170) | copy-start | bytes 76 | tf_op jit(solution)/shard_map/while
  583.4 32.6 %copy-start.60 = (bf16[2,1024,6]{1,2,0:T(8,128)(2,1)S(1)}, bf16[2,1024,6]{1,2,0:T(8,128)(2,1)}, u32[]{:S(2)}) copy-start(bf16[2,1024,6]{1,2,0:T(8,128)(2,1)} %get-tuple-element.2168) | copy-start | bytes 73732 | tf_op jit(solution)/shard_map/while
  583.4 32.6 %copy-start.111 = (bf16[2,1024,6]{1,2,0:T(8,128)(2,1)S(1)}, bf16[2,1024,6]{1,2,0:T(8,128)(2,1)}, u32[]{:S(2)}) copy-start(bf16[2,1024,6]{1,2,0:T(8,128)(2,1)} %get-tuple-element.2122) | copy-start | bytes 73732 | tf_op jit(solution)/shard_map/while
  583.4 32.7 %copy-start.137 = (f32[2,6]{1,0:T(2,128)S(1)}, f32[2,6]{1,0:T(2,128)}, u32[]{:S(2)}) copy-start(f32[2,6]{1,0:T(2,128)} %get-tuple-element.2128) | copy-start | bytes 148 | tf_op jit(solution)/shard_map/while
  583.4 32.7 %copy-start.143 = (f32[1,6]{1,0:T(1,128)S(1)}, f32[1,6]{1,0:T(1,128)}, u32[]{:S(2)}) copy-start(f32[1,6]{1,0:T(1,128)} %get-tuple-element.2173) | copy-start | bytes 76 | tf_op jit(solution)/shard_map/while
  583.4 32.8 %copy-start.135 = (f32[2,6]{1,0:T(2,128)S(1)}, f32[2,6]{1,0:T(2,128)}, u32[]{:S(2)}) copy-start(f32[2,6]{1,0:T(2,128)} %get-tuple-element.2129) | copy-start | bytes 148 | tf_op jit(solution)/shard_map/while
  583.5 33.0 %copy-start.18 = (f32[1024,256]{1,0:T(8,128)S(1)}, f32[1024,256]{1,0:T(8,128)}, u32[]{:S(2)}) copy-start(f32[1024,256]{1,0:T(8,128)} %get-tuple-element.1922) | copy-start | bytes 3145732 | tf_op jit(solution)/shard_map/while
  583.5 33.0 %copy-start.79 = (f32[256,1]{0,1:T(1,128)S(1)}, f32[256,1]{0,1:T(1,128)}, u32[]{:S(2)}) copy-start(f32[256,1]{0,1:T(1,128)} %copy-done.78) | copy-start | bytes 3076 | tf_op jit(solution)/shard_map/while
  583.5 33.0 %copy-start.81 = (f32[256,1]{0,1:T(1,128)S(1)}, f32[256,1]{0,1:T(1,128)}, u32[]{:S(2)}) copy-start(f32[256,1]{0,1:T(1,128)} %copy-done.80) | copy-start | bytes 3076 | tf_op jit(solution)/shard_map/while
  583.5 33.0 %copy-start.83 = (f32[256,1]{0,1:T(1,128)S(1)}, f32[256,1]{0,1:T(1,128)}, u32[]{:S(2)}) copy-start(f32[256,1]{0,1:T(1,128)} %copy-done.82) | copy-start | bytes 3076 | tf_op jit(solution)/shard_map/while
  583.5 33.0 %copy-start.85 = (f32[256,1]{0,1:T(1,128)S(1)}, f32[256,1]{0,1:T(1,128)}, u32[]{:S(2)}) copy-start(f32[256,1]{0,1:T(1,128)} %copy-done.84) | copy-start | bytes 3076 | tf_op jit(solution)/shard_map/while
  624.7 11.3 copy-start.70
  624.7 13.5 copy-start.15
  626.1 15.5 copy-start.78
  626.1 15.5 copy-start.80
  626.1 15.5 copy-start.82
  626.1 15.5 copy-start.84
  627.5 14.2 copy-start.28
  711.8 32.4 %copy-start.100 = (f32[1,1,6]{2,1,0:T(1,128)S(1)}, f32[1,1,6]{2,1,0:T(1,128)}, u32[]{:S(2)}) copy-start(f32[1,1,6]{2,1,0:T(1,128)} %get-tuple-element.2170) | copy-start | bytes 76 | tf_op jit(solution)/shard_map/while
  711.8 32.6 %copy-start.60 = (bf16[2,1024,6]{1,2,0:T(8,128)(2,1)S(1)}, bf16[2,1024,6]{1,2,0:T(8,128)(2,1)}, u32[]{:S(2)}) copy-start(bf16[2,1024,6]{1,2,0:T(8,128)(2,1)} %get-tuple-element.2168) | copy-start | bytes 73732 | tf_op jit(solution)/shard_map/while
  711.8 32.6 %copy-start.111 = (bf16[2,1024,6]{1,2,0:T(8,128)(2,1)S(1)}, bf16[2,1024,6]{1,2,0:T(8,128)(2,1)}, u32[]{:S(2)}) copy-start(bf16[2,1024,6]{1,2,0:T(8,128)(2,1)} %get-tuple-element.2122) | copy-start | bytes 73732 | tf_op jit(solution)/shard_map/while
  711.8 32.7 %copy-start.137 = (f32[2,6]{1,0:T(2,128)S(1)}, f32[2,6]{1,0:T(2,128)}, u32[]{:S(2)}) copy-start(f32[2,6]{1,0:T(2,128)} %get-tuple-element.2128) | copy-start | bytes 148 | tf_op jit(solution)/shard_map/while
  711.8 32.7 %copy-start.143 = (f32[1,6]{1,0:T(1,128)S(1)}, f32[1,6]{1,0:T(1,128)}, u32[]{:S(2)}) copy-start(f32[1,6]{1,0:T(1,128)} %get-tuple-element.2173) | copy-start | bytes 76 | tf_op jit(solution)/shard_map/while
  711.8 32.8 %copy-start.135 = (f32[2,6]{1,0:T(2,128)S(1)}, f32[2,6]{1,0:T(2,128)}, u32[]{:S(2)}) copy-start(f32[2,6]{1,0:T(2,128)} %get-tuple-element.2129) | copy-start | bytes 148 | tf_op jit(solution)/shard_map/while
  711.8 33.2 %copy-start.18 = (f32[1024,256]{1,0:T(8,128)S(1)}, f32[1024,256]{1,0:T(8,128)}, u32[]{:S(2)}) copy-start(f32[1024,256]{1,0:T(8,128)} %get-tuple-element.1922) | copy-start | bytes 3145732 | tf_op jit(solution)/shard_map/while
  711.8 33.2 %copy-start.79 = (f32[256,1]{0,1:T(1,128)S(1)}, f32[256,1]{0,1:T(1,128)}, u32[]{:S(2)}) copy-start(f32[256,1]{0,1:T(1,128)} %copy-done.78) | copy-start | bytes 3076 | tf_op jit(solution)/shard_map/while
  711.9 33.2 %copy-start.81 = (f32[256,1]{0,1:T(1,128)S(1)}, f32[256,1]{0,1:T(1,128)}, u32[]{:S(2)}) copy-start(f32[256,1]{0,1:T(1,128)} %copy-done.80) | copy-start | bytes 3076 | tf_op jit(solution)/shard_map/while
  711.9 33.2 %copy-start.83 = (f32[256,1]{0,1:T(1,128)S(1)}, f32[256,1]{0,1:T(1,128)}, u32[]{:S(2)}) copy-start(f32[256,1]{0,1:T(1,128)} %copy-done.82) | copy-start | bytes 3076 | tf_op jit(solution)/shard_map/while
  711.9 33.2 %copy-start.85 = (f32[256,1]{0,1:T(1,128)S(1)}, f32[256,1]{0,1:T(1,128)}, u32[]{:S(2)}) copy-start(f32[256,1]{0,1:T(1,128)} %copy-done.84) | copy-start | bytes 3076 | tf_op jit(solution)/shard_map/while
  763.2 9.3 all-to-all-start.5
  766.5 188.1 %reduce-scatter.13.cloned.1.call-start = ((), (), s32[]{:S(2)}) async-start(), calls=%async_computation.17 | async-start | bytes 811008 | tf_op jit(solution)/shard_map/reduce_scatter | solution.py:265
  775.8 221.1 %reduce-scatter.11.cloned.1.call-start = ((), (), s32[]{:S(2)}) async-start(), calls=%async_computation.16 | async-start | bytes 1622016 | tf_op jit(solution)/shard_map/reduce_scatter | solution.py:264
  798.7 410.5 %reduce-scatter.15.cloned.1.call-start = ((), (), s32[]{:S(2)}) async-start(), calls=%async_computation.18 | async-start | bytes 19464192 | tf_op jit(solution)/shard_map/reduce_scatter | solution.py:196
  807.9 754.8 %reduce-scatter.9.cloned.1.call-start = ((), (), s32[]{:S(2)}) async-start(), calls=%async_computation.15 | async-start | bytes 38928384 | tf_op jit(solution)/shard_map/reduce_scatter | solution.py:263
  873.8 24.1 %copy-start.56 = (bf16[1536,48]{1,0:T(8,128)(2,1)S(1)}, bf16[1536,48]{1,0:T(8,128)(2,1)}, u32[]{:S(2)}) copy-start(bf16[1536,48]{1,0:T(8,128)(2,1)} %copy-done.55) | copy-start | bytes 442372
  881.2 19.0 %copy-start.43 = (bf16[1536,256]{1,0:T(8,128)(2,1)S(1)}, bf16[1536,256]{1,0:T(8,128)(2,1)}, u32[]{:S(2)}) copy-start(bf16[1536,256]{1,0:T(8,128)(2,1)} %copy-done.42) | copy-start | bytes 2359300
  881.2 19.0 %copy-start.66 = (bf16[2,128,256]{2,1,0:T(8,128)(2,1)S(1)}, bf16[2,128,256]{2,1,0:T(8,128)(2,1)}, u32[]{:S(2)}) copy-start(bf16[2,128,256]{2,1,0:T(8,128)(2,1)} %copy-done.65) | copy-start | bytes 393220
  902.4 10.9 copy-start.117
  902.4 50.8 %copy-start.58 = (bf16[2,128,1536]{2,1,0:T(8,128)(2,1)S(1)}, bf16[2,128,1536]{2,1,0:T(8,128)(2,1)}, u32[]{:S(2)}) copy-start(bf16[2,128,1536]{2,1,0:T(8,128)(2,1)} %param.39) | copy-start | bytes 2359300
  (189 other events, 439.4 us)
Sparse Core Ops, SparseCore 0:
  11.9 130.2 all-gather.4
Sparse Core Ops, SparseCore 1:
  234.2 19.2 all-gather.6
  256.4 81.5 all-gather.8
  760.7 33.4 reduce-scatter.6
  799.9 94.9 reduce-scatter.12
  900.6 96.2 reduce-scatter.10
  1003.9 205.2 reduce-scatter.14
  1216.0 346.7 reduce-scatter.8
where the time goes:
time: 1580 us; the launch traced here: 1570 us
  waiting for transfers between devices  746 us (47%)
  blocking collectives  287 us (18%)
  other arithmetic  183 us (12%)
  matrix products  158 us (10%)
  local copies, waits for them, and re-layouts  149 us (9%)
  starting transfers between devices  18 us (1%)
  between operations  16.6 us (1%)
    reduce_scatter x1, waiting for transfers between devices, on_device(): lax.psum_scatter(first_terms, ('dp', 'sp'), scatter_dimension=0, tiled=True)  354 us
    reduce_scatter x1, waiting for transfers between devices, on_device(): lax.psum_scatter(wout_terms, ('dp', 'sp'), scatter_dimension=0, tiled=True)  212 us
    another operation x31, other arithmetic  91.9 us
    unnamed x2, blocking collectives  80.5 us
    all_gather x1, blocking collectives, on_device(): lax.all_gather(w_bc, ('dp', 'sp'), axis=0, tiled=True)  70.9 us
    all_gather x1, blocking collectives, on_device(): lax.all_gather(w_dt, ('dp', 'sp'), axis=0, tiled=True)  44.3 us
    all_to_all x1, blocking collectives, on_device(): lax.all_to_all(dx_heads, 'sp', split_axis=1, concat_axis=2, tiled=True)  42.6 us
    reduce_scatter x1, waiting for transfers between devices, on_device(): lax.psum_scatter(bc_terms, ('dp', 'sp'), scatter_dimension=0, tiled=True)  42.3 us
  transfers between devices with their start and end apart: 13, of which 8 were waited for; matrix products, arithmetic and copies ran while one was open for 13% of the time, Pallas kernels for 0%

commit v1 on v0

v1 whole, which is shorter than its diff:
```python
import functools

import jax
import jax.numpy as jnp
from jax import lax
from jax.experimental import pallas as pl
from jax.experimental.pallas import tpu as pltpu
from jax.sharding import PartitionSpec as P

P_SIZE = 64
EPS = 1e-05
F32 = jnp.float32
BF16 = jnp.bfloat16
HIGH = lax.Precision.HIGHEST
LANES = 128
VMEM_LIMIT = 48 * 1024 * 1024


def dot(left, right, dims=((1,), (0,)), precision=None):
    return lax.dot_general(
        left, right, (dims, ((), ())), precision=precision, preferred_element_type=F32
    )


def iota(shape, axis):
    return lax.broadcasted_iota(jnp.int32, shape, axis)


def spread(cols, pair, low_half):
    return jnp.where(low_half, cols[:, 2 * pair : 2 * pair + 1], cols[:, 2 * pair + 1 : 2 * pair + 2])


def spread_all(cols, pairs, low_half):
    return jnp.concatenate([spread(cols, pair, low_half) for pair in range(pairs)], axis=1)


def stack_heads(values, low_half):
    zero = jnp.zeros_like(values)
    return jnp.concatenate(
        [jnp.where(low_half, values, zero), jnp.where(low_half, zero, values)], axis=0
    )


def softplus(value):
    return jnp.maximum(value, 0.0) + jnp.log1p(jnp.exp(-jnp.abs(value)))


def conv_pre(ext, rows, taps):
    total = taps[4:5, :]
    for tap in range(4):
        total = total + taps[tap : tap + 1, :] * ext[pl.ds(5 + tap, rows), :]
    return total


def steps_of(dt_raw, head_ref):
    pre = dt_raw.astype(F32) + head_ref[0:1, :]
    steps = softplus(pre)
    return pre, steps, -steps * head_ref[1:2, :]


def scan_forward(wide, chans, zx, taps, heads, skip, mixed, enter, ext, halo, state):
    chunk, seq = pl.program_id(0), pl.program_id(1)
    rows = zx.shape[0]
    pairs = chans // LANES
    low_half = iota((rows, LANES), 1) < P_SIZE

    @pl.when(chunk == 0)
    def _():
        halo[seq] = jnp.zeros(halo.shape[1:], F32)
        state[seq] = jnp.zeros(state.shape[1:], F32)

    raw = zx[:, chans : 2 * chans + wide].astype(F32)
    ext[0:8, :] = halo[seq]
    ext[8 : 8 + rows, :] = raw
    halo[seq] = raw[rows - 8 :, :]
    pre = conv_pre(ext, rows, taps)
    act = (pre * jax.nn.sigmoid(pre)).astype(BF16)
    half = wide // 2
    bmat = act[:, chans : chans + half]
    cmat = act[:, chans + half :]
    _, steps, logs = steps_of(zx[:, 2 * chans + wide :], heads)
    earlier = iota((rows, rows), 0) >= iota((rows, rows), 1)
    cumul = dot(earlier.astype(F32), logs, precision=HIGH)
    cumul_t = cumul.T
    last = cumul[rows - 1 :, :]
    scores = dot(cmat, bmat, ((1,), (1,)))
    grown = jnp.exp(cumul)
    to_end = steps * jnp.exp(last - cumul)
    final = jnp.exp(last)
    entering = state[seq]
    enter[...] = entering.astype(BF16)
    across = dot(cmat, entering.astype(BF16))
    for pair in range(pairs):
        lanes = slice(pair * LANES, (pair + 1) * LANES)
        weights = []
        for head in (2 * pair, 2 * pair + 1):
            differ = cumul[:, head : head + 1] - cumul_t[head : head + 1, :]
            decay = jnp.where(earlier, jnp.exp(jnp.minimum(differ, 0.0)), 0.0)
            weights.append((decay * scores).astype(BF16))
        values = act[:, lanes].astype(F32)
        scaled = (values * spread(steps, pair, low_half)).astype(BF16)
        total = dot(jnp.concatenate(weights, axis=1), stack_heads(scaled, low_half))
        total = total + spread(grown, pair, low_half) * across[:, lanes]
        total = total + skip[0:1, lanes] * values
        mixed[:, lanes] = total.astype(BF16)
        ending = (values * spread(to_end, pair, low_half)).astype(BF16)
        state[seq, :, lanes] = entering[:, lanes] * spread(
            final, pair, low_half[0:1, :]
        ) + dot(bmat, ending, ((0,), (0,)))


def scan_backward(
    wide, chans, inner,
    zx, before, taps, heads, skip, gain, mixed, enter, grads, sums,
    dz, dtaps, dheads, dskip,
    ext, gext, halo, dstate,
):
    step, seq = pl.program_id(0), pl.program_id(1)
    chunk = pl.num_programs(0) - 1 - step
    rows = zx.shape[0]
    pairs = chans // LANES
    half = wide // 2
    low_half = iota((rows, LANES), 1) < P_SIZE

    @pl.when(step == 0)
    def _():
        halo[seq] = jnp.zeros(halo.shape[1:], F32)
        dstate[seq] = jnp.zeros(dstate.shape[1:], F32)

    @pl.when((step == 0) & (seq == 0))
    def _():
        dtaps[...] = jnp.zeros_like(dtaps)
        dheads[...] = jnp.zeros_like(dheads)
        dskip[...] = jnp.zeros_like(dskip)

    gate = zx[:, :chans].astype(F32)
    sig = jax.nn.sigmoid(gate)
    silu = gate * sig
    mix = mixed[...].astype(F32)
    scale = lax.rsqrt(sums[:, 0:1] * (1.0 / inner) + EPS)
    mean = sums[:, 1:2] * scale * (1.0 / inner)
    back = scale * (grads[...] * gain[0:1, :] - mix * silu * (scale * mean))
    dy_half = (back * silu).astype(BF16)
    dz[:, :chans] = (back * mix * sig * (1.0 + gate * (1.0 - sig))).astype(BF16)
    dy = dy_half.astype(F32)

    raw = zx[:, chans : 2 * chans + wide].astype(F32)
    past = before[before.shape[0] - 8 :, chans : 2 * chans + wide].astype(F32)
    ext[0:8, :] = jnp.where(chunk == 0, 0.0, past)
    ext[8 : 8 + rows, :] = raw
    pre = conv_pre(ext, rows, taps)
    sig_pre = jax.nn.sigmoid(pre)
    act = (pre * sig_pre).astype(BF16)
    slope = sig_pre * (1.0 + pre * (1.0 - sig_pre))
    bmat = act[:, chans : chans + half]
    cmat = act[:, chans + half :]
    xmat = act[:, :chans]
    xval = xmat.astype(F32)
    dt_pre, steps, logs = steps_of(zx[:, 2 * chans + wide :], heads)
    row, col = iota((rows, rows), 0), iota((rows, rows), 1)
    cumul = dot((row >= col).astype(F32), logs, precision=HIGH)
    cumul_t = cumul.T
    last = cumul[rows - 1 :, :]
    later = row <= col
    scores = dot(bmat, cmat, ((1,), (1,)))
    grown = jnp.exp(cumul)
    shrunk = jnp.exp(last - cumul)
    final = jnp.exp(last)
    entering = enter[...]
    dleave = dstate[seq]
    dleave_half = dleave.astype(BF16)
    from_state = dot(bmat, dleave_half)
    across = dot(cmat, entering)
    grown_all = spread_all(grown, pairs, low_half)
    ending_all = spread_all(steps * shrunk, pairs, low_half)
    dy_grown = (dy * grown_all).astype(BF16)
    x_end = (xval * ending_all).astype(BF16)
    dstate[seq] = dleave * spread_all(final, pairs, low_half[0:1, :]) + dot(
        cmat, dy_grown, ((0,), (0,))
    )
    owner = (iota((chans, LANES), 0) // P_SIZE == iota((chans, LANES), 1)).astype(F32)
    near = dot(xval * from_state, owner, precision=HIGH) * shrunk
    reach = dot(dy * across, owner, precision=HIGH) * grown
    kept = jnp.sum(entering.astype(F32) * dleave, axis=0, keepdims=True)
    kept = dot(jnp.broadcast_to(kept, (8, chans)), owner, precision=HIGH)[0:1, :] * final
    pairs_sum = jnp.zeros((rows, rows), F32)
    head_lane = iota((rows, LANES), 1)
    col_sum = jnp.zeros((rows, LANES), F32)
    row_sums = []
    for pair in range(pairs):
        lanes = slice(pair * LANES, (pair + 1) * LANES)
        products = dot(stack_heads(xmat[:, lanes], low_half), dy_half[:, lanes], ((1,), (1,)))
        weights = []
        for place, head in enumerate((2 * pair, 2 * pair + 1)):
            product = products[place * rows : (place + 1) * rows, :]
            differ = cumul_t[head : head + 1, :] - cumul[:, head : head + 1]
            decay = jnp.where(later, jnp.exp(jnp.minimum(differ, 0.0)), 0.0)
            weight = decay * scores
            step_col = steps[:, head : head + 1]
            weights.append(weight.astype(BF16))
            pairs_sum = pairs_sum + decay * product * step_col
            terms = weight * product
            col_sum = jnp.where(head_lane == head, jnp.sum(terms, axis=1, keepdims=True), col_sum)
            row_sums.append(jnp.sum(terms * step_col, axis=0, keepdims=True))
        inside = dot(
            jnp.concatenate(weights, axis=1), stack_heads(dy_half[:, lanes], low_half)
        )
        dx = spread(steps, pair, low_half) * (
            inside + spread(shrunk, pair, low_half) * from_state[:, lanes]
        )
        dx = dx + skip[0:1, lanes] * dy[:, lanes]
        gext[0:rows, lanes] = dx * slope[:, lanes]
    pairs_half = pairs_sum.astype(BF16)
    d_b = dot(pairs_half, cmat) + dot(x_end, dleave_half, ((1,), (1,)))
    d_c = dot(pairs_half, bmat, ((0,), (0,))) + dot(dy_grown, entering, ((1,), (1,)))
    gext[0:rows, chans : chans + half] = d_b * slope[:, chans : chans + half]
    gext[0:rows, chans + half :] = d_c * slope[:, chans + half :]

    row_sum = jnp.concatenate(
        row_sums + [jnp.zeros((LANES - 2 * pairs, rows), F32)], axis=0
    ).T
    d_logs = dot((row <= col).astype(F32), row_sum - steps * col_sum + reach, precision=HIGH)
    d_logs = d_logs + dot((row > col).astype(F32), steps * near, precision=HIGH) + kept
    d_steps = col_sum + near - heads[1:2, :] * d_logs
    d_pre = d_steps * jax.nn.sigmoid(dt_pre)
    dz[:, 2 * chans + wide :] = d_pre.astype(BF16)
    dheads[0:1, :] += jnp.sum(d_pre, axis=0, keepdims=True)
    dheads[1:2, :] += jnp.sum(d_logs * logs, axis=0, keepdims=True)
    dskip[0:1, :] += jnp.sum(dy * xval, axis=0, keepdims=True)

    gext[rows : rows + 8, :] = halo[seq]
    g = gext[0:rows, :]
    halo[seq] = g[0:8, :]
    d_in = jnp.zeros((rows, chans + wide), F32)
    for tap in range(4):
        d_in = d_in + taps[tap : tap + 1, :] * gext[pl.ds(3 - tap, rows), :]
        dtaps[tap : tap + 1, :] += jnp.sum(g * ext[pl.ds(5 + tap, rows), :], axis=0, keepdims=True)
    dtaps[4:5, :] += jnp.sum(g, axis=0, keepdims=True)
    dz[:, chans : 2 * chans + wide] = d_in.astype(BF16)


def run_forward(zx, taps, heads, skip, chans, wide):
    blocks, seqs, rows, cols = zx.shape
    states = wide // 2
    block = lambda n: pl.BlockSpec((None, None, rows, n), lambda i, j: (i, j, 0, 0))
    whole = lambda a: pl.BlockSpec(a.shape, lambda i, j: (0,) * a.ndim)
    return pl.pallas_call(
        functools.partial(scan_forward, wide, chans),
        grid=(blocks, seqs),
        in_specs=[block(cols), whole(taps), whole(heads), whole(skip)],
        out_specs=[
            block(chans),
            pl.BlockSpec((None, None, states, chans), lambda i, j: (i, j, 0, 0)),
        ],
        out_shape=[
            jax.ShapeDtypeStruct((blocks, seqs, rows, chans), BF16),
            jax.ShapeDtypeStruct((blocks, seqs, states, chans), BF16),
        ],
        scratch_shapes=[
            pltpu.VMEM((rows + 8, chans + wide), F32),
            pltpu.VMEM((seqs, 8, chans + wide), F32),
            pltpu.VMEM((seqs, states, chans), F32),
        ],
        compiler_params=pltpu.CompilerParams(vmem_limit_bytes=VMEM_LIMIT),
        name="scan_forward",
    )(zx, taps, heads, skip)


def run_backward(zx, taps, heads, skip, gain, mixed, enter, grads, sums, chans, wide, inner):
    blocks, seqs, rows, cols = zx.shape
    states = wide // 2
    back = lambda i: blocks - 1 - i
    block = lambda n: pl.BlockSpec((None, None, rows, n), lambda i, j: (back(i), j, 0, 0))
    whole = lambda a: pl.BlockSpec(a.shape, lambda i, j: (0,) * a.ndim)
    before = pl.BlockSpec(
        (None, None, 16, cols),
        lambda i, j: (jnp.maximum(back(i) - 1, 0), j, rows // 16 - 1, 0),
    )
    fixed = lambda n: pl.BlockSpec((8, n), lambda i, j: (0, 0))
    return pl.pallas_call(
        functools.partial(scan_backward, wide, chans, inner),
        grid=(blocks, seqs),
        in_specs=[
            block(cols), before, whole(taps), whole(heads), whole(skip), whole(gain),
            block(chans),
            pl.BlockSpec((None, None, states, chans), lambda i, j: (back(i), j, 0, 0)),
            block(chans), block(2),
        ],
        out_specs=[block(cols), fixed(chans + wide), fixed(LANES), fixed(chans)],
        out_shape=[
            jax.ShapeDtypeStruct(zx.shape, BF16),
            jax.ShapeDtypeStruct((8, chans + wide), F32),
            jax.ShapeDtypeStruct((8, LANES), F32),
            jax.ShapeDtypeStruct((8, chans), F32),
        ],
        scratch_shapes=[
            pltpu.VMEM((rows + 8, chans + wide), F32),
            pltpu.VMEM((rows + 8, chans + wide), F32),
            pltpu.VMEM((seqs, 8, chans + wide), F32),
            pltpu.VMEM((seqs, states, chans), F32),
        ],
        compiler_params=pltpu.CompilerParams(vmem_limit_bytes=VMEM_LIMIT),
        name="scan_backward",
    )(zx, zx, taps, heads, skip, gain, mixed, enter, grads, sums)


def pad_last(value, size):
    return jnp.pad(value, [(0, 0)] * (value.ndim - 1) + [(0, size - value.shape[-1])])


def eight_rows(*rows):
    stacked = jnp.stack(rows, axis=0)
    return jnp.pad(stacked, ((0, 8 - stacked.shape[0]), (0, 0)))


def on_device(
    dp, sp,
    hidden_in, w_zx, w_bc, w_dt, norm_gain, conv_bc_weight, conv_bc_bias,
    conv_x_weight, conv_x_bias, dt_bias, a_log, d_skip, gate_gain, w_out, cotangent,
):
    both = ("dp", "sp")
    me_dp, me_sp = lax.axis_index("dp"), lax.axis_index("sp")
    seqs, block, width = hidden_in.shape
    rows = sp * seqs * block
    wide = w_bc.shape[1]
    heads = w_dt.shape[1]
    own_heads = dt_bias.shape[0]
    inner = heads * P_SIZE
    own = own_heads * P_SIZE
    chans = -(-own // LANES) * LANES
    share = w_zx.shape[0]
    taps_n = conv_x_weight.shape[1]

    hidden_all = lax.all_gather(hidden_in, "sp", axis=0, tiled=False)
    cot_all = lax.all_gather(cotangent, "sp", axis=0, tiled=False)
    zx_parts = jnp.transpose(w_zx.reshape(share, 2, sp, own), (2, 0, 1, 3))
    zx_mine = lax.all_to_all(zx_parts, "sp", split_axis=0, concat_axis=0, tiled=True)
    zx_mine = lax.all_gather(zx_mine, "dp", axis=0, tiled=False).reshape(width, 2, own)
    bcdt = lax.all_gather(jnp.concatenate([w_bc, w_dt], axis=1), both, axis=0, tiled=True)
    dt_cols = lax.dynamic_slice_in_dim(bcdt, wide + me_sp * own_heads, own_heads, axis=1)
    weights = jnp.concatenate(
        [pad_last(zx_mine, chans).reshape(width, 2 * chans), bcdt[:, :wide], pad_last(dt_cols, LANES)],
        axis=1,
    )
    pieces = dp * sp
    to_group = [(src, (src % dp) * sp + src // dp) for src in range(pieces)]
    to_owner = [(dst, src) for src, dst in to_group]
    out_mine = lax.all_gather(
        lax.ppermute(w_out, both, to_group), "dp", axis=0, tiled=True
    )
    small = jnp.concatenate(
        [
            norm_gain.reshape(-1),
            gate_gain.reshape(-1),
            jnp.concatenate([conv_bc_weight, conv_bc_bias[:, None]], axis=1).reshape(-1),
        ]
    )
    small_all = lax.all_gather(small, both, axis=0, tiled=False)
    gate_share = gate_gain.shape[0]
    bc_share = conv_bc_bias.shape[0]
    norm_all = small_all[:, :share].reshape(width).astype(F32)
    gate_all = small_all[:, share : share + gate_share].reshape(inner)
    gate_mine = lax.dynamic_slice_in_dim(gate_all, me_sp * own, own).astype(F32)
    bc_all = small_all[:, share + gate_share :].reshape(wide, taps_n + 1).astype(F32)

    x_taps = pad_last(conv_x_weight.astype(F32).T, chans)
    x_bias = pad_last(conv_x_bias.astype(F32), chans)
    taps = jnp.concatenate(
        [
            eight_rows(*[x_taps[k] for k in range(taps_n)], x_bias),
            eight_rows(*[bc_all[:, k] for k in range(taps_n + 1)]),
        ],
        axis=1,
    )
    head_rows = eight_rows(
        pad_last(dt_bias.astype(F32), LANES), pad_last(jnp.exp(a_log.astype(F32)), LANES)
    )
    skip = eight_rows(pad_last(jnp.repeat(d_skip.astype(F32), P_SIZE), chans))
    gain = eight_rows(pad_last(gate_mine, chans))

    hidden = hidden_all.reshape(rows, width).astype(F32)
    scale_in = lax.rsqrt(jnp.mean(hidden * hidden, axis=-1, keepdims=True) + EPS)
    normed = (hidden * scale_in * norm_all).astype(BF16)
    zx = dot(normed, weights).astype(BF16)
    zx_blocks = zx.reshape(sp, seqs, block, -1)
    mixed, entering = run_forward(zx_blocks, taps, head_rows, skip, chans, wide)

    cot_rows = cot_all.reshape(rows, width)
    out_rows = jnp.pad(out_mine, ((0, chans - own), (0, 0)))
    d_gated = dot(cot_rows, out_rows, ((1,), (1,)))
    gate = zx[:, :chans].astype(F32)
    gated_in = mixed.reshape(rows, chans).astype(F32) * gate * jax.nn.sigmoid(gate)
    sums = jnp.stack(
        [
            jnp.sum(gated_in * gated_in, axis=1),
            jnp.sum(gated_in * d_gated * gain[0:1, :], axis=1),
        ],
        axis=1,
    )
    sums = lax.psum(sums, "sp")
    scale_out = lax.rsqrt(sums[:, 0:1] * (1.0 / inner) + EPS)
    gated = (gated_in * scale_out * gain[0:1, :]).astype(BF16)
    out_part = dot(gated, out_rows).astype(BF16).reshape(sp, seqs * block, width)
    out_sum = lax.psum_scatter(out_part, "sp", scatter_dimension=0, tiled=False)
    hidden_out = (
        hidden_in.astype(F32) + out_sum.astype(F32).reshape(hidden_in.shape)
    ).astype(BF16)
    out_terms = dot(gated, cot_rows, ((0,), (0,)))[:own].astype(BF16)
    out_grad = lax.psum_scatter(out_terms, "dp", scatter_dimension=0, tiled=True)
    grad_w_out = lax.ppermute(out_grad, both, to_owner).astype(F32)
    grad_gate_gain = jnp.sum(grad_w_out * w_out.astype(F32), axis=1) / gate_gain.astype(F32)

    dz, dtaps, dheads, dskip = run_backward(
        zx_blocks, taps, head_rows, skip, gain, mixed, entering,
        d_gated.reshape(sp, seqs, block, chans), sums.reshape(sp, seqs, block, 2),
        chans, wide, inner,
    )
    dz = dz.reshape(rows, -1)
    d_part = dot(dz, weights, ((1,), (1,))).astype(BF16).reshape(sp, seqs * block, width)
    d_normed = lax.psum_scatter(d_part, "sp", scatter_dimension=0, tiled=False).astype(F32)
    terms = dot(normed, dz, ((0,), (0,)))
    terms = jnp.concatenate(
        [terms[:, :own], terms[:, chans : chans + own], terms[:, 2 * chans : 2 * chans + wide + own_heads]],
        axis=1,
    ).astype(BF16)
    terms = lax.psum_scatter(terms, "dp", scatter_dimension=0, tiled=True)
    terms = terms.reshape(sp, share, -1)
    terms = lax.all_to_all(terms, "sp", split_axis=0, concat_axis=0, tiled=True).astype(F32)
    grad_w_zx = jnp.transpose(
        terms[:, :, : 2 * own].reshape(sp, share, 2, own), (1, 2, 0, 3)
    ).reshape(share, 2 * inner)
    grad_w_bc = jnp.sum(terms[:, :, 2 * own : 2 * own + wide], axis=0)
    grad_w_dt = jnp.transpose(terms[:, :, 2 * own + wide :], (1, 0, 2)).reshape(share, heads)
    grad_norm_gain = (
        jnp.sum(grad_w_zx * w_zx.astype(F32), axis=1)
        + jnp.sum(grad_w_bc * w_bc.astype(F32), axis=1)
        + jnp.sum(grad_w_dt * w_dt.astype(F32), axis=1)
    ) / norm_gain.astype(F32)

    hid = hidden_in.reshape(seqs * block, width).astype(F32)
    scale_own = lax.rsqrt(jnp.mean(hid * hid, axis=-1, keepdims=True) + EPS)
    unit_own = hid * scale_own
    weighted = d_normed * norm_all
    grad_rows = cotangent.reshape(seqs * block, width).astype(F32) + scale_own * (
        weighted - unit_own * jnp.mean(weighted * unit_own, axis=-1, keepdims=True)
    )
    grad_hidden = grad_rows.astype(BF16).reshape(hidden_in.shape)

    per_head = jnp.sum(dskip[0, :own].reshape(own_heads, P_SIZE), axis=1)
    g_x, g_dt, g_log, g_skip = lax.psum(
        (dtaps[:5, :own], dheads[0, :own_heads], dheads[1, :own_heads], per_head), "dp"
    )
    g_bc = lax.psum(dtaps[:5, chans:], both)
    mine = (me_dp * sp + me_sp) * bc_share
    g_bc = lax.dynamic_slice_in_dim(g_bc, mine, bc_share, axis=1)
    return (
        hidden_out,
        grad_hidden,
        grad_w_zx,
        grad_w_bc,
        grad_w_dt,
        grad_norm_gain,
        g_bc[:taps_n].T,
        g_bc[taps_n],
        g_x[:taps_n].T,
        g_x[taps_n],
        g_dt,
        g_log,
        g_skip,
        grad_gate_gain,
        grad_w_out,
    )


def solution(mesh):
    both = P(("dp", "sp"))
    rows = P(("dp", "sp"), None)
    tokens = P("dp", "sp", None)
    return jax.shard_map(
        functools.partial(on_device, mesh.shape["dp"], mesh.shape["sp"]),
        mesh=mesh,
        in_specs=(
            tokens, rows, rows, rows, both, rows, both, P("sp", None), P("sp"), P("sp"),
            P("sp"), P("sp"), both, rows, tokens,
        ),
        out_specs=(
            tokens, tokens, rows, rows, rows, both, rows, both, P("sp", None), P("sp"),
            P("sp"), P("sp"), P("sp"), both, rows,
        ),
        check_vma=False,
    )
```

time: 1580 us -> 591 us (0.37)
  waiting for transfers between devices: 746 us -> 167 us
  other arithmetic: 183 us -> 21.5 us
  local copies, waits for them, and re-layouts: 149 us -> 29.1 us
  matrix products: 158 us -> 60.8 us
  blocking collectives: 287 us -> 228 us
  Pallas kernels: 0 us -> 54.6 us
    reduce_scatter x5 -> x4, waiting for transfers between devices: 626 us -> 117 us  [the longest x1 72 us: on_device(): out_sum = lax.psum_scatter(out_part, 'sp', scatter_dimension=0, tiled=False)]
    all_gather x3 -> x1, blocking collectives: 152 us -> 56.9 us  [on_device(): lax.all_gather(jnp.concatenate([w_bc, w_dt], axis=1), both, axis=0, tiled...]
    dot_general x40 -> x6, matrix products: 154 us -> 60.8 us  [dot(): lax.dot_general(left, right, (dims, ((), ())), precision=precision, prefe...]
    another operation x31 -> x3, other arithmetic: 91.9 us -> 0.03 us  [the longest x1 0.02 us: on_device(): jnp.stack([jnp.sum(gated_in * gated_in, axis=1), jnp.sum(gated_in * d_gat...]
    all_to_all x5 -> x1, waiting for transfers between devices: 80.9 us -> 0.01 us  [on_device(): lax.all_to_all(terms, 'sp', split_axis=0, concat_axis=0, tiled=True)]
    psum x1 -> x3, blocking collectives: 11.7 us -> 86.1 us  [the longest x1 42.2 us: on_device(): g_bc = lax.psum(dtaps[:5, chans:], both)]
    pallas_call x0 -> x2, Pallas kernels: none -> 54.6 us  [the longest x1 37.6 us: run_backward(): pl.pallas_call(functools.partial(scan_backward, wide, chans, inner), grid...]
    while x395 -> x0, local copies, waits for them, and re-layouts: 35.5 us -> none
  transfers between devices with their start and end apart: 13 -> 11, of which waited for: 8 -> 4; matrix products, arithmetic and copies ran while one was open for 13% -> 12% of each run, Pallas kernels for 0% -> 3%
where the time goes in v1:
time: 591 us; the launch traced here: 584 us
  blocking collectives  228 us (39%)
  waiting for transfers between devices  167 us (28%)
  matrix products  60.8 us (10%)
  Pallas kernels  54.6 us (9%)
  local copies, waits for them, and re-layouts  29.1 us (5%)
  other arithmetic  21.5 us (4%)
  between operations  15.2 us (3%)
  starting transfers between devices  7.21 us (1%)
    reduce_scatter x1, waiting for transfers between devices, on_device(): out_sum = lax.psum_scatter(out_part, 'sp', scatter_dimension=0, tiled=False)  72 us
    unnamed x1, blocking collectives  62.3 us
    dot_general x6, matrix products, dot(): lax.dot_general(left, right, (dims, ((), ())), precision=precision, prefe...  60.8 us
    all_gather x1, blocking collectives, on_device(): lax.all_gather(jnp.concatenate([w_bc, w_dt], axis=1), both, axis=0, tiled...  56.9 us
    all_gather x1, waiting for transfers between devices, on_device(): cot_all = lax.all_gather(cotangent, 'sp', axis=0, tiled=False)  49.2 us
    psum x1, blocking collectives, on_device(): g_bc = lax.psum(dtaps[:5, chans:], both)  42.2 us
    pallas_call x1, Pallas kernels, run_backward(): pl.pallas_call(functools.partial(scan_backward, wide, chans, inner), grid...  37.6 us
    reduce_scatter x1, waiting for transfers between devices, on_device(): lax.psum_scatter(d_part, 'sp', scatter_dimension=0, tiled=False).astype(F32)  29.7 us
  transfers between devices with their start and end apart: 11, of which 4 were waited for; matrix products, arithmetic and copies ran while one was open for 12% of the time, Pallas kernels for 3%

profile of v1, /device:TPU:0, one launch (start us, length us, event | category | flops | bytes accessed | tf_op | source)
XLA Modules:
  0.0 583.7 jit_solution(16051059752054707266)
XLA Ops:
  7.2 1.2 copy.77
  8.5 0.5 copy.63
  9.0 22.9 %all_to_all.10 = bf16[8,48,2,384]{3,2,1,0:T(2,128)(2,1)S(1)} all-to-all(bf16[8,48,2,384]{3,2,1,0:T(2,128)(2,1)S(1)} %copy.63), channel_id=1, replica_groups=mesh['dp'=4,'sp'=8] {'sp'}, dimensions={0} | all-to-all | bytes 1179648 | tf_op jit(solution)/shard_map/all_to_all | solution.py:337
  31.9 0.9 copy.64
  32.8 0.7 all-gather.11.cloned.1.call-update
  33.6 0.7 collective-permute-start
  34.3 0.7 copy-done.11
  35.1 0.5 all-gather.15.cloned.1.call-update
  36.0 0.2 dynamic-update-slice
  36.2 62.3 %all-reduce.8 = bf16[5888]{0:T(1024)(128)(2,1)S(1)} all-reduce(bf16[5888]{0:T(1024)(128)(2,1)S(1)} %dynamic-update-slice), channel_id=3, replica_groups=mesh['dp'=4,'sp'=8] {'dp','sp'}, use_global_device_ids=true, to_apply=%add.8 | all-reduce | flops 5888 | bytes 23552
  98.5 0.1 reshape.208
  99.0 56.9 %all_gather.36 = bf16[1536,304]{1,0:T(8,128)(2,1)S(1)} all-gather(bf16[48,304]{1,0:T(8,128)(2,1)S(1)} %pad_maximum_fusion), channel_id=1, replica_groups=mesh['dp'=4,'sp'=8] {'dp','sp'}, dimensions={0}, use_global_device_ids=true | all-gather | bytes 963072 | tf_op jit(solution)/shard_map/all_gather | solution.py:339
  156.3 0.4 slice_reduce_fusion.1
  156.8 0.9 constant_dynamic-slice_fusion.1
  157.8 3.5 copy.65
  161.3 0.5 copy.78
  161.8 9.6 %multiply_reduce_fusion = (f32[8,2,128]{2,1,0:T(2,128)S(1)}, f32[8,2,128,1536]{3,2,1,0:T(8,128)}) fusion(bf16[8,2,128,1536]{3,2,1,0:T(8,128)(2,1)} %bitcast.96), kind=kLoop, calls=%fused_computation.4 | loop fusion | flops 9435136 | bytes 18882560 | tf_op jit(solution)/shard_map/reduce_sum | solution.py:382
  171.5 1.5 fusion.1
  173.0 10.0 %convolution_convert_fusion.2 = bf16[2048,1152]{1,0:T(8,128)(2,1)} fusion(bf16[2048,1536]{1,0:T(8,128)(2,1)S(1)} %fusion.1, bf16[1536,6]{1,0:T(8,128)(2,1)S(1)} %copy-done.10, bf16[1536,256]{1,0:T(8,128)(2,1)S(1)} %slice.108, bf16[1536,768]{1,0:T(8,128)(2,1)S(1)} %bitcast.108), kind=kOutput, calls=%fused_computation.8 | convolution fusion | flops 7264272384 | bytes 14174208 | tf_op jit(solution)/shard_map/dot_general | solution.py:20
  183.0 16.9 %scan_forward.1 = (bf16[8,2,128,384]{3,2,1,0:T(8,128)(2,1)S(1)}, bf16[8,2,128,384]{3,2,1,0:T(8,128)(2,1)S(1)}) custom-call(bf16[8,2,128,1152]{3,2,1,0:T(8,128)(2,1)} %bitcast.93, f32[8,640]{1,0:T(8,128)S(1)} %select_maximum_fusion.taps, f32[8,128]{1,0:T(8,128)S(1)} %select_maximum_fusion.1.heads, f32[8,384]{1,0:T(8,128)S(1)} %pad.41.skip), custom_call_target="tpu_custom_call" | custom-call | tf_op jit(solution)/shard_map/scan_forward/pallas_call | solution.py:247
  199.9 1.2 copy-done
  201.1 49.2 %all-gather.15.cloned.1.call-done = bf16[16,128,1536]{2,1,0:T(8,128)(2,1)} async-done(((bf16[2,128,1536]{2,1,0:T(8,128)(2,1)}), bf16[16,128,1536]{2,1,0:T(8,128)(2,1)}) %all-gather.15.cloned.1.call-update) | async-done | bytes 6291472 | tf_op jit(solution)/shard_map/all_gather | solution.py:335
  250.3 10.0 %multiply_reduce_fusion.2 = (f32[2048]{0:T(1024)S(1)}, f32[2048]{0:T(1024)S(1)}, f32[2048,384]{1,0:T(8,128)}, f32[2048,384]{1,0:T(8,128)}) fusion(f32[384]{0:T(512)S(1)} %dynamic-slice_convert_fusion, bf16[2048,1152]{1,0:T(8,128)(2,1)} %convolution_convert_fusion.2, bf16[8,2,128,384]{3,2,1,0:T(8,128)(2,1)S(1)} %get-tuple-element.21.mixed, ...), kind=kOutput, calls=%fused_computation.23 | convolution fusion | flops 2425352192 | bytes 16926208 | tf_op jit(solution)/shard_map/dot_general | solution.py:20
  260.3 26.6 %psum.42 = f32[2048,2]{0,1:T(2,128)S(1)} all-reduce(f32[2048,2]{0,1:T(2,128)S(1)} %pad_maximum_fusion.1), channel_id=1, replica_groups=mesh['dp'=4,'sp'=8] {'sp'}, use_global_device_ids=true, to_apply=%region_3.4 | all-reduce | flops 4096 | bytes 32768 | tf_op jit(solution)/shard_map/psum | solution.py:400
  287.0 0.4 copy.66
  287.4 1.4 copy-done.1
  288.8 37.6 %scan_backward.1 = (bf16[8,2,128,1152]{3,2,1,0:T(8,128)(2,1)}, f32[8,640]{1,0:T(8,128)S(1)}, f32[8,128]{1,0:T(8,128)S(1)}, f32[8,384]{1,0:T(8,128)S(1)}) custom-call(bf16[8,2,128,1152]{3,2,1,0:T(8,128)(2,1)} %bitcast.94, bf16[8,2,128,1152]{3,2,1,0:T(8,128)(2,1)} %bitcast.95, f32[8,640]{1,0:T(8,128)S(1)} %select_maximum_fusion.taps, ...), custom_call_target="tpu_custom_call" | custom-call | tf_op jit(solution)/shard_map/scan_backward/pallas_call | solution.py:280
  326.4 12.7 %convolution_bitcast_fusion = bf16[1536,1152]{0,1:T(8,128)(2,1)S(1)} fusion(bf16[8,2,128,1152]{3,2,1,0:T(8,128)(2,1)} %get-tuple-element.23, f32[8,2,128,1536]{3,2,1,0:T(8,128)} %get-tuple-element.102, f32[1536]{0:T(1024)S(1)} %reshape.199, f32[8,2,128]{2,1,0:T(2,128)S(1)} %add_rsqrt_fusion), kind=kOutput, calls=%fused_computation.5 | convolution fusion | flops 7257194496 | bytes 20854784 | tf_op jit(solution)/shard_map/dot_general | solution.py:20
  339.1 0.2 slice.147
  339.3 3.9 copy.75
  343.3 7.6 %convolution_convert_fusion.3 = bf16[384,1536]{1,0:T(8,128)(2,1)} fusion(bf16[2048,1536]{1,0:T(8,128)(2,1)} %bitcast.127, f32[2048,384]{1,0:T(8,128)} %get-tuple-element.100, f32[2048]{0:T(1024)S(1)} %bitcast.115, f32[384]{0:T(512)S(1)} %dynamic-slice_convert_fusion), kind=kOutput, calls=%fused_computation.24 | convolution fusion | flops 2418868224 | bytes 10626560 | tf_op jit(solution)/shard_map/dot_general | solution.py:20
  351.1 13.0 %convolution_convert_fusion = bf16[2048,1536]{1,0:T(8,128)(2,1)} fusion(bf16[2048,1152]{1,0:T(8,128)(2,1)} %bitcast.128, bf16[1536,6]{1,0:T(8,128)(2,1)} %constant_dynamic-slice_fusion.1, bf16[1536,256]{1,0:T(8,128)(2,1)S(1)} %copy-done.9, bf16[1536,768]{1,0:T(8,128)(2,1)S(1)} %bitcast.109), kind=kOutput, calls=%fused_computation.6 | convolution fusion | flops 7265058816 | bytes 14174208 | tf_op jit(solution)/shard_map/dot_general | solution.py:20
  364.2 1.2 copy-done.27
  365.4 7.5 %convolution_convert_fusion.1 = bf16[2048,1536]{1,0:T(8,128)(2,1)} fusion(bf16[384,1536]{1,0:T(8,128)(2,1)S(1)} %copy-done.27, f32[2048,384]{1,0:T(8,128)} %get-tuple-element.100, f32[2048]{0:T(1024)S(1)} %bitcast.116, f32[384]{0:T(512)S(1)} %dynamic-slice_convert_fusion), kind=kOutput, calls=%fused_computation.7 | convolution fusion | flops 2421424128 | bytes 10626560 | tf_op jit(solution)/shard_map/dot_general | solution.py:20
  372.9 0.7 copy-done.17
  373.6 0.4 copy-done.2
  374.0 0.2 multiply_reduce_fusion.3
  374.2 14.8 %reduce-scatter.13.cloned.1.call-done = bf16[384,1030]{1,0:T(8,128)(2,1)} async-done(((bf16[1536,1030]{1,0:T(8,128)(2,1)}), bf16[384,1030]{1,0:T(8,128)(2,1)}) %reduce-scatter.13.cloned.1.call-update) | async-done | bytes 791056 | tf_op jit(solution)/shard_map/reduce_scatter | solution.py:426
  389.0 4.6 all-to-all-start.1
  393.7 0.1 reduce_sum.108
  393.9 42.2 %psum.43 = f32[5,256]{1,0:T(8,128)S(1)} all-reduce(f32[5,256]{1,0:T(8,128)S(1)} %slice.98), channel_id=1, replica_groups=mesh['dp'=4,'sp'=8] {'dp','sp'}, use_global_device_ids=true, to_apply=%region_13.14 | all-reduce | flops 1280 | bytes 10240 | tf_op jit(solution)/shard_map/psum | solution.py:453
  436.1 17.3 %all-reduce.9 = (f32[5,384]{1,0:T(8,128)S(1)}, f32[6]{0:T(128)}, f32[6]{0:T(128)}, f32[6]{0:T(128)}) all-reduce(f32[5,384]{1,0:T(8,128)S(1)} %slice.101, f32[6]{0:T(128)S(1)} %get-tuple-element.106, f32[6]{0:T(128)S(1)} %get-tuple-element.105, f32[6]{0:T(128)S(1)} %reduce_sum.108), channel_id=1, replica_groups=mesh['dp'=4,'sp'=8] {'dp'}, use_global_device_ids=true, to_apply=%region_14.15 | all-reduce | flops 1938 | bytes 15504 | tf_op jit(solution)/shard_map/psum | solution.py:450
  453.4 0.5 slice_bitcast_fusion.5
  453.9 0.6 slice_bitcast_fusion.2
  454.5 1.6 collective-permute-start.1
  456.1 0.6 slice_reduce_fusion.6
  456.7 0.6 slice_bitcast_fusion.1
  457.3 1.0 multiply_reduce_fusion.5
  458.3 0.5 convert_divide_fusion
  458.8 1.1 slice.119
  459.9 1.9 reshape.195
  461.9 0.7 copy.69
  462.6 0.4 copy.79
  463.0 1.5 convert_element_type.179
  464.5 1.7 slice_bitcast_fusion
  466.1 1.0 copy.70
  467.2 0.7 copy.72
  467.9 1.0 slice_reduce_fusion
  469.1 0.2 multiply_reduce_fusion.4
  469.3 0.5 convert_divide_fusion.1
  469.9 29.7 %reduce-scatter.9.cloned.1.call-done = bf16[1,256,1536]{2,1,0:T(8,128)(2,1)} async-done(((bf16[8,256,1536]{2,1,0:T(8,128)(2,1)}), bf16[1,256,1536]{2,1,0:T(8,128)(2,1)}) %reduce-scatter.9.cloned.1.call-update) | async-done | bytes 786448 | tf_op jit(solution)/shard_map/reduce_scatter | solution.py:420
  499.5 1.6 fusion.12
  501.1 72.0 %reduce-scatter.7.cloned.1.call-done = bf16[1,256,1536]{2,1,0:T(8,128)(2,1)} async-done(((bf16[8,256,1536]{2,1,0:T(8,128)(2,1)}), bf16[1,256,1536]{2,1,0:T(8,128)(2,1)}) %reduce-scatter.7.cloned.1.call-update) | async-done | bytes 786448 | tf_op jit(solution)/shard_map/reduce_scatter | solution.py:404
  573.2 3.2 add_convert_fusion
  (122 shorter events, 2.1 us)
Async XLA Ops:
  7.2 26.4 %copy-start.12 = (bf16[96,1536]{1,0:T(8,128)(2,1)S(1)}, bf16[96,1536]{1,0:T(8,128)(2,1)}, u32[]{:S(2)}) copy-start(bf16[96,1536]{1,0:T(8,128)(2,1)} %param.28) | copy-start | bytes 884740
  7.2 150.6 %all-gather.13.cloned.1.call-start = ((), (), s32[]{:S(2)}) async-start(), calls=%async_computation.11 | async-start | bytes 2949120 | tf_op jit(solution)/shard_map/all_gather | solution.py:338
  8.4 27.2 %copy-start.21 = (bf16[8,4]{0,1:T(4,128)(2,1)S(1)}, bf16[8,4]{0,1:T(4,128)(2,1)}, u32[]{:S(2)}) copy-start(bf16[8,4]{0,1:T(4,128)(2,1)} %param.20) | copy-start | bytes 196
  8.4 27.2 %copy-start.23 = (bf16[8]{0:T(256)(128)(2,1)S(1)}, bf16[8]{0:T(256)(128)(2,1)}, u32[]{:S(2)}) copy-start(bf16[8]{0:T(256)(128)(2,1)} %param.21) | copy-start | bytes 52
  8.4 27.4 %copy-start.19 = (bf16[48]{0:T(256)(128)(2,1)S(1)}, bf16[48]{0:T(256)(128)(2,1)}, u32[]{:S(2)}) copy-start(bf16[48]{0:T(256)(128)(2,1)} %param.19) | copy-start | bytes 292
  8.5 27.4 %copy-start.25 = (bf16[96]{0:T(256)(128)(2,1)S(1)}, bf16[96]{0:T(256)(128)(2,1)}, u32[]{:S(2)}) copy-start(bf16[96]{0:T(256)(128)(2,1)} %param.27) | copy-start | bytes 580
  8.5 90.4 %copy-start.22 = (bf16[384]{0:T(512)(128)(2,1)S(1)}, bf16[384]{0:T(512)(128)(2,1)}, u32[]{:S(2)}) copy-start(bf16[384]{0:T(512)(128)(2,1)} %param.23) | copy-start | bytes 2308
  8.5 90.5 %copy-start.15 = (bf16[48,256]{1,0:T(8,128)(2,1)S(1)}, bf16[48,256]{1,0:T(8,128)(2,1)}, u32[]{:S(2)}) copy-start(bf16[48,256]{1,0:T(8,128)(2,1)} %param.17) | copy-start | bytes 73732
  8.5 90.5 %copy-start.16 = (bf16[48,48]{1,0:T(8,128)(2,1)S(1)}, bf16[48,48]{1,0:T(8,128)(2,1)}, u32[]{:S(2)}) copy-start(bf16[48,48]{1,0:T(8,128)(2,1)} %param.18) | copy-start | bytes 13828
  31.9 124.1 %copy-start.24 = (bf16[6]{0:T(256)(128)(2,1)S(1)}, bf16[6]{0:T(256)(128)(2,1)}, u32[]{:S(2)}) copy-start(bf16[6]{0:T(256)(128)(2,1)} %param.26) | copy-start | bytes 40
  32.7 124.0 %copy-start.28 = (bf16[6]{0:T(256)(128)(2,1)S(1)}, bf16[6]{0:T(256)(128)(2,1)}, u32[]{:S(2)}) copy-start(bf16[6]{0:T(256)(128)(2,1)} %param.25) | copy-start | bytes 40
  32.8 124.0 %copy-start.29 = (bf16[6]{0:T(256)(128)(2,1)S(1)}, bf16[6]{0:T(256)(128)(2,1)}, u32[]{:S(2)}) copy-start(bf16[6]{0:T(256)(128)(2,1)} %param.24) | copy-start | bytes 40
  32.8 124.0 %copy-start.18 = (bf16[384,4]{0,1:T(4,128)(2,1)S(1)}, bf16[384,4]{0,1:T(4,128)(2,1)}, u32[]{:S(2)}) copy-start(bf16[384,4]{0,1:T(4,128)(2,1)} %param.22) | copy-start | bytes 9220
  32.8 129.0 %all-gather.11.cloned.1.call-start = ((), (), s32[]{:S(2)}) async-start(), calls=%async_computation.10 | async-start | bytes 7077888 | tf_op jit(solution)/shard_map/all_gather | solution.py:334
  33.5 167.6 %all-gather.9.cloned.1.call-start = ((), (), s32[]{:S(2)}) async-start(), calls=%async_computation.6 | async-start | bytes 1474560 | tf_op jit(solution)/shard_map/all_gather | solution.py:348
  33.6 0.7 collective-permute-start
  34.3 0.7 copy-start.11
  35.0 215.3 %all-gather.15.cloned.1.call-start = ((), (), s32[]{:S(2)}) async-start(), calls=%async_computation.12 | async-start | bytes 7077888 | tf_op jit(solution)/shard_map/all_gather | solution.py:335
  35.6 353.4 %reduce-scatter.13.cloned.1.call-start = ((), (), s32[]{:S(2)}) async-start(), calls=%async_computation.13 | async-start | bytes 4423680 | tf_op jit(solution)/shard_map/reduce_scatter | solution.py:426
  155.9 17.0 %copy-start.8 = (bf16[1536,256]{1,0:T(8,128)(2,1)}, bf16[1536,256]{1,0:T(8,128)(2,1)S(1)}, u32[]{:S(2)}) copy-start(bf16[1536,256]{1,0:T(8,128)(2,1)S(1)} %slice.108) | copy-start | bytes 2359300
  161.7 11.2 %copy-start.5 = (bf16[192,8,2,384]{3,1,2,0:T(8,128)(2,1)}, bf16[192,8,2,384]{3,1,2,0:T(8,128)(2,1)S(1)}, u32[]{:S(2)}) copy-start(bf16[192,8,2,384]{3,1,2,0:T(8,128)(2,1)S(1)} %copy.78) | copy-start | bytes 7077892
  161.8 9.7 %slice-start = ((s8[6291456]{0:T(1024)(128)(4,1)}), s8[4194304]{0:T(1024)(128)(4,1)S(1)}, s32[]{:S(2)}) async-start(s8[6291456]{0:T(1024)(128)(4,1)} %bitcast.97), calls=%async_computation.14 | async-start | bytes 8388608
  161.8 9.6 %slice-start.1 = ((s8[6291456]{0:T(1024)(128)(4,1)}), s8[2097152]{0:T(1024)(128)(4,1)S(1)}, s32[]{:S(2)}) async-start(s8[6291456]{0:T(1024)(128)(4,1)} %bitcast.97), calls=%async_computation.15 | async-start | bytes 4194304
  171.5 1.5 copy-start.10
  199.9 1.2 copy-start
  287.3 1.4 copy-start.1
  343.2 111.2 %reduce-scatter.11.cloned.1.call-start = ((), (), s32[]{:S(2)}) async-start(), calls=%async_computation.9 | async-start | bytes 1474560 | tf_op jit(solution)/shard_map/reduce_scatter | solution.py:409
  343.3 7.7 %copy-start.6 = (bf16[192,8,2,384]{3,1,2,0:T(8,128)(2,1)S(1)}, bf16[192,8,2,384]{3,1,2,0:T(8,128)(2,1)}, u32[]{:S(2)}) copy-start(bf16[192,8,2,384]{3,1,2,0:T(8,128)(2,1)} %copy-done.5) | copy-start | bytes 7077892
  343.3 7.7 %copy-start.9 = (bf16[1536,256]{1,0:T(8,128)(2,1)S(1)}, bf16[1536,256]{1,0:T(8,128)(2,1)}, u32[]{:S(2)}) copy-start(bf16[1536,256]{1,0:T(8,128)(2,1)} %copy-done.8) | copy-start | bytes 2359300
  351.0 148.5 %reduce-scatter.9.cloned.1.call-start = ((), (), s32[]{:S(2)}) async-start(), calls=%async_computation.8 | async-start | bytes 7077888 | tf_op jit(solution)/shard_map/reduce_scatter | solution.py:420
  364.1 1.3 copy-start.27
  364.1 209.0 %reduce-scatter.7.cloned.1.call-start = ((), (), s32[]{:S(2)}) async-start(), calls=%async_computation.7 | async-start | bytes 7077888 | tf_op jit(solution)/shard_map/reduce_scatter | solution.py:404
  372.8 0.7 copy-start.17
  372.8 1.1 copy-start.2
  372.8 84.5 %copy-start.13 = (bf16[96,1536]{1,0:T(8,128)(2,1)S(1)}, bf16[96,1536]{1,0:T(8,128)(2,1)}, u32[]{:S(2)}) copy-start(bf16[96,1536]{1,0:T(8,128)(2,1)} %param.28) | copy-start | bytes 884740
  373.5 84.8 %copy-start.26 = (bf16[96]{0:T(256)(128)(2,1)S(1)}, bf16[96]{0:T(256)(128)(2,1)}, u32[]{:S(2)}) copy-start(bf16[96]{0:T(256)(128)(2,1)} %param.27) | copy-start | bytes 580
  389.0 69.8 %all-to-all-start.1 = ((bf16[8,48,1030]{2,1,0:T(8,128)(2,1)}), bf16[8,48,1030]{2,1,0:T(8,128)(2,1)S(1)}, u32[]{:S(2)}, u32[]{:S(2)}) async-start(bf16[8,48,1030]{2,1,0:T(8,128)(2,1)} %bitcast.112), calls=%async_computation.3 | async-start | bytes 1769472 | tf_op jit(solution)/shard_map/all_to_all | solution.py:428
  454.5 2.8 collective-permute-start.1
  462.6 6.5 %copy-start.7 = (bf16[48,6144]{1,0:T(8,128)(2,1)S(1)}, bf16[48,6144]{1,0:T(8,128)(2,1)}, u32[]{:S(2)}) copy-start(bf16[48,6144]{1,0:T(8,128)(2,1)} %param.16) | copy-start | bytes 1769476
  462.9 38.2 %copy-start.3 = (f32[6,8,16,384]{3,1,2,0:T(8,128)}, f32[6,8,16,384]{3,1,2,0:T(8,128)S(1)}, u32[]{:S(2)}) copy-start(f32[6,8,16,384]{3,1,2,0:T(8,128)S(1)} %copy.79) | copy-start | bytes 3538948
  463.0 6.4 %copy-start.20 = (bf16[48]{0:T(256)(128)(2,1)S(1)}, bf16[48]{0:T(256)(128)(2,1)}, u32[]{:S(2)}) copy-start(bf16[48]{0:T(256)(128)(2,1)} %param.19) | copy-start | bytes 292
  464.5 108.7 %copy-start.4 = (bf16[2,128,1536]{2,1,0:T(8,128)(2,1)S(1)}, bf16[2,128,1536]{2,1,0:T(8,128)(2,1)}, u32[]{:S(2)}) copy-start(bf16[2,128,1536]{2,1,0:T(8,128)(2,1)} %param.29) | copy-start | bytes 2359300
  469.0 107.4 %copy-start.14 = (f32[48,256]{1,0:T(8,128)}, f32[48,256]{1,0:T(8,128)S(1)}, u32[]{:S(2)}) copy-start(f32[48,256]{1,0:T(8,128)S(1)} %slice_reduce_fusion) | copy-start | bytes 147460
Sparse Core Ops, SparseCore 0:
  32.9 44.4 all-gather.12
  79.0 76.1 all-gather.10
  157.7 26.3 all-gather.8
  185.5 64.7 all-gather.14
  343.4 45.6 reduce-scatter.12
  392.4 28.6 reduce-scatter.10
  423.4 76.1 reduce-scatter.8
  501.8 71.3 reduce-scatter.6

commit v2 on v1

v2 whole, which is shorter than its diff:
```python
import functools

import jax
import jax.numpy as jnp
from jax import lax
from jax.experimental import pallas as pl
from jax.experimental.pallas import tpu as pltpu
from jax.sharding import PartitionSpec as P

P_SIZE = 64
EPS = 1e-05
F32 = jnp.float32
BF16 = jnp.bfloat16
HIGH = lax.Precision.HIGHEST
LANES = 128
VMEM_LIMIT = 48 * 1024 * 1024


def dot(left, right, dims=((1,), (0,)), precision=None):
    return lax.dot_general(
        left, right, (dims, ((), ())), precision=precision, preferred_element_type=F32
    )


def iota(shape, axis):
    return lax.broadcasted_iota(jnp.int32, shape, axis)


def spread(cols, pair, low_half):
    return jnp.where(low_half, cols[:, 2 * pair : 2 * pair + 1], cols[:, 2 * pair + 1 : 2 * pair + 2])


def spread_all(cols, pairs, low_half):
    return jnp.concatenate([spread(cols, pair, low_half) for pair in range(pairs)], axis=1)


def stack_heads(values, low_half):
    zero = jnp.zeros_like(values)
    return jnp.concatenate(
        [jnp.where(low_half, values, zero), jnp.where(low_half, zero, values)], axis=0
    )


def softplus(value):
    return jnp.maximum(value, 0.0) + jnp.log1p(jnp.exp(-jnp.abs(value)))


def conv_pre(ext, rows, taps):
    total = taps[4:5, :]
    for tap in range(4):
        total = total + taps[tap : tap + 1, :] * ext[pl.ds(5 + tap, rows), :]
    return total


def steps_of(dt_raw, head_ref):
    pre = dt_raw.astype(F32) + head_ref[0:1, :]
    steps = softplus(pre)
    return pre, steps, -steps * head_ref[1:2, :]


def scan_forward(wide, chans, x, bd, taps, heads, skip, mixed, enter, ext, halo, state):
    rows = x.shape[0]
    pairs = chans // LANES
    low_half = iota((rows, LANES), 1) < P_SIZE

    @pl.when(pl.program_id(0) == 0)
    def _():
        halo[...] = jnp.zeros(halo.shape, F32)
        state[...] = jnp.zeros(state.shape, F32)

    ext[0:8, :] = halo[...]
    ext[8 : 8 + rows, :chans] = x[...].astype(F32)
    ext[8 : 8 + rows, chans:] = bd[:, :wide].astype(F32)
    halo[...] = ext[rows : rows + 8, :]
    pre = conv_pre(ext, rows, taps)
    act = (pre * jax.nn.sigmoid(pre)).astype(BF16)
    half = wide // 2
    bmat = act[:, chans : chans + half]
    cmat = act[:, chans + half :]
    _, steps, logs = steps_of(bd[:, wide:], heads)
    earlier = iota((rows, rows), 0) >= iota((rows, rows), 1)
    cumul = dot(earlier.astype(F32), logs, precision=HIGH)
    cumul_t = cumul.T
    last = cumul[rows - 1 :, :]
    scores = dot(cmat, bmat, ((1,), (1,)))
    grown = jnp.exp(cumul)
    to_end = steps * jnp.exp(last - cumul)
    final = jnp.exp(last)
    entering = state[...]
    enter[...] = entering.astype(BF16)
    across = dot(cmat, entering.astype(BF16))
    for pair in range(pairs):
        lanes = slice(pair * LANES, (pair + 1) * LANES)
        weights = []
        for head in (2 * pair, 2 * pair + 1):
            differ = cumul[:, head : head + 1] - cumul_t[head : head + 1, :]
            decay = jnp.where(earlier, jnp.exp(jnp.minimum(differ, 0.0)), 0.0)
            weights.append((decay * scores).astype(BF16))
        values = act[:, lanes].astype(F32)
        scaled = (values * spread(steps, pair, low_half)).astype(BF16)
        total = dot(jnp.concatenate(weights, axis=1), stack_heads(scaled, low_half))
        total = total + spread(grown, pair, low_half) * across[:, lanes]
        total = total + skip[0:1, lanes] * values
        mixed[:, lanes] = total.astype(BF16)
        ending = (values * spread(to_end, pair, low_half)).astype(BF16)
        state[:, lanes] = entering[:, lanes] * spread(final, pair, low_half[0:1, :]) + dot(
            bmat, ending, ((0,), (0,))
        )


def scan_backward(
    wide, chans, inner,
    gate_in, x, x_before, bd, bd_before, taps, heads, skip, gain, mixed, enter, grads, sums,
    dgate, dx_out, dbd, dtaps, dheads, dskip,
    ext, gext, halo, dstate,
):
    step = pl.program_id(0)
    chunk = pl.num_programs(0) - 1 - step
    rows = x.shape[0]
    pairs = chans // LANES
    half = wide // 2
    low_half = iota((rows, LANES), 1) < P_SIZE

    @pl.when(step == 0)
    def _():
        halo[...] = jnp.zeros(halo.shape, F32)
        dstate[...] = jnp.zeros(dstate.shape, F32)
        dtaps[...] = jnp.zeros_like(dtaps)
        dheads[...] = jnp.zeros_like(dheads)
        dskip[...] = jnp.zeros_like(dskip)

    gate = gate_in[...].astype(F32)
    sig = jax.nn.sigmoid(gate)
    silu = gate * sig
    mix = mixed[...].astype(F32)
    scale = lax.rsqrt(sums[:, 0:1] * (1.0 / inner) + EPS)
    mean = sums[:, 1:2] * scale * (1.0 / inner)
    back = scale * (grads[...] * gain[0:1, :] - mix * silu * (scale * mean))
    dy_half = (back * silu).astype(BF16)
    dgate[...] = (back * mix * sig * (1.0 + gate * (1.0 - sig))).astype(BF16)
    dy = dy_half.astype(F32)

    last_rows = x_before.shape[0] - 8
    past = jnp.concatenate(
        [x_before[last_rows:, :], bd_before[last_rows:, :wide]], axis=1
    ).astype(F32)
    ext[0:8, :] = jnp.where(chunk == 0, 0.0, past)
    ext[8 : 8 + rows, :chans] = x[...].astype(F32)
    ext[8 : 8 + rows, chans:] = bd[:, :wide].astype(F32)
    pre = conv_pre(ext, rows, taps)
    sig_pre = jax.nn.sigmoid(pre)
    act = (pre * sig_pre).astype(BF16)
    slope = sig_pre * (1.0 + pre * (1.0 - sig_pre))
    bmat = act[:, chans : chans + half]
    cmat = act[:, chans + half :]
    xmat = act[:, :chans]
    xval = xmat.astype(F32)
    dt_pre, steps, logs = steps_of(bd[:, wide:], heads)
    row, col = iota((rows, rows), 0), iota((rows, rows), 1)
    cumul = dot((row >= col).astype(F32), logs, precision=HIGH)
    cumul_t = cumul.T
    last = cumul[rows - 1 :, :]
    later = row <= col
    scores = dot(bmat, cmat, ((1,), (1,)))
    grown = jnp.exp(cumul)
    shrunk = jnp.exp(last - cumul)
    final = jnp.exp(last)
    entering = enter[...]
    dleave = dstate[...]
    dleave_half = dleave.astype(BF16)
    from_state = dot(bmat, dleave_half)
    across = dot(cmat, entering)
    grown_all = spread_all(grown, pairs, low_half)
    ending_all = spread_all(steps * shrunk, pairs, low_half)
    dy_grown = (dy * grown_all).astype(BF16)
    x_end = (xval * ending_all).astype(BF16)
    dstate[...] = dleave * spread_all(final, pairs, low_half[0:1, :]) + dot(
        cmat, dy_grown, ((0,), (0,))
    )
    owner = (iota((chans, LANES), 0) // P_SIZE == iota((chans, LANES), 1)).astype(F32)
    near = dot(xval * from_state, owner, precision=HIGH) * shrunk
    reach = dot(dy * across, owner, precision=HIGH) * grown
    kept = jnp.sum(entering.astype(F32) * dleave, axis=0, keepdims=True)
    kept = dot(jnp.broadcast_to(kept, (8, chans)), owner, precision=HIGH)[0:1, :] * final
    pairs_sum = jnp.zeros((rows, rows), F32)
    head_lane = iota((rows, LANES), 1)
    col_sum = jnp.zeros((rows, LANES), F32)
    row_sums = []
    for pair in range(pairs):
        lanes = slice(pair * LANES, (pair + 1) * LANES)
        products = dot(stack_heads(xmat[:, lanes], low_half), dy_half[:, lanes], ((1,), (1,)))
        weights = []
        for place, head in enumerate((2 * pair, 2 * pair + 1)):
            product = products[place * rows : (place + 1) * rows, :]
            differ = cumul_t[head : head + 1, :] - cumul[:, head : head + 1]
            decay = jnp.where(later, jnp.exp(jnp.minimum(differ, 0.0)), 0.0)
            weight = decay * scores
            step_col = steps[:, head : head + 1]
            weights.append(weight.astype(BF16))
            pairs_sum = pairs_sum + decay * product * step_col
            terms = weight * product
            col_sum = jnp.where(head_lane == head, jnp.sum(terms, axis=1, keepdims=True), col_sum)
            row_sums.append(jnp.sum(terms * step_col, axis=0, keepdims=True))
        inside = dot(
            jnp.concatenate(weights, axis=1), stack_heads(dy_half[:, lanes], low_half)
        )
        dx = spread(steps, pair, low_half) * (
            inside + spread(shrunk, pair, low_half) * from_state[:, lanes]
        )
        dx = dx + skip[0:1, lanes] * dy[:, lanes]
        gext[0:rows, lanes] = dx * slope[:, lanes]
    pairs_half = pairs_sum.astype(BF16)
    d_b = dot(pairs_half, cmat) + dot(x_end, dleave_half, ((1,), (1,)))
    d_c = dot(pairs_half, bmat, ((0,), (0,))) + dot(dy_grown, entering, ((1,), (1,)))
    gext[0:rows, chans : chans + half] = d_b * slope[:, chans : chans + half]
    gext[0:rows, chans + half :] = d_c * slope[:, chans + half :]

    row_sum = jnp.concatenate(
        row_sums + [jnp.zeros((LANES - 2 * pairs, rows), F32)], axis=0
    ).T
    d_logs = dot((row <= col).astype(F32), row_sum - steps * col_sum + reach, precision=HIGH)
    d_logs = d_logs + dot((row > col).astype(F32), steps * near, precision=HIGH) + kept
    d_steps = col_sum + near - heads[1:2, :] * d_logs
    d_pre = d_steps * jax.nn.sigmoid(dt_pre)
    dbd[:, wide:] = d_pre.astype(BF16)
    dheads[0:1, :] += jnp.sum(d_pre, axis=0, keepdims=True)
    dheads[1:2, :] += jnp.sum(d_logs * logs, axis=0, keepdims=True)
    dskip[0:1, :] += jnp.sum(dy * xval, axis=0, keepdims=True)

    gext[rows : rows + 8, :] = halo[...]
    g = gext[0:rows, :]
    halo[...] = g[0:8, :]
    d_in = jnp.zeros((rows, chans + wide), F32)
    for tap in range(4):
        d_in = d_in + taps[tap : tap + 1, :] * gext[pl.ds(3 - tap, rows), :]
        dtaps[tap : tap + 1, :] += jnp.sum(g * ext[pl.ds(5 + tap, rows), :], axis=0, keepdims=True)
    dtaps[4:5, :] += jnp.sum(g, axis=0, keepdims=True)
    dx_out[...] = d_in[:, :chans].astype(BF16)
    dbd[:, :wide] = d_in[:, chans:].astype(BF16)


def run_forward(x, bd, taps, heads, skip, wide):
    blocks, rows, chans = x.shape
    states = wide // 2
    block = lambda n: pl.BlockSpec((None, rows, n), lambda i: (i, 0, 0))
    whole = lambda a: pl.BlockSpec(a.shape, lambda i: (0,) * a.ndim)
    return pl.pallas_call(
        functools.partial(scan_forward, wide, chans),
        grid=(blocks,),
        in_specs=[block(chans), block(bd.shape[2]), whole(taps), whole(heads), whole(skip)],
        out_specs=[block(chans), pl.BlockSpec((None, states, chans), lambda i: (i, 0, 0))],
        out_shape=[
            jax.ShapeDtypeStruct((blocks, rows, chans), BF16),
            jax.ShapeDtypeStruct((blocks, states, chans), BF16),
        ],
        scratch_shapes=[
            pltpu.VMEM((rows + 8, chans + wide), F32),
            pltpu.VMEM((8, chans + wide), F32),
            pltpu.VMEM((states, chans), F32),
        ],
        compiler_params=pltpu.CompilerParams(vmem_limit_bytes=VMEM_LIMIT),
        name="scan_forward",
    )(x, bd, taps, heads, skip)


def run_backward(gate, x, bd, taps, heads, skip, gain, mixed, enter, grads, sums, wide, inner):
    blocks, rows, chans = x.shape
    states = wide // 2
    back = lambda i: blocks - 1 - i
    block = lambda n: pl.BlockSpec((None, rows, n), lambda i: (back(i), 0, 0))
    whole = lambda a: pl.BlockSpec(a.shape, lambda i: (0,) * a.ndim)
    before = lambda n: pl.BlockSpec(
        (None, 16, n), lambda i: (jnp.maximum(back(i) - 1, 0), rows // 16 - 1, 0)
    )
    fixed = lambda n: pl.BlockSpec((8, n), lambda i: (0, 0))
    cols = bd.shape[2]
    return pl.pallas_call(
        functools.partial(scan_backward, wide, chans, inner),
        grid=(blocks,),
        in_specs=[
            block(chans), block(chans), before(chans), block(cols), before(cols),
            whole(taps), whole(heads), whole(skip), whole(gain), block(chans),
            pl.BlockSpec((None, states, chans), lambda i: (back(i), 0, 0)),
            block(chans), block(2),
        ],
        out_specs=[
            block(chans), block(chans), block(cols), fixed(chans + wide), fixed(LANES),
            fixed(chans),
        ],
        out_shape=[
            jax.ShapeDtypeStruct(x.shape, BF16),
            jax.ShapeDtypeStruct(x.shape, BF16),
            jax.ShapeDtypeStruct(bd.shape, BF16),
            jax.ShapeDtypeStruct((8, chans + wide), F32),
            jax.ShapeDtypeStruct((8, LANES), F32),
            jax.ShapeDtypeStruct((8, chans), F32),
        ],
        scratch_shapes=[
            pltpu.VMEM((rows + 8, chans + wide), F32),
            pltpu.VMEM((rows + 8, chans + wide), F32),
            pltpu.VMEM((8, chans + wide), F32),
            pltpu.VMEM((states, chans), F32),
        ],
        compiler_params=pltpu.CompilerParams(vmem_limit_bytes=VMEM_LIMIT),
        name="scan_backward",
    )(gate, x, x, bd, bd, taps, heads, skip, gain, mixed, enter, grads, sums)


MESH = pl.DeviceIdType.MESH
ANY = pl.BlockSpec(memory_space=pl.ANY)


class Place:
    def __init__(self, dp, sp, seqs):
        self.dp, self.sp, self.seqs = dp, sp, seqs
        self.groups = sp // seqs
        self.chips = sp // 2
        self.per = self.groups // 2
        self.p = lax.axis_index("dp")
        self.s = lax.axis_index("sp")
        self.chip = self.s // 2
        self.core = lax.rem(self.s, 2)
        self.seq = self.s // self.groups
        self.group = lax.rem(self.s, self.groups)
        self.low = self.seq * self.per
        self.high = self.low + self.per - 1
        self.bits = [1 << i for i in range(dp.bit_length() - 1)]

    def along_sp(self, other):
        return (self.p, other)

    def along_dp(self, other):
        return (other, self.s)

    def flip(self, bit):
        return self.p + bit - 2 * bit * lax.rem(self.p // bit, 2)

    def masked(self, mask):
        other = self.p
        for bit in self.bits:
            if mask & bit:
                other = other + bit - 2 * bit * lax.rem(self.p // bit, 2)
        return other

    def sp_peer(self, step):
        return lax.rem(self.s + step, self.sp)

    def meet(self, sp_peers=True, dp_peers=True, group_peers=False):
        barrier = pltpu.get_barrier_semaphore()
        peers = []
        if sp_peers:
            peers += [self.along_sp(self.sp_peer(i)) for i in range(1, self.sp)]
        if group_peers:
            peers += [self.along_sp(self.group_peer(i)) for i in range(1, self.groups)]
        if dp_peers:
            peers += [self.along_dp(self.masked(m)) for m in range(1, self.dp)]
        for peer in peers:
            pl.semaphore_signal(barrier, inc=1, device_id=peer, device_id_type=MESH)
        pl.semaphore_wait(barrier, len(peers))

    def group_peer(self, step):
        return self.seq * self.groups + lax.rem(self.group + step, self.groups)


def remote(src, dst, send, recv, device):
    return pltpu.make_async_remote_copy(
        src_ref=src, dst_ref=dst, send_sem=send, recv_sem=recv, device_id=device,
        device_id_type=MESH,
    )


def dma(*shape):
    return pltpu.SemaphoreType.DMA(shape)


class SequenceGather:
    @staticmethod
    def scratch(dp, sp, seqs):
        chips = sp // 2
        return [dma(6, chips), dma(seqs + 1)]

    def __init__(self, place, x, out, sems, more):
        self.at, self.x, self.out = place, x, out
        self.own, self.other, self.up, self.down, self.cross = (sems.at[i] for i in range(5))
        self.far, self.local = more, more.at[place.seqs]

    def copy(self, src, k, chip, core, send, recv):
        at = self.at
        return remote(src, self.out.at[k * 2 + at.core], send, recv, at.along_sp(chip * 2 + core))

    def passes(self, k, src):
        at = self.at
        return (
            ((k <= at.chip) & (at.chip < at.high),
             self.copy(src, k, at.chip + 1, at.core, self.up.at[k], self.own.at[k])),
            ((k >= at.chip) & (at.chip > at.low),
             self.copy(src, k, at.chip - 1, at.core, self.down.at[k], self.own.at[k])),
        )

    def crossing(self, k, src):
        at = self.at
        return self.copy(src, k, at.chip, 1 - at.core, self.cross.at[k], self.other.at[k])

    def far_copies(self):
        at = self.at
        for target in range(at.seqs):
            low = target * at.per
            entry = jnp.where(at.chip < low, low, low + at.per - 1)
            yield target != at.seq, self.copy(
                self.x.at[target], at.chip, entry, at.core, self.far.at[target],
                self.own.at[at.chip],
            )

    def keep(self):
        return pltpu.make_async_copy(self.x.at[self.at.seq], self.out.at[self.at.s], self.local)

    def start(self):
        for needed, copy in self.far_copies():
            pl.when(needed)(copy.start)
        for needed, copy in self.passes(self.at.chip, self.x.at[self.at.seq]):
            pl.when(needed)(copy.start)
        self.crossing(self.at.chip, self.x.at[self.at.seq]).start()
        self.keep().start()

    def step(self, i):
        at = self.at
        for k in (at.chip + i, at.chip - i):

            @pl.when((k >= 0) & (k < at.chips))
            def _():
                src = self.out.at[k * 2 + at.core]
                self.copy(src, k, at.chip, at.core, self.up.at[k], self.own.at[k]).wait_recv()
                for needed, copy in self.passes(k, src):
                    pl.when(needed)(copy.start)
                self.crossing(k, src).start()

    def finish(self):
        at = self.at
        for k in range(at.chips):
            dst = self.out.at[k * 2 + 1 - at.core]
            remote(dst, dst, self.cross.at[k], self.other.at[k], at.along_sp(at.s)).wait_recv()
        for k in range(at.chips):
            src = self.out.at[k * 2 + at.core]
            for needed, copy in self.passes(k, src):
                pl.when(needed)(copy.wait_send)
            self.crossing(k, src).wait_send()
        for needed, copy in self.far_copies():
            pl.when(needed)(copy.wait_send)
        self.keep().wait()


class ShardGather:
    @staticmethod
    def scratch(dp, sp, seqs):
        steps = dp.bit_length() - 1
        return [dma(2, sp), dma(sp, dp), dma(sp, dp, steps), dma(1)]

    def __init__(self, place, piece, out, along, recv, send, local):
        self.at, self.piece, self.out = place, piece, out
        self.along, self.recv, self.send, self.local = along, recv, send, local.at[0]

    def order(self, slot_parity):
        return self.at.bits if slot_parity == 0 else self.at.bits[::-1]

    def sp_copy(self, i):
        at = self.at
        target = at.sp_peer(i)
        return remote(
            self.piece(lax.rem(target, at.groups)), self.out.at[at.p, at.s],
            self.along.at[0, i], self.along.at[1, i], at.along_sp(target),
        )

    def keep(self):
        at = self.at
        return pltpu.make_async_copy(self.piece(at.group), self.out.at[at.p, at.s], self.local)

    def start(self):
        for i in range(1, self.at.sp):
            self.sp_copy(i).start()
        self.keep().start()

    def children(self, slot, parity, mask):
        at, order = self.at, self.order(parity)
        last = max([order.index(b) for b in order if mask & b], default=-1)
        src = self.out.at[at.masked(mask), slot]
        for bit in order[last + 1 :]:
            yield remote(
                src, src, self.send.at[slot, mask, at.bits.index(bit)],
                self.recv.at[slot, mask ^ bit], at.along_dp(at.flip(bit)),
            )

    def slot_of(self, i):
        at = self.at
        return lax.rem(at.s + at.sp - i, at.sp)

    def both(self, slot, fn):
        odd = lax.rem(slot, 2)
        pl.when(odd == 0)(lambda: fn(0))
        pl.when(odd == 1)(lambda: fn(1))

    def along_dp(self, i):
        at = self.at
        slot = self.slot_of(i)
        if i == 0:
            self.keep().wait()
        else:
            dst = self.out.at[at.p, slot]
            remote(dst, dst, self.along.at[0, i], self.along.at[1, i], at.along_sp(at.s)).wait_recv()
        self.both(slot, lambda odd: [copy.start() for copy in self.children(slot, odd, 0)] and None)

    def masks(self, odd):
        return [m for m in sorted(range(1, self.at.dp), key=lambda m: (bin(m).count("1"), m))]

    def forward(self, i):
        at = self.at
        slot = self.slot_of(i)

        def go(odd):
            for mask in self.masks(odd):
                dst = self.out.at[at.masked(mask), slot]
                remote(
                    dst, dst, self.send.at[slot, 0, 0], self.recv.at[slot, mask],
                    at.along_dp(at.p),
                ).wait_recv()
                for copy in self.children(slot, odd, mask):
                    copy.start()

        self.both(slot, go)

    def finish(self):
        for i in range(1, self.at.sp):
            self.sp_copy(i).wait_send()
        for slot in range(self.at.sp):
            for mask in range(self.at.dp):
                for copy in self.children(slot, slot % 2, mask):
                    copy.wait_send()


class OutGather:
    @staticmethod
    def scratch(dp, sp, seqs):
        steps = dp.bit_length() - 1
        return [dma(seqs), dma(sp), dma(2), dma(2, steps), dma(1)]

    def __init__(self, place, x, out, sent, got, recv, send, local):
        self.at, self.x, self.out = place, x, out
        self.sent, self.got, self.recv, self.send, self.local = sent, got, recv, send, local.at[0]
        self.root = place.group == place.p

    def sp_copies(self):
        at = self.at
        for target in range(at.seqs):
            device = target * at.groups + at.p
            yield device != at.s, remote(
                self.x, self.out.at[at.s], self.sent.at[target], self.got.at[at.s],
                at.along_sp(device),
            )

    def keep(self):
        return pltpu.make_async_copy(self.x, self.out.at[self.at.s], self.local)

    def start(self):
        for needed, copy in self.sp_copies():
            pl.when(needed)(copy.start)
        pl.when(self.root)(lambda: self.keep().start())

    def collect(self):
        at = self.at

        @pl.when(self.root)
        def _():
            self.keep().wait()
            for slot in range(at.sp):

                @pl.when(at.s != slot)
                def _():
                    dst = self.out.at[slot]
                    remote(dst, dst, self.sent.at[0], self.got.at[slot], at.along_sp(at.s)).wait_recv()

    def tree(self, odd):
        at = self.at
        order = at.bits if odd == 0 else at.bits[::-1]
        half = at.sp // 2
        part = self.out.at[pl.ds(odd * half, half)]
        digits = {b: (lax.rem(at.p // b, 2) != lax.rem(at.group // b, 2)) for b in at.bits}
        for place, bit in enumerate(order):
            later_clear = jnp.bool_(True)
            for b in order[place + 1 :]:
                later_clear = later_clear & jnp.logical_not(digits[b])
            copy = remote(
                part, part, self.send.at[odd, place], self.recv.at[odd], at.along_dp(at.flip(bit))
            )
            yield later_clear & jnp.logical_not(digits[bit]), later_clear & digits[bit], copy

    def spread(self):
        steps = [list(self.tree(0)), list(self.tree(1))]
        for place in range(len(steps[0])):
            for odd in range(2):
                sends, receives, copy = steps[odd][place]
                pl.when(receives)(copy.wait_recv)
                pl.when(sends)(copy.start)

    def finish(self):
        for needed, copy in self.sp_copies():
            pl.when(needed)(copy.wait_send)
        for odd in range(2):
            for sends, _, copy in self.tree(odd):
                pl.when(sends)(copy.wait_send)


class SequenceReduce:
    @staticmethod
    def scratch(dp, sp, seqs, rows, cols):
        chips = sp // 2
        return [
            pltpu.VMEM((4, chips, rows, cols), BF16),
            dma(7, chips), dma(2, seqs),
        ]

    def __init__(self, place, part, total, bufs, sems, ends):
        self.at, self.part, self.total = place, part, total
        self.acc, self.cross, self.from_low, self.from_high = (bufs.at[i] for i in range(4))
        (self.local, self.cross_send, self.cross_recv, self.chain_send, self.low_recv,
         self.high_recv, self.far_send) = (sems.at[i] for i in range(7))
        self.end_send, self.end_recv = ends.at[0], ends.at[1]

    def keep(self, k):
        at = self.at
        return pltpu.make_async_copy(self.part.at[k * 2 + at.core], self.acc.at[k], self.local.at[k])

    def crossing(self, k):
        at = self.at
        return remote(
            self.part.at[k * 2 + 1 - at.core], self.cross.at[k], self.cross_send.at[k],
            self.cross_recv.at[k], at.along_sp(at.chip * 2 + 1 - at.core),
        )

    def onward(self, k, up):
        at = self.at
        step = 1 if up else -1
        return remote(
            self.acc.at[k], (self.from_low if up else self.from_high).at[k], self.chain_send.at[k],
            (self.low_recv if up else self.high_recv).at[k],
            at.along_sp((at.chip + step) * 2 + at.core),
        )

    def ending(self, k):
        at = self.at
        return remote(
            self.acc.at[k], self.total.at[at.seq], self.far_send.at[k], self.end_recv.at[at.seq],
            at.along_sp(k * 2 + at.core),
        )

    def start(self):
        for k in range(self.at.chips):
            self.crossing(k).start()
            self.keep(k).start()

    def gather(self, k, exit_chip):
        at = self.at
        self.crossing(k).wait_recv()
        self.keep(k).wait()
        self.acc[k] = (self.acc[k].astype(F32) + self.cross[k].astype(F32)).astype(BF16)

        @pl.when((at.chip <= exit_chip) & (at.chip > at.low))
        def _():
            self.onward(k, True).wait_recv()
            self.acc[k] = (self.acc[k].astype(F32) + self.from_low[k].astype(F32)).astype(BF16)

        @pl.when((at.chip >= exit_chip) & (at.chip < at.high))
        def _():
            self.onward(k, False).wait_recv()
            self.acc[k] = (self.acc[k].astype(F32) + self.from_high[k].astype(F32)).astype(BF16)

    def exit_of(self, k):
        return jnp.clip(k, self.at.low, self.at.high)

    def run(self):
        at = self.at
        for i in range(at.chips - 1, 0, -1):
            for k in (at.chip + i, at.chip - i):

                @pl.when((k >= 0) & (k < at.chips))
                def _():
                    out = self.exit_of(k)

                    @pl.when(at.chip != out)
                    def _():
                        self.gather(k, out)
                        pl.when(at.chip < out)(lambda: self.onward(k, True).start())
                        pl.when(at.chip > out)(lambda: self.onward(k, False).start())

        for i in range(at.chips - 1, 0, -1):
            for k in (at.chip + i, at.chip - i):

                @pl.when((k >= 0) & (k < at.chips))
                def _():
                    out = self.exit_of(k)

                    @pl.when(at.chip == out)
                    def _():
                        self.gather(k, out)
                        self.ending(k).start()

        self.gather(at.chip, at.chip)
        self.total[at.seq] = self.acc[at.chip]

    def finish(self):
        at = self.at
        for target in range(at.seqs):

            @pl.when(target != at.seq)
            def _():
                dst = self.total.at[target]
                remote(dst, dst, self.end_send.at[0], self.end_recv.at[target], at.along_sp(at.s)).wait_recv()

        for k in range(at.chips):
            self.crossing(k).wait_send()
            out = self.exit_of(k)
            pl.when(at.chip < out)(lambda: self.onward(k, True).wait_send())
            pl.when(at.chip > out)(lambda: self.onward(k, False).wait_send())
            pl.when((at.chip == out) & (at.chip != k))(lambda: self.ending(k).wait_send())


class ShardReduce:
    @staticmethod
    def scratch(dp, sp, shape):
        return [
            pltpu.VMEM((dp, sp) + shape, BF16),
            dma(2, dp), dma(2, sp), dma(1),
        ]

    def __init__(self, place, terms, out, buf, along_dp, along_sp, local):
        self.at, self.terms, self.out, self.buf = place, terms, out, buf
        self.dp_sems, self.sp_sems, self.local = along_dp, along_sp, local.at[0]

    def dp_copy(self, mask):
        at = self.at
        return remote(
            self.terms.at[at.masked(mask)], self.buf.at[mask], self.dp_sems.at[0, mask],
            self.dp_sems.at[1, mask], at.along_dp(at.masked(mask)),
        )

    def keep(self):
        return pltpu.make_async_copy(self.terms.at[self.at.p], self.buf.at[0], self.local)

    def sp_copy(self, i):
        at = self.at
        target = at.sp_peer(i)
        return remote(
            self.buf.at[0, target], self.out.at[at.s], self.sp_sems.at[0, i], self.sp_sems.at[1, i],
            at.along_sp(target),
        )

    def back(self):
        at = self.at
        return pltpu.make_async_copy(self.buf.at[0, at.s], self.out.at[at.s], self.local)

    def start(self):
        for mask in range(1, self.at.dp):
            self.dp_copy(mask).start()
        self.keep().start()

    def add(self):
        at = self.at
        self.keep().wait()
        for mask in range(1, at.dp):
            self.dp_copy(mask).wait_recv()
        for i in list(range(1, at.sp)) + [0]:
            slot = at.sp_peer(i)
            total = self.buf[0, slot].astype(F32)
            for mask in range(1, at.dp):
                total = total + self.buf[mask, slot].astype(F32)
            self.buf[0, slot] = total.astype(BF16)
            if i:
                self.sp_copy(i).start()
            else:
                self.back().start()

    def finish(self):
        at = self.at
        for mask in range(1, at.dp):
            self.dp_copy(mask).wait_send()
        for i in range(1, at.sp):
            dst = self.out.at[lax.rem(at.s + at.sp - i, at.sp)]
            remote(dst, dst, self.sp_sems.at[0, i], self.sp_sems.at[1, i], at.along_sp(at.s)).wait_recv()
            self.sp_copy(i).wait_send()
        self.back().wait()


class OutReduce:
    @staticmethod
    def scratch(dp, sp, seqs, shape):
        return [pltpu.VMEM((dp, sp) + shape, BF16), dma(2, dp), dma(2, sp), dma(1 + seqs)]

    def __init__(self, place, terms, out, buf, dp_sems, sp_sems, local):
        self.at, self.terms, self.out, self.buf = place, terms, out, buf
        self.dp_sems, self.sp_sems, self.local = dp_sems, sp_sems, local
        self.root = place.group == place.p

    def dp_copy(self):
        at = self.at
        return remote(
            self.terms, self.buf.at[at.p], self.dp_sems.at[0, 0], self.dp_sems.at[1, at.p],
            at.along_dp(at.group),
        )

    def keep(self):
        return pltpu.make_async_copy(self.terms, self.buf.at[self.at.p], self.local.at[0])

    def start(self):
        pl.when(self.root)(lambda: self.keep().start())
        pl.when(jnp.logical_not(self.root))(lambda: self.dp_copy().start())

    def sp_copy(self, slot):
        at = self.at
        return remote(
            self.buf.at[at.p, slot], self.out.at[at.seq], self.sp_sems.at[0, slot],
            self.sp_sems.at[1, at.seq], at.along_sp(slot),
        )

    def add(self):
        at = self.at

        @pl.when(self.root)
        def _():
            self.keep().wait()
            for mask in range(1, at.dp):
                other = at.masked(mask)
                dst = self.buf.at[other]
                remote(
                    self.terms, dst, self.dp_sems.at[0, 0], self.dp_sems.at[1, other], at.along_dp(other)
                ).wait_recv()
            for slot in range(at.sp):
                total = self.buf[0, slot].astype(F32)
                for other in range(1, at.dp):
                    total = total + self.buf[other, slot].astype(F32)
                total = total.astype(BF16)

                @pl.when(at.s == slot)
                def _():
                    self.out[at.seq] = total

                @pl.when(at.s != slot)
                def _():
                    self.buf[at.p, slot] = total
                    self.sp_copy(slot).start()

    def finish(self):
        at = self.at
        pl.when(jnp.logical_not(self.root))(lambda: self.dp_copy().wait_send())

        @pl.when(self.root)
        def _():
            for slot in range(at.sp):
                pl.when(at.s != slot)(lambda: self.sp_copy(slot).wait_send())

        for seq in range(at.seqs):
            sender = seq * at.groups + at.p

            @pl.when(sender != at.s)
            def _():
                dst = self.out.at[seq]
                remote(dst, dst, self.sp_sems.at[0, 0], self.sp_sems.at[1, seq], at.along_sp(sender)).wait_recv()


class SmallReduce:
    @staticmethod
    def scratch(dp, sp, seqs, shape):
        return [pltpu.VMEM((dp,) + shape, F32), dma(2, dp), dma(2, sp)]

    def __init__(self, place, x, out, buf, dp_sems, sp_sems):
        self.at, self.x, self.out, self.buf = place, x, out, buf
        self.dp_sems, self.sp_sems = dp_sems, sp_sems

    def dp_copy(self, mask):
        at = self.at
        return remote(
            self.x, self.buf.at[mask], self.dp_sems.at[0, mask], self.dp_sems.at[1, mask],
            at.along_dp(at.masked(mask)),
        )

    def sp_copy(self, i):
        at = self.at
        return remote(
            self.buf.at[0], self.out.at[at.s], self.sp_sems.at[0, i], self.sp_sems.at[1, i],
            at.along_sp(at.sp_peer(i)),
        )

    def start(self):
        for mask in range(1, self.at.dp):
            self.dp_copy(mask).start()

    def add(self):
        at = self.at
        total = self.x[...]
        for mask in range(1, at.dp):
            self.dp_copy(mask).wait_recv()
            total = total + self.buf[mask]
        self.buf[0] = total
        self.out[at.s] = total
        for i in range(1, at.sp):
            self.sp_copy(i).start()

    def finish(self):
        at = self.at
        for mask in range(1, at.dp):
            self.dp_copy(mask).wait_send()
        for i in range(1, at.sp):
            dst = self.out.at[lax.rem(at.s + at.sp - i, at.sp)]
            remote(dst, dst, self.sp_sems.at[0, i], self.sp_sems.at[1, i], at.along_sp(at.s)).wait_recv()
            self.sp_copy(i).wait_send()


def comm_params(number):
    return pltpu.CompilerParams(
        collective_id=number, has_side_effects=True, vmem_limit_bytes=VMEM_LIMIT
    )


def first_kernel(dp, sp, seqs, chans, w_ref, misc_ref, hid_ref, wx_out, misc_out, hid_out, *sems):
    place = Place(dp, sp, seqs)
    inner = w_ref.shape[1] // 2
    columns = lambda g: w_ref.at[:, pl.ds(pl.multiple_of(inner + g * chans, LANES), chans)]
    wx = ShardGather(place, columns, wx_out, *sems[:4])
    misc = ShardGather(place, lambda g: misc_ref, misc_out, *sems[4:8])
    hid = SequenceGather(place, hid_ref, hid_out, *sems[8:])
    place.meet()
    misc.start()
    wx.start()
    hid.start()
    for i in range(sp):
        misc.along_dp(i)
        wx.along_dp(i)
    steps = place.chips - 1
    for i in range(1, steps + 1):
        hid.step(i)
        for slot in range((i - 1) * sp // steps, i * sp // steps):
            misc.forward(slot)
            wx.forward(slot)
    hid.finish()
    misc.finish()
    wx.finish()


def run_first(dp, sp, seqs, chans, w_zx, misc, hidden):
    share = w_zx.shape[0]
    _, rows, cols = hidden.shape
    shards = ShardGather.scratch(dp, sp, seqs)
    return pl.pallas_call(
        functools.partial(first_kernel, dp, sp, seqs, chans),
        in_specs=[ANY] * 3,
        out_specs=[ANY] * 3,
        out_shape=[
            jax.ShapeDtypeStruct((dp, sp, share, chans), BF16),
            jax.ShapeDtypeStruct((dp, sp) + misc.shape, BF16),
            jax.ShapeDtypeStruct((sp, rows, cols), BF16),
        ],
        scratch_shapes=shards + shards + SequenceGather.scratch(dp, sp, seqs),
        compiler_params=comm_params(1),
        name="first_gather",
    )(w_zx, misc, hidden)


def second_kernel(dp, sp, seqs, chans, w_ref, o_ref, cot_ref, wg_out, o_out, cot_out, *sems):
    place = Place(dp, sp, seqs)
    columns = lambda g: w_ref.at[:, pl.ds(pl.multiple_of(g * chans, LANES), chans)]
    wg = ShardGather(place, columns, wg_out, *sems[:4])
    out = OutGather(place, o_ref, o_out, *sems[4:9])
    cot = SequenceGather(place, cot_ref, cot_out, *sems[9:])
    place.meet()
    out.start()
    wg.start()
    cot.start()
    out.collect()
    out.spread()
    for i in range(sp):
        wg.along_dp(i)
    steps = place.chips - 1
    for i in range(1, steps + 1):
        cot.step(i)
        for slot in range((i - 1) * sp // steps, i * sp // steps):
            wg.forward(slot)
    cot.finish()
    out.finish()
    wg.finish()


def run_second(dp, sp, seqs, chans, w_zx, w_out, cotangent):
    share = w_zx.shape[0]
    _, rows, cols = cotangent.shape
    return pl.pallas_call(
        functools.partial(second_kernel, dp, sp, seqs, chans),
        in_specs=[ANY] * 3,
        out_specs=[ANY] * 3,
        out_shape=[
            jax.ShapeDtypeStruct((dp, sp, share, chans), BF16),
            jax.ShapeDtypeStruct((sp,) + w_out.shape, BF16),
            jax.ShapeDtypeStruct((sp, rows, cols), BF16),
        ],
        scratch_shapes=ShardGather.scratch(dp, sp, seqs)
        + OutGather.scratch(dp, sp, seqs)
        + SequenceGather.scratch(dp, sp, seqs),
        compiler_params=comm_params(2),
        name="second_gather",
    )(w_zx, w_out, cotangent)


def sums_kernel(dp, sp, seqs, own, total, got, sems):
    place = Place(dp, sp, seqs)
    place.meet(sp_peers=False, dp_peers=False, group_peers=True)
    copies = []
    for i in range(1, place.groups):
        copies.append(
            remote(
                own, got.at[i], sems.at[0, i], sems.at[1, i], place.along_sp(place.group_peer(i))
            )
        )
        copies[-1].start()
    value = own[...]
    for i, copy in enumerate(copies):
        copy.wait_recv()
        value = value + got[i + 1]
    total[...] = value
    for copy in copies:
        copy.wait_send()


def run_sums(dp, sp, seqs, own):
    groups = sp // seqs
    return pl.pallas_call(
        functools.partial(sums_kernel, dp, sp, seqs),
        in_specs=[pl.BlockSpec(memory_space=pltpu.VMEM)],
        out_specs=pl.BlockSpec(memory_space=pltpu.VMEM),
        out_shape=jax.ShapeDtypeStruct(own.shape, F32),
        scratch_shapes=[pltpu.VMEM((groups,) + own.shape, F32), dma(2, groups)],
        compiler_params=comm_params(3),
        name="norm_sums",
    )(own)


def out_reduce_kernel(dp, sp, seqs, part, total, *scratch):
    place = Place(dp, sp, seqs)
    reduce = SequenceReduce(place, part, total, *scratch)
    place.meet(dp_peers=False)
    reduce.start()
    reduce.run()
    reduce.finish()


def run_out_reduce(dp, sp, seqs, part):
    _, rows, cols = part.shape
    return pl.pallas_call(
        functools.partial(out_reduce_kernel, dp, sp, seqs),
        in_specs=[ANY],
        out_specs=pl.BlockSpec(memory_space=pltpu.VMEM),
        out_shape=jax.ShapeDtypeStruct((seqs, rows, cols), BF16),
        scratch_shapes=SequenceReduce.scratch(dp, sp, seqs, rows, cols),
        compiler_params=comm_params(4),
        name="out_reduce",
    )(part)


def last_kernel(dp, sp, seqs, part, tg, tx, tb, to, small, total, og, ox, ob, oo, osmall, *scratch):
    place = Place(dp, sp, seqs)
    reduce = SequenceReduce(place, part, total, *scratch[:3])
    shards = []
    rest = scratch[3:]
    for terms, out in ((tx, ox), (tb, ob), (tg, og)):
        shards.append(ShardReduce(place, terms, out, *rest[:4]))
        rest = rest[4:]
    outs = OutReduce(place, to, oo, *rest[:4])
    few = SmallReduce(place, small, osmall, *rest[4:])
    place.meet()
    for shard in shards:
        shard.start()
    few.start()
    outs.start()
    reduce.start()
    reduce.run()
    for shard in shards:
        shard.add()
    outs.add()
    few.add()
    reduce.finish()
    for shard in shards:
        shard.finish()
    outs.finish()
    few.finish()


def run_last(dp, sp, seqs, part, terms_gate, terms_x, terms_bd, terms_out, small):
    _, rows, cols = part.shape
    args = (part, terms_gate, terms_x, terms_bd, terms_out, small)
    scratch = SequenceReduce.scratch(dp, sp, seqs, rows, cols)
    for terms in (terms_x, terms_bd, terms_gate):
        scratch += ShardReduce.scratch(dp, sp, terms.shape[2:])
    scratch += OutReduce.scratch(dp, sp, seqs, terms_out.shape[1:])
    scratch += SmallReduce.scratch(dp, sp, seqs, small.shape)
    return pl.pallas_call(
        functools.partial(last_kernel, dp, sp, seqs),
        in_specs=[ANY] * 5 + [pl.BlockSpec(memory_space=pltpu.VMEM)],
        out_specs=[pl.BlockSpec(memory_space=pltpu.VMEM)]
        + [ANY] * 3
        + [pl.BlockSpec(memory_space=pltpu.VMEM)] * 2,
        out_shape=[
            jax.ShapeDtypeStruct((seqs, rows, cols), BF16),
            jax.ShapeDtypeStruct((sp,) + terms_gate.shape[2:], BF16),
            jax.ShapeDtypeStruct((sp,) + terms_x.shape[2:], BF16),
            jax.ShapeDtypeStruct((sp,) + terms_bd.shape[2:], BF16),
            jax.ShapeDtypeStruct((seqs,) + terms_out.shape[1:], BF16),
            jax.ShapeDtypeStruct((sp,) + small.shape, F32),
        ],
        scratch_shapes=scratch,
        compiler_params=comm_params(5),
        name="last_reduce",
    )(*args)


def pad_last(value, size):
    return jnp.pad(value, [(0, 0)] * (value.ndim - 1) + [(0, size - value.shape[-1])])


def eight_rows(*rows):
    stacked = jnp.stack(rows, axis=0)
    return jnp.pad(stacked, ((0, 8 - stacked.shape[0]), (0, 0)))


def on_device(
    dp, sp,
    hidden_in, w_zx, w_bc, w_dt, norm_gain, conv_bc_weight, conv_bc_bias,
    conv_x_weight, conv_x_bias, dt_bias, a_log, d_skip, gate_gain, w_out, cotangent,
):
    me_dp, me_sp = lax.axis_index("dp"), lax.axis_index("sp")
    seqs, block, width = hidden_in.shape
    groups = sp // seqs
    group = lax.rem(me_sp, groups)
    rows = sp * block
    wide, heads = w_bc.shape[1], w_dt.shape[1]
    share, taps_n = w_zx.shape[0], conv_x_weight.shape[1]
    inner = heads * P_SIZE
    chans = inner // groups
    own_heads = heads // groups
    gate_share, bc_share = gate_gain.shape[0], conv_bc_bias.shape[0]
    x_share, head_share = conv_x_bias.shape[0], dt_bias.shape[0]
    cols = wide + LANES

    small = jnp.concatenate(
        [
            norm_gain,
            gate_gain,
            jnp.concatenate([conv_bc_weight, conv_bc_bias[:, None]], axis=1).reshape(-1),
            jnp.concatenate([conv_x_weight, conv_x_bias[:, None]], axis=1).reshape(-1),
            dt_bias,
            a_log,
            d_skip,
        ]
    )
    high = -(-share // 16) * 16
    lines = -(-small.shape[0] // (16 * cols)) * 16
    misc = jnp.concatenate(
        [
            jnp.pad(jnp.concatenate([w_bc, w_dt], axis=1), ((0, high - share), (0, LANES - heads))),
            pad_last(small, lines * cols).reshape(lines, cols),
        ],
        axis=0,
    )
    wx, misc_all, hidden_all = run_first(dp, sp, seqs, chans, w_zx, misc, hidden_in)
    wg, out_mine, cot_all = run_second(dp, sp, seqs, chans, w_zx, w_out, cotangent)

    wx = wx.reshape(width, chans)
    bd_all = misc_all[:, :, :share, :].reshape(width, cols)
    dt_cols = lax.dynamic_slice_in_dim(bd_all[:, wide:], group * own_heads, own_heads, axis=1)
    wb = jnp.concatenate([bd_all[:, :wide], pad_last(dt_cols, LANES)], axis=1)
    few = misc_all[:, :, high:, :].reshape(dp, sp, lines * cols)
    ends = []
    for size in (share, gate_share, bc_share * (taps_n + 1), x_share * (taps_n + 1)) + (head_share,) * 3:
        ends.append(size + (ends[-1] if ends else 0))
    piece = lambda i: few[:, :, (ends[i - 1] if i else 0) : ends[i]]
    mine = lambda i: lax.dynamic_slice_in_dim(piece(i)[0], group * seqs, seqs, axis=0).astype(F32)
    norm_all = piece(0).reshape(width).astype(F32)
    gate_mine = lax.dynamic_slice_in_dim(
        piece(1).reshape(inner), group * chans, chans
    ).astype(F32)
    bc_all = piece(2).reshape(wide, taps_n + 1).astype(F32)
    x_all = mine(3).reshape(chans, taps_n + 1)
    taps = jnp.concatenate([x_all, bc_all], axis=0).T
    taps = jnp.pad(taps, ((0, 8 - taps.shape[0]), (0, 0)))
    head_rows = eight_rows(
        pad_last(mine(4).reshape(own_heads), LANES),
        pad_last(jnp.exp(mine(5).reshape(own_heads)), LANES),
    )
    skip = eight_rows(jnp.repeat(mine(6).reshape(own_heads), P_SIZE))
    gain = eight_rows(gate_mine)

    hidden = hidden_all.reshape(rows, width).astype(F32)
    scale_in = lax.rsqrt(jnp.mean(hidden * hidden, axis=-1, keepdims=True) + EPS)
    normed = (hidden * scale_in * norm_all).astype(BF16)
    x = dot(normed, wx).astype(BF16)
    bd = dot(normed, wb).astype(BF16)
    x_blocks, bd_blocks = x.reshape(sp, block, chans), bd.reshape(sp, block, cols)
    mixed, entering = run_forward(x_blocks, bd_blocks, taps, head_rows, skip, wide)

    gate = dot(normed, wg.reshape(width, chans)).astype(BF16)
    cot_rows = cot_all.reshape(rows, width)
    out_rows = out_mine.reshape(chans, width)
    d_gated = dot(cot_rows, out_rows, ((1,), (1,)))
    gate_f = gate.astype(F32)
    gated_in = mixed.reshape(rows, chans).astype(F32) * gate_f * jax.nn.sigmoid(gate_f)
    sums = jnp.stack(
        [
            jnp.sum(gated_in * gated_in, axis=1),
            jnp.sum(gated_in * d_gated * gain[0:1, :], axis=1),
        ],
        axis=0,
    )
    sums = run_sums(dp, sp, seqs, sums.reshape(2 * sp, block)).reshape(2, rows).T
    scale_out = lax.rsqrt(sums[:, 0:1] * (1.0 / inner) + EPS)
    gated = (gated_in * scale_out * gain[0:1, :]).astype(BF16)
    out_part = dot(gated, out_rows).astype(BF16).reshape(sp, block, width)
    out_sum = run_out_reduce(dp, sp, seqs, out_part)
    hidden_out = (hidden_in.astype(F32) + out_sum.astype(F32)).astype(BF16)
    terms_out = dot(gated, cot_rows, ((0,), (0,))).astype(BF16).reshape(sp, gate_share, width)

    dgate, dx, dbd, dtaps, dheads, dskip = run_backward(
        gate.reshape(sp, block, chans), x_blocks, bd_blocks, taps, head_rows, skip, gain, mixed,
        entering, d_gated.reshape(sp, block, chans), sums.reshape(sp, block, 2), wide, inner,
    )
    dgate, dx, dbd = (v.reshape(rows, -1) for v in (dgate, dx, dbd))
    d_part = (
        dot(dgate, wg.reshape(width, chans), ((1,), (1,)))
        + dot(dx, wx, ((1,), (1,)))
        + dot(dbd, wb, ((1,), (1,)))
    )
    d_part = d_part.astype(BF16).reshape(sp, block, width)
    terms = lambda v: dot(normed, v, ((0,), (0,))).astype(BF16).reshape(dp, sp, share, -1)
    small_terms = jnp.concatenate(
        [jnp.concatenate([dtaps[:5, :chans], dskip[0:1], dtaps[6:8, :chans]], axis=0),
         dtaps[:, chans:], dheads], axis=1,
    )
    d_normed, og, ox, ob, oo, osmall = run_last(
        dp, sp, seqs, d_part, terms(dgate), terms(dx), terms(dbd), terms_out, small_terms
    )
    spread_cols = lambda v: jnp.transpose(
        jnp.sum(v.astype(F32).reshape(seqs, groups, share, -1), axis=0), (1, 0, 2)
    ).reshape(share, -1)
    grad_w_zx = jnp.concatenate([spread_cols(og), spread_cols(ox)], axis=1)
    ob = ob.astype(F32)
    grad_w_bc = jnp.sum(ob[:, :, :wide], axis=0)
    grad_w_dt = spread_cols(ob[:, :, wide : wide + own_heads])
    grad_norm_gain = (
        jnp.sum(grad_w_zx * w_zx.astype(F32), axis=1)
        + jnp.sum(grad_w_bc * w_bc.astype(F32), axis=1)
        + jnp.sum(grad_w_dt * w_dt.astype(F32), axis=1)
    ) / norm_gain.astype(F32)
    grad_w_out = jnp.sum(oo.astype(F32), axis=0)
    grad_gate_gain = jnp.sum(grad_w_out * w_out.astype(F32), axis=1) / gate_gain.astype(F32)

    hid = hidden_in.reshape(seqs * block, width).astype(F32)
    scale_own = lax.rsqrt(jnp.mean(hid * hid, axis=-1, keepdims=True) + EPS)
    unit_own = hid * scale_own
    weighted = d_normed.reshape(seqs * block, width).astype(F32) * norm_all
    grad_rows = cotangent.reshape(seqs * block, width).astype(F32) + scale_own * (
        weighted - unit_own * jnp.mean(weighted * unit_own, axis=-1, keepdims=True)
    )
    grad_hidden = grad_rows.astype(BF16).reshape(hidden_in.shape)

    by_group = jnp.sum(osmall.reshape(seqs, groups, 8, -1), axis=0)
    from_group = lax.dynamic_index_in_dim(by_group, me_sp // seqs, axis=0, keepdims=False)
    part = lax.rem(me_sp, seqs)
    g_x = lax.dynamic_slice_in_dim(from_group[:, :chans], part * x_share, x_share, axis=1)
    g_heads = lax.dynamic_slice_in_dim(
        from_group[:, chans + wide :], part * head_share, head_share, axis=1
    )
    g_skip = jnp.sum(g_x[5].reshape(head_share, P_SIZE), axis=1)
    g_bc = jnp.sum(by_group[:, :, chans : chans + wide], axis=0)
    first = (me_dp * sp + me_sp) * bc_share
    g_bc = lax.dynamic_slice_in_dim(g_bc, first, bc_share, axis=1)
    return (
        hidden_out,
        grad_hidden,
        grad_w_zx,
        grad_w_bc,
        grad_w_dt,
        grad_norm_gain,
        g_bc[:taps_n].T,
        g_bc[taps_n],
        g_x[:taps_n].T,
        g_x[taps_n],
        g_heads[0],
        g_heads[1],
        g_skip,
        grad_gate_gain,
        grad_w_out,
    )


def solution(mesh):
    both = P(("dp", "sp"))
    rows = P(("dp", "sp"), None)
    tokens = P("dp", "sp", None)
    return jax.shard_map(
        functools.partial(on_device, mesh.shape["dp"], mesh.shape["sp"]),
        mesh=mesh,
        in_specs=(
            tokens, rows, rows, rows, both, rows, both, P("sp", None), P("sp"), P("sp"),
            P("sp"), P("sp"), both, rows, tokens,
        ),
        out_specs=(
            tokens, tokens, rows, rows, rows, both, rows, both, P("sp", None), P("sp"),
            P("sp"), P("sp"), P("sp"), both, rows,
        ),
        check_vma=False,
    )
```

time: 591 us -> 545 us (0.922)
  Pallas kernels: 54.6 us -> 450 us
  blocking collectives: 228 us -> 0 us
  waiting for transfers between devices: 167 us -> 0 us
  matrix products: 60.8 us -> 41.1 us
  between operations: 15.2 us -> 1.72 us
  starting transfers between devices: 7.21 us -> 0 us
  other arithmetic: 21.5 us -> 15.5 us
    pallas_call x0 -> x5, Pallas kernels: none -> 406 us  [the longest x1 145 us: run_last(): pl.pallas_call(functools.partial(last_kernel, dp, sp, seqs), in_specs=[AN...]
    reduce_scatter x4 -> x0, waiting for transfers between devices: 117 us -> none  [the longest x1 72 us: on_device(): out_sum = lax.psum_scatter(out_part, 'sp', scatter_dimension=0, tiled=False)]
    psum x3 -> x0, blocking collectives: 86.1 us -> none  [the longest x1 42.2 us: on_device(): g_bc = lax.psum(dtaps[:5, chans:], both)]
    unnamed x1 -> x0, blocking collectives: 62.3 us -> none
    all_gather x1 -> x0, blocking collectives: 56.9 us -> none  [on_device(): lax.all_gather(jnp.concatenate([w_bc, w_dt], axis=1), both, axis=0, tiled...]
    all_gather x4 -> x0, waiting for transfers between devices: 49.3 us -> none  [the longest x1 49.2 us: on_device(): cot_all = lax.all_gather(cotangent, 'sp', axis=0, tiled=False)]
    all_to_all x1 -> x0, blocking collectives: 22.9 us -> none  [on_device(): lax.all_to_all(zx_parts, 'sp', split_axis=0, concat_axis=0, tiled=True)]
    dot_general x6 -> x12, matrix products: 60.8 us -> 41.1 us  [dot(): lax.dot_general(left, right, (dims, ((), ())), precision=precision, prefe...]
  transfers between devices with their start and end apart: 11 -> 0, of which waited for: 4 -> 0; matrix products, arithmetic and copies ran while one was open for 12% -> 0% of each run, Pallas kernels for 3% -> 0%
where the time goes in v2:
time: 545 us; the launch traced here: 535 us
  Pallas kernels  450 us (83%)
  matrix products  41.1 us (8%)
  local copies, waits for them, and re-layouts  27.2 us (5%)
  other arithmetic  15.5 us (3%)
    pallas_call x1, Pallas kernels, run_last(): pl.pallas_call(functools.partial(last_kernel, dp, sp, seqs), in_specs=[AN...  145 us
    pallas_call x1, Pallas kernels, run_second(): pl.pallas_call(functools.partial(second_kernel, dp, sp, seqs, chans), in_...  125 us
    pallas_call x1, Pallas kernels, run_first(): pl.pallas_call(functools.partial(first_kernel, dp, sp, seqs, chans), in_s...  96.4 us
    dot_general x12, matrix products, dot(): lax.dot_general(left, right, (dims, ((), ())), precision=precision, prefe...  41.1 us
    pallas_call x1, Pallas kernels, run_out_reduce(): pl.pallas_call(functools.partial(out_reduce_kernel, dp, sp, seqs), in_spe...  35.8 us
    pallas_call x1, Pallas kernels, run_backward(): pl.pallas_call(functools.partial(scan_backward, wide, chans, inner), grid...  32.2 us
    pallas_call x1, Pallas kernels, run_forward(): pl.pallas_call(functools.partial(scan_forward, wide, chans), grid=(blocks...  12 us

profile of v2, /device:TPU:0, one launch (start us, length us, event | category | flops | bytes accessed | tf_op | source)
XLA Modules:
  0.0 535.4 jit_solution(12081506774079281817)
XLA Ops:
  0.7 1.4 fusion.16
  2.1 0.6 add_rsqrt_fusion.1
  2.6 0.7 broadcast_in_dim.7
  3.3 0.7 pad_maximum_fusion.4
  4.2 0.7 pad_maximum_fusion.3
  4.9 1.4 copy.67
  6.3 0.8 fusion.22
  7.2 0.2 reshape.299
  7.5 3.4 concatenate.34
  10.9 1.1 copy-done.1
  12.1 1.1 copy-done.3
  13.1 96.4 %first_gather.1 = (bf16[4,8,48,768]{3,2,1,0:T(8,128)(2,1)S(1)}, bf16[4,8,64,384]{3,2,1,0:T(8,128)(2,1)S(1)}, bf16[8,128,1536]{2,1,0:T(8,128)(2,1)}) custom-call(bf16[48,6144]{1,0:T(8,128)(2,1)S(1)} %copy-done.3, bf16[64,384]{1,0:T(8,128)(2,1)S(1)} %pad_maximum_fusion.misc_ref, bf16[2,128,1536]{2,1,0:T(8,128)(2,1)S(1)} %copy-done.1), custom_call_target="tpu_custom_call" | custom-call | tf_op jit(solution)/shard_map/first_gather/pallas_call | solution.py:950
  109.5 1.4 copy-done.10
  111.0 2.6 multiply_reduce_fusion
  113.5 0.6 fusion.32
  114.2 1.1 slice.96
  115.3 0.9 reshape.301
  116.2 1.0 fusion.34
  117.7 0.8 slice.130
  118.6 0.8 slice.126
  119.4 0.7 slice_convert_fusion
  120.1 0.8 slice.125
  121.3 0.4 convert_element_type.183
  121.8 1.0 slice.124
  122.8 1.2 slice.123
  124.0 0.2 constant_dynamic-slice_fusion.6
  124.2 0.8 multiply_convert_fusion
  125.0 0.8 fusion.1
  125.8 1.8 convolution_convert_fusion.4
  127.7 2.6 convolution_convert_fusion.3
  130.4 12.0 %scan_forward.1 = (bf16[8,128,768]{2,1,0:T(8,128)(2,1)S(1)}, bf16[8,128,768]{2,1,0:T(8,128)(2,1)S(1)}) custom-call(bf16[8,128,768]{2,1,0:T(8,128)(2,1)S(1)} %bitcast.101, bf16[8,128,384]{2,1,0:T(8,128)(2,1)S(1)} %bitcast.104, f32[8,1024]{1,0:T(8,128)S(1)} %pad_convert_fusion.taps, f32[8,128]{1,0:T(8,128)S(1)} %select_maximum_fusion.heads, f32[8,768]{1,0:T(8,128)S(1)} %pad.45.skip), custom_call_target="tpu_custom_call" | custom-call | tf_op jit(solution)/shard_map/scan_forward/pallas_call | solution.py:247
  142.5 1.2 copy-done.8
  143.7 125.1 %second_gather.1 = (bf16[4,8,48,768]{3,2,1,0:T(8,128)(2,1)S(1)}, bf16[8,96,1536]{2,1,0:T(8,128)(2,1)}, bf16[8,128,1536]{2,1,0:T(8,128)(2,1)}) custom-call(bf16[48,6144]{1,0:T(8,128)(2,1)S(1)} %copy-done.4, bf16[96,1536]{1,0:T(8,128)(2,1)S(1)} %copy-done.9, bf16[2,128,1536]{2,1,0:T(8,128)(2,1)S(1)} %copy-done.5), custom_call_target="tpu_custom_call" | custom-call | tf_op jit(solution)/shard_map/second_gather/pallas_call | solution.py:992
  268.9 2.6 convolution_convert_fusion.2
  271.6 0.7 copy-done.35
  272.3 5.2 multiply_reduce_fusion.2
  277.6 3.8 norm_sums.1
  281.4 7.2 %convolution_convert_fusion.1 = bf16[768,1536]{1,0:T(8,128)(2,1)} fusion(bf16[1024,1536]{1,0:T(8,128)(2,1)} %bitcast.143, f32[1024,768]{1,0:T(8,128)} %get-tuple-element.104, f32[1024]{0:T(1024)S(1)} %bitcast.138, f32[768]{0:T(1024)S(1)} %dynamic-slice_convert_fusion), kind=kOutput, calls=%fused_computation.11 | convolution fusion | flops 2419458048 | bytes 8657920 | tf_op jit(solution)/shard_map/dot_general | solution.py:20
  288.6 3.0 convolution_convert_fusion
  291.7 35.8 %out_reduce.1 = bf16[2,128,1536]{2,1,0:T(8,128)(2,1)S(1)} custom-call(bf16[8,128,1536]{2,1,0:T(8,128)(2,1)S(1)} %bitcast.107), custom_call_target="tpu_custom_call" | custom-call | tf_op jit(solution)/shard_map/out_reduce/pallas_call | solution.py:1053
  327.5 0.2 copy.60
  327.7 32.2 %scan_backward.1 = (bf16[8,128,768]{2,1,0:T(8,128)(2,1)S(1)}, bf16[8,128,768]{2,1,0:T(8,128)(2,1)S(1)}, bf16[8,128,384]{2,1,0:T(8,128)(2,1)S(1)}, f32[8,1024]{1,...) custom-call(bf16[8,128,768]{2,1,0:T(8,128)(2,1)} %bitcast.133, bf16[8,128,768]{2,1,0:T(8,128)(2,1)} %bitcast.102, ...), custom_call_target="tpu_custom_call" | custom-call | tf_op jit(solution)/shard_map/scan_backward/pallas_call | solution.py:277
  360.0 1.8 fusion.6
  361.9 4.0 bitcast_convert_fusion.1
  365.8 4.1 bitcast_convert_fusion
  370.0 2.6 fusion.36
  372.6 2.6 fusion.35
  375.3 3.5 add_convert_fusion
  378.8 144.5 %last_reduce.1 = (bf16[2,128,1536]{2,1,0:T(8,128)(2,1)S(1)}, bf16[8,48,768]{2,1,0:T(8,128)(2,1)S(1)}, bf16[8,48,768]{2,1,0:T(8,128)(2,1)S(1)}, bf16[8,48,384]{2,...) custom-call(bf16[8,128,1536]{2,1,0:T(8,128)(2,1)} %bitcast.120, ...), custom_call_target="tpu_custom_call" | custom-call | tf_op jit(solution)/shard_map/last_reduce/pallas_call | solution.py:1100
  523.5 0.9 copy.72
  524.4 0.9 copy.73
  525.3 0.4 fusion.10
  525.7 1.9 fusion.14
  527.8 0.5 slice_bitcast_fusion.3
  528.3 0.6 slice_bitcast_fusion
  528.9 0.5 slice_bitcast_fusion.1
  529.5 0.7 dynamic-slice_reduce_fusion
  530.1 0.6 dynamic-slice_bitcast_fusion.1
  530.8 0.6 reduce_sum.167
  531.6 0.8 multiply_reduce_fusion.6
  532.4 0.7 copy.68
  533.6 0.5 convert_divide_fusion
  534.2 0.2 multiply_reduce_fusion.3
  534.5 0.6 convert_divide_fusion.1
  (131 shorter events, 3.1 us)
Async XLA Ops:
  10.9 1.1 copy-start.1
  12.1 1.1 copy-start.3
  109.5 1.4 copy-start.10
  115.3 8.9 %copy-start.15 = (bf16[8,128,1536]{2,1,0:T(8,128)(2,1)S(1)}, bf16[8,128,1536]{2,1,0:T(8,128)(2,1)}, u32[]{:S(2)}) copy-start(bf16[8,128,1536]{2,1,0:T(8,128)(2,1)} %get-tuple-element.35) | copy-start | bytes 9437188
  116.2 8.0 %copy-start.30 = (f32[8,128]{1,0:T(8,128)S(1)}, f32[8,128]{1,0:T(8,128)}, u32[]{:S(2)}) copy-start(f32[8,128]{1,0:T(8,128)} %get-tuple-element.113) | copy-start | bytes 12292
  124.0 1.8 copy-start.16
  124.2 1.6 copy-start.26
  125.0 143.9 %copy-start.18 = (bf16[8,128,1536]{2,1,0:T(8,128)(2,1)}, bf16[8,128,1536]{2,1,0:T(8,128)(2,1)S(1)}, u32[]{:S(2)}) copy-start(bf16[8,128,1536]{2,1,0:T(8,128)(2,1)S(1)} %multiply_convert_fusion) | copy-start | bytes 9437188
  125.8 1.9 copy-start.11
  130.3 141.1 %copy-start = (bf16[1024,768]{1,0:T(8,128)(2,1)}, bf16[1024,768]{1,0:T(8,128)(2,1)S(1)}, u32[]{:S(2)}) copy-start(bf16[1024,768]{1,0:T(8,128)(2,1)S(1)} %convolution_convert_fusion.3) | copy-start | bytes 4718596
  130.4 13.3 %copy-start.4 = (bf16[48,6144]{1,0:T(8,128)(2,1)S(1)}, bf16[48,6144]{1,0:T(8,128)(2,1)}, u32[]{:S(2)}) copy-start(bf16[48,6144]{1,0:T(8,128)(2,1)} %w_ref.3) | copy-start | bytes 1769476
  130.4 13.3 %copy-start.5 = (bf16[2,128,1536]{2,1,0:T(8,128)(2,1)S(1)}, bf16[2,128,1536]{2,1,0:T(8,128)(2,1)}, u32[]{:S(2)}) copy-start(bf16[2,128,1536]{2,1,0:T(8,128)(2,1)} %cot_ref.1) | copy-start | bytes 2359300
  130.4 13.3 %copy-start.9 = (bf16[96,1536]{1,0:T(8,128)(2,1)S(1)}, bf16[96,1536]{1,0:T(8,128)(2,1)}, u32[]{:S(2)}) copy-start(bf16[96,1536]{1,0:T(8,128)(2,1)} %o_ref.1) | copy-start | bytes 884740
  142.4 1.2 copy-start.8
  143.7 127.8 %copy-start.7 = (bf16[8,128,768]{2,1,0:T(8,128)(2,1)}, bf16[8,128,768]{2,1,0:T(8,128)(2,1)S(1)}, u32[]{:S(2)}) copy-start(bf16[8,128,768]{2,1,0:T(8,128)(2,1)S(1)} %get-tuple-element.38.mixed) | copy-start | bytes 4718596
  268.8 2.7 copy-start.13
  268.9 2.7 copy-start.34
  268.9 3.5 copy-start.35
  271.5 6.0 %copy-start.25 = (bf16[1024,768]{1,0:T(8,128)(2,1)}, bf16[1024,768]{1,0:T(8,128)(2,1)S(1)}, u32[]{:S(2)}) copy-start(bf16[1024,768]{1,0:T(8,128)(2,1)S(1)} %convolution_convert_fusion.2) | copy-start | bytes 4718596
  281.4 7.2 %copy-start.36 = (bf16[8,96,1536]{2,1,0:T(8,128)(2,1)S(1)}, bf16[8,96,1536]{2,1,0:T(8,128)(2,1)}, u32[]{:S(2)}) copy-start(bf16[8,96,1536]{2,1,0:T(8,128)(2,1)} %get-tuple-element.41) | copy-start | bytes 7077892
  281.4 7.2 %copy-start.37 = (f32[1024,768]{1,0:T(8,128)S(1)}, f32[1024,768]{1,0:T(8,128)}, u32[]{:S(2)}) copy-start(f32[1024,768]{1,0:T(8,128)} %get-tuple-element.104) | copy-start | bytes 9437188
  327.7 32.3 %copy-start.19 = (bf16[8,128,1536]{2,1,0:T(8,128)(2,1)S(1)}, bf16[8,128,1536]{2,1,0:T(8,128)(2,1)}, u32[]{:S(2)}) copy-start(bf16[8,128,1536]{2,1,0:T(8,128)(2,1)} %copy-done.18) | copy-start | bytes 9437188
  361.9 4.0 copy-start.20
  365.8 4.1 copy-start.12
  369.9 2.6 copy-start.14
  372.6 2.7 copy-start.17
  372.6 2.7 copy-start.27
  523.3 1.9 copy-start.2
  523.3 1.9 copy-start.31
  523.4 2.3 copy-start.6
  527.6 5.5 %copy-start.29 = (bf16[48,256]{1,0:T(8,128)(2,1)S(1)}, bf16[48,256]{1,0:T(8,128)(2,1)}, u32[]{:S(2)}) copy-start(bf16[48,256]{1,0:T(8,128)(2,1)} %param.17) | copy-start | bytes 73732
  527.6 5.9 %copy-start.33 = (bf16[96]{0:T(256)(128)(2,1)S(1)}, bf16[96]{0:T(256)(128)(2,1)}, u32[]{:S(2)}) copy-start(bf16[96]{0:T(256)(128)(2,1)} %param.27) | copy-start | bytes 580
  527.6 6.5 %copy-start.22 = (f32[4,6,8,768]{3,2,0,1:T(8,128)S(1)}, f32[4,6,8,768]{3,2,0,1:T(8,128)}, u32[]{:S(2)}) copy-start(f32[4,6,8,768]{3,2,0,1:T(8,128)} %copy.72) | copy-start | bytes 1769476
  531.6 2.6 copy-start.23
  533.2 1.3 copy-start.28
  533.4 1.1 copy-start.24
  533.4 1.1 copy-start.32
  534.2 1.0 copy-start.21

commit v3 on v1

v3 whole, which is shorter than its diff:
```python
import functools

import jax
import jax.numpy as jnp
from jax import lax
from jax.experimental import pallas as pl
from jax.experimental.pallas import tpu as pltpu
from jax.sharding import PartitionSpec as P

P_SIZE = 64
EPS = 1e-05
F32 = jnp.float32
BF16 = jnp.bfloat16
HIGH = lax.Precision.HIGHEST
LANES = 128
VMEM_LIMIT = 58 * 1024 * 1024


def dot(left, right, dims=((1,), (0,)), precision=None):
    return lax.dot_general(
        left, right, (dims, ((), ())), precision=precision, preferred_element_type=F32
    )


def iota(shape, axis):
    return lax.broadcasted_iota(jnp.int32, shape, axis)


def spread(cols, pair, low_half):
    return jnp.where(low_half, cols[:, 2 * pair : 2 * pair + 1], cols[:, 2 * pair + 1 : 2 * pair + 2])


def spread_all(cols, pairs, low_half):
    return jnp.concatenate([spread(cols, pair, low_half) for pair in range(pairs)], axis=1)


def stack_heads(values, low_half):
    zero = jnp.zeros_like(values)
    return jnp.concatenate(
        [jnp.where(low_half, values, zero), jnp.where(low_half, zero, values)], axis=0
    )


def softplus(value):
    return jnp.maximum(value, 0.0) + jnp.log1p(jnp.exp(-jnp.abs(value)))


def conv_pre(ext, rows, taps):
    total = taps[4:5, :]
    for tap in range(4):
        total = total + taps[tap : tap + 1, :] * ext[pl.ds(5 + tap, rows), :]
    return total


def steps_of(dt_raw, head_ref):
    pre = dt_raw.astype(F32) + head_ref[0:1, :]
    steps = softplus(pre)
    return pre, steps, -steps * head_ref[1:2, :]


def scan_backward(
    wide, chans,
    dy_in, x, x_before, bd, bd_before, taps, heads, skip, enter,
    dx_out, dbd, dtaps, dheads, dskip,
    ext, gext, halo, dstate,
):
    step = pl.program_id(0)
    chunk = pl.num_programs(0) - 1 - step
    rows = x.shape[0]
    pairs = chans // LANES
    half = wide // 2
    low_half = iota((rows, LANES), 1) < P_SIZE

    @pl.when(step == 0)
    def _():
        halo[...] = jnp.zeros(halo.shape, F32)
        dstate[...] = jnp.zeros(dstate.shape, F32)
        dtaps[...] = jnp.zeros_like(dtaps)
        dheads[...] = jnp.zeros_like(dheads)
        dskip[...] = jnp.zeros_like(dskip)

    dy_half = dy_in[...]
    dy = dy_half.astype(F32)

    last_rows = x_before.shape[0] - 8
    past = jnp.concatenate(
        [x_before[last_rows:, :], bd_before[last_rows:, :wide]], axis=1
    ).astype(F32)
    ext[0:8, :] = jnp.where(chunk == 0, 0.0, past)
    ext[8 : 8 + rows, :chans] = x[...].astype(F32)
    ext[8 : 8 + rows, chans:] = bd[:, :wide].astype(F32)
    pre = conv_pre(ext, rows, taps)
    sig_pre = jax.nn.sigmoid(pre)
    act = (pre * sig_pre).astype(BF16)
    slope = sig_pre * (1.0 + pre * (1.0 - sig_pre))
    bmat = act[:, chans : chans + half]
    cmat = act[:, chans + half :]
    xmat = act[:, :chans]
    xval = xmat.astype(F32)
    dt_pre, steps, logs = steps_of(bd[:, wide:], heads)
    row, col = iota((rows, rows), 0), iota((rows, rows), 1)
    cumul = dot((row >= col).astype(F32), logs, precision=HIGH)
    cumul_t = cumul.T
    last = cumul[rows - 1 :, :]
    later = row <= col
    scores = dot(bmat, cmat, ((1,), (1,)))
    grown = jnp.exp(cumul)
    shrunk = jnp.exp(last - cumul)
    final = jnp.exp(last)
    entering = enter[...]
    dleave = dstate[...]
    dleave_half = dleave.astype(BF16)
    from_state = dot(bmat, dleave_half)
    across = dot(cmat, entering)
    grown_all = spread_all(grown, pairs, low_half)
    ending_all = spread_all(steps * shrunk, pairs, low_half)
    dy_grown = (dy * grown_all).astype(BF16)
    x_end = (xval * ending_all).astype(BF16)
    dstate[...] = dleave * spread_all(final, pairs, low_half[0:1, :]) + dot(
        cmat, dy_grown, ((0,), (0,))
    )
    owner = (iota((chans, LANES), 0) // P_SIZE == iota((chans, LANES), 1)).astype(F32)
    near = dot(xval * from_state, owner, precision=HIGH) * shrunk
    reach = dot(dy * across, owner, precision=HIGH) * grown
    kept = jnp.sum(entering.astype(F32) * dleave, axis=0, keepdims=True)
    kept = dot(jnp.broadcast_to(kept, (8, chans)), owner, precision=HIGH)[0:1, :] * final
    pairs_sum = jnp.zeros((rows, rows), F32)
    head_lane = iota((rows, LANES), 1)
    col_sum = jnp.zeros((rows, LANES), F32)
    row_sums = []
    for pair in range(pairs):
        lanes = slice(pair * LANES, (pair + 1) * LANES)
        products = dot(stack_heads(xmat[:, lanes], low_half), dy_half[:, lanes], ((1,), (1,)))
        weights = []
        for place, head in enumerate((2 * pair, 2 * pair + 1)):
            product = products[place * rows : (place + 1) * rows, :]
            differ = cumul_t[head : head + 1, :] - cumul[:, head : head + 1]
            decay = jnp.where(later, jnp.exp(jnp.minimum(differ, 0.0)), 0.0)
            weight = decay * scores
            step_col = steps[:, head : head + 1]
            weights.append(weight.astype(BF16))
            pairs_sum = pairs_sum + decay * product * step_col
            terms = weight * product
            col_sum = jnp.where(head_lane == head, jnp.sum(terms, axis=1, keepdims=True), col_sum)
            row_sums.append(jnp.sum(terms * step_col, axis=0, keepdims=True))
        inside = dot(
            jnp.concatenate(weights, axis=1), stack_heads(dy_half[:, lanes], low_half)
        )
        dx = spread(steps, pair, low_half) * (
            inside + spread(shrunk, pair, low_half) * from_state[:, lanes]
        )
        dx = dx + skip[0:1, lanes] * dy[:, lanes]
        gext[0:rows, lanes] = dx * slope[:, lanes]
    pairs_half = pairs_sum.astype(BF16)
    d_b = dot(pairs_half, cmat) + dot(x_end, dleave_half, ((1,), (1,)))
    d_c = dot(pairs_half, bmat, ((0,), (0,))) + dot(dy_grown, entering, ((1,), (1,)))
    gext[0:rows, chans : chans + half] = d_b * slope[:, chans : chans + half]
    gext[0:rows, chans + half :] = d_c * slope[:, chans + half :]

    row_sum = jnp.concatenate(
        row_sums + [jnp.zeros((LANES - 2 * pairs, rows), F32)], axis=0
    ).T
    d_logs = dot((row <= col).astype(F32), row_sum - steps * col_sum + reach, precision=HIGH)
    d_logs = d_logs + dot((row > col).astype(F32), steps * near, precision=HIGH) + kept
    d_steps = col_sum + near - heads[1:2, :] * d_logs
    d_pre = d_steps * jax.nn.sigmoid(dt_pre)
    dbd[:, wide:] = d_pre.astype(BF16)
    dheads[0:1, :] += jnp.sum(d_pre, axis=0, keepdims=True)
    dheads[1:2, :] += jnp.sum(d_logs * logs, axis=0, keepdims=True)
    dskip[0:1, :] += jnp.sum(dy * xval, axis=0, keepdims=True)

    gext[rows : rows + 8, :] = halo[...]
    g = gext[0:rows, :]
    halo[...] = g[0:8, :]
    d_in = jnp.zeros((rows, chans + wide), F32)
    for tap in range(4):
        d_in = d_in + taps[tap : tap + 1, :] * gext[pl.ds(3 - tap, rows), :]
        dtaps[tap : tap + 1, :] += jnp.sum(g * ext[pl.ds(5 + tap, rows), :], axis=0, keepdims=True)
    dtaps[4:5, :] += jnp.sum(g, axis=0, keepdims=True)
    dx_out[...] = d_in[:, :chans].astype(BF16)
    dbd[:, :wide] = d_in[:, chans:].astype(BF16)


MESH = pl.DeviceIdType.MESH
ANY = pl.BlockSpec(memory_space=pl.ANY)


class Place:
    def __init__(self, dp, sp, seqs):
        self.dp, self.sp, self.seqs = dp, sp, seqs
        self.groups = sp // seqs
        self.chips = sp // 2
        self.per = self.groups // 2
        self.p = lax.axis_index("dp")
        self.s = lax.axis_index("sp")
        self.chip = self.s // 2
        self.core = lax.rem(self.s, 2)
        self.seq = self.s // self.groups
        self.group = lax.rem(self.s, self.groups)
        self.low = self.seq * self.per
        self.high = self.low + self.per - 1
        self.bits = [1 << i for i in range(dp.bit_length() - 1)]

    def along_sp(self, other):
        return (self.p, other)

    def along_dp(self, other):
        return (other, self.s)

    def flip(self, bit):
        return self.p + bit - 2 * bit * lax.rem(self.p // bit, 2)

    def masked(self, mask):
        other = self.p
        for bit in self.bits:
            if mask & bit:
                other = other + bit - 2 * bit * lax.rem(self.p // bit, 2)
        return other

    def sp_peer(self, step):
        return lax.rem(self.s + step, self.sp)

    def meet(self, sp_peers=True, dp_peers=True, group_peers=False, more=0):
        barrier = pltpu.get_barrier_semaphore()
        peers = []
        if sp_peers:
            peers += [self.along_sp(self.sp_peer(i)) for i in range(1, self.sp)]
        if group_peers:
            peers += [self.along_sp(self.group_peer(i)) for i in range(1, self.groups)]
        if dp_peers:
            peers += [self.along_dp(self.masked(m)) for m in range(1, self.dp)]
        for peer in peers:
            pl.semaphore_signal(barrier, inc=1, device_id=peer, device_id_type=MESH)
        pl.semaphore_wait(barrier, len(peers) + more)

    def group_peer(self, step):
        return self.seq * self.groups + lax.rem(self.group + step, self.groups)


def remote(src, dst, send, recv, device):
    return pltpu.make_async_remote_copy(
        src_ref=src, dst_ref=dst, send_sem=send, recv_sem=recv, device_id=device,
        device_id_type=MESH,
    )


def dma(*shape):
    return pltpu.SemaphoreType.DMA(shape)


class DpTree:
    @staticmethod
    def scratch(dp):
        return [dma(2, dp), dma(2, dp, dp.bit_length() - 1)]

    def __init__(self, place, part, recv, send):
        self.at, self.part, self.recv, self.send = place, part, recv, send

    def children(self, odd, mask):
        at = self.at
        order = at.bits if odd == 0 else at.bits[::-1]
        last = max([order.index(b) for b in order if mask & b], default=-1)
        src = self.part(at.masked(mask), odd)
        return [
            remote(
                src, src, self.send.at[odd, mask, at.bits.index(bit)],
                self.recv.at[odd, mask ^ bit], at.along_dp(at.flip(bit)),
            )
            for bit in order[last + 1 :]
        ]

    def start(self, odd):
        for copy in self.children(odd, 0):
            copy.start()

    def forward(self, odd):
        at = self.at
        for mask in sorted(range(1, at.dp), key=lambda m: (bin(m).count("1"), m)):
            dst = self.part(at.masked(mask), odd)
            remote(dst, dst, self.send.at[odd, 0, 0], self.recv.at[odd, mask], at.along_dp(at.p)).wait_recv()
            for copy in self.children(odd, mask):
                copy.start()

    def finish(self):
        for odd in range(2):
            for mask in range(self.at.dp):
                for copy in self.children(odd, mask):
                    copy.wait_send()


class Owners:
    def __init__(self, place):
        self.at, self.each = place, place.sp // place.dp

    def holder(self, seq):
        at = self.at
        p, s = at.s // self.each, seq * at.groups + at.p
        return (p, s), (p == at.p) & (s == at.s)

    def owner(self, i):
        at = self.at
        p, s = at.group, at.p * self.each + i
        return (p, s), (p == at.p) & (s == at.s)

    def meet(self, spread):
        barrier = pltpu.get_barrier_semaphore()
        holders = [self.holder(seq) for seq in range(self.at.seqs)]
        owners = [self.owner(i) for i in range(self.each)]
        greet, wait = (owners, holders) if spread else (holders, owners)
        for device, mine in greet:

            @pl.when(jnp.logical_not(mine))
            def _():
                pl.semaphore_signal(barrier, inc=1, device_id=device, device_id_type=MESH)

        count = jnp.int32(0)
        for _, mine in wait:
            count = count + jnp.where(mine, 0, 1)
        return count


class OutGather:
    @staticmethod
    def scratch(dp, sp, seqs):
        return [dma(seqs), dma(sp), dma(1)] + DpTree.scratch(dp)

    def __init__(self, place, x, out, sent, got, local, *tree):
        self.at, self.x, self.out = place, x, out
        self.sent, self.got, self.local = sent, got, local.at[0]
        self.ways = Owners(place)
        each = self.ways.each
        size = each // 2
        part = lambda p, odd: out.at[pl.ds(p * each + odd * size, size)]
        self.tree = DpTree(place, part, *tree)

    def shard_copy(self, seq):
        at = self.at
        device, mine = self.ways.holder(seq)
        return jnp.logical_not(mine), remote(
            self.x, self.out.at[at.s], self.sent.at[seq], self.got.at[at.s], device
        )

    def keep(self):
        return pltpu.make_async_copy(self.x, self.out.at[self.at.s], self.local)

    def start(self):
        for seq in range(self.at.seqs):
            needed, copy = self.shard_copy(seq)
            pl.when(needed)(copy.start)
        for i in range(self.ways.each):
            pl.when(self.ways.owner(i)[1])(lambda: self.keep().start())

    def along_dp(self, odd):
        at, each = self.at, self.ways.each
        for i in range(odd * each // 2, (odd + 1) * each // 2):
            _, mine = self.ways.owner(i)
            slot = at.p * each + i
            pl.when(mine)(lambda: self.keep().wait())

            @pl.when(jnp.logical_not(mine))
            def _():
                dst = self.out.at[slot]
                remote(dst, dst, self.sent.at[0], self.got.at[slot], at.along_sp(at.s)).wait_recv()

        self.tree.start(odd)

    def forward(self, odd):
        self.tree.forward(odd)

    def finish(self):
        for seq in range(self.at.seqs):
            needed, copy = self.shard_copy(seq)
            pl.when(needed)(copy.wait_send)
        self.tree.finish()


class BlockReduce:
    @staticmethod
    def scratch(dp, sp, seqs, rows, cols, own):
        chips, sides = sp // 2, (2 if sp // seqs > 4 else 1)
        block = lambda *n: pltpu.VMEM(n + (rows, cols), BF16)
        return ([block(chips)] if own else []) + [
            block(chips), block(sides, chips), block(seqs), dma(7, chips), dma(2, seqs),
        ]

    def __init__(self, place, part, acc, cross, chain, total, sems, ends):
        self.at, self.part, self.acc = place, part, acc
        self.cross, self.chain, self.total = cross, chain, total
        (self.local, self.cross_send, self.cross_recv, self.chain_send, self.low_recv,
         self.high_recv, self.far_send) = (sems.at[i] for i in range(7))
        self.end_send, self.end_recv = ends.at[0], ends.at[1]

    def mine(self, k):
        return self.part.at[k * 2 + self.at.core] if self.acc is None else self.acc.at[k]

    def keep(self, k):
        return pltpu.make_async_copy(
            self.part.at[k * 2 + self.at.core], self.acc.at[k], self.local.at[k]
        )

    def crossing(self, k):
        at = self.at
        return remote(
            self.part.at[k * 2 + 1 - at.core], self.cross.at[k], self.cross_send.at[k],
            self.cross_recv.at[k], at.along_sp(at.chip * 2 + 1 - at.core),
        )

    def onward(self, k, up):
        at = self.at
        side = 0 if up else self.chain.shape[0] - 1
        return remote(
            self.mine(k), self.chain.at[side, k], self.chain_send.at[k],
            (self.low_recv if up else self.high_recv).at[k],
            at.along_sp((at.chip + (1 if up else -1)) * 2 + at.core),
        )

    def ending(self, k):
        at = self.at
        return remote(
            self.mine(k), self.total.at[at.seq], self.far_send.at[k], self.end_recv.at[at.seq],
            at.along_sp(k * 2 + at.core),
        )

    def exit_of(self, k):
        return jnp.clip(k, self.at.low, self.at.high)

    def add(self, k, other):
        mine = self.mine(k)
        mine[...] = (mine[...].astype(F32) + other[...].astype(F32)).astype(BF16)

    def start(self, k):
        self.crossing(k).start()
        if self.acc is not None:
            self.keep(k).start()

    def upstream(self, k, out):
        at = self.at

        @pl.when((at.chip <= out) & (at.chip > at.low))
        def _():
            self.onward(k, True).wait_recv()
            self.add(k, self.chain.at[0, k])

        @pl.when((at.chip >= out) & (at.chip < at.high))
        def _():
            self.onward(k, False).wait_recv()
            self.add(k, self.chain.at[self.chain.shape[0] - 1, k])

    def collect(self, k):
        at, out = self.at, self.exit_of(k)
        self.crossing(k).wait_recv()
        if self.acc is not None:
            self.keep(k).wait()
        self.add(k, self.cross.at[k])

        @pl.when(at.chip != out)
        def _():
            self.upstream(k, out)
            pl.when(at.chip < out)(lambda: self.onward(k, True).start())
            pl.when(at.chip > out)(lambda: self.onward(k, False).start())

    def settle(self, k):
        at, out = self.at, self.exit_of(k)

        @pl.when(at.chip == out)
        def _():
            self.upstream(k, out)

            @pl.when(k == at.chip)
            def _():
                self.total[at.seq] = self.mine(k)[...]

            @pl.when(k != at.chip)
            def _():
                self.ending(k).start()

    def finish(self):
        at = self.at
        for target in range(at.seqs):

            @pl.when(target != at.seq)
            def _():
                dst = self.total.at[target]
                remote(dst, dst, self.end_send.at[0], self.end_recv.at[target], at.along_sp(at.s)).wait_recv()

        for k in range(at.chips):
            out = self.exit_of(k)
            self.crossing(k).wait_send()
            pl.when(at.chip < out)(lambda: self.onward(k, True).wait_send())
            pl.when(at.chip > out)(lambda: self.onward(k, False).wait_send())
            pl.when((at.chip == out) & (at.chip != k))(lambda: self.ending(k).wait_send())


class ShardReduce:
    @staticmethod
    def scratch(dp, sp, shape):
        return [
            pltpu.VMEM((dp, sp) + shape, BF16),
            dma(2, dp), dma(2, sp), dma(1),
        ]

    def __init__(self, place, terms, out, buf, along_dp, along_sp, local):
        self.at, self.terms, self.out, self.buf = place, terms, out, buf
        self.dp_sems, self.sp_sems, self.local = along_dp, along_sp, local.at[0]

    def dp_copy(self, mask):
        at = self.at
        return remote(
            self.terms.at[at.masked(mask)], self.buf.at[mask], self.dp_sems.at[0, mask],
            self.dp_sems.at[1, mask], at.along_dp(at.masked(mask)),
        )

    def keep(self):
        return pltpu.make_async_copy(self.terms.at[self.at.p], self.buf.at[0], self.local)

    def sp_copy(self, i):
        at = self.at
        target = at.sp_peer(i)
        return remote(
            self.buf.at[0, target], self.out.at[at.s], self.sp_sems.at[0, i], self.sp_sems.at[1, i],
            at.along_sp(target),
        )

    def back(self):
        at = self.at
        return pltpu.make_async_copy(self.buf.at[0, at.s], self.out.at[at.s], self.local)

    def start(self):
        for mask in range(1, self.at.dp):
            self.dp_copy(mask).start()
        self.keep().start()

    def add(self, kept=True):
        at = self.at
        if kept:
            self.keep().wait()
        for mask in range(1, at.dp):
            self.dp_copy(mask).wait_recv()
        for i in list(range(1, at.sp)) + [0]:
            slot = at.sp_peer(i)
            total = self.buf[0, slot].astype(F32)
            for mask in range(1, at.dp):
                total = total + self.buf[mask, slot].astype(F32)
            self.buf[0, slot] = total.astype(BF16)
            if i:
                self.sp_copy(i).start()
            else:
                self.back().start()

    def finish(self):
        at = self.at
        for mask in range(1, at.dp):
            self.dp_copy(mask).wait_send()
        for i in range(1, at.sp):
            dst = self.out.at[lax.rem(at.s + at.sp - i, at.sp)]
            remote(dst, dst, self.sp_sems.at[0, i], self.sp_sems.at[1, i], at.along_sp(at.s)).wait_recv()
            self.sp_copy(i).wait_send()
        self.back().wait()


class OutReduce:
    @staticmethod
    def scratch(dp, sp, seqs, shape):
        each = sp // dp
        return [pltpu.VMEM((dp, each) + shape, BF16), dma(2, dp), dma(each), dma(seqs), dma(2)]

    def __init__(self, place, terms, out, buf, dp_sems, sent, got, local):
        self.at, self.terms, self.out, self.buf = place, terms, out, buf
        self.dp_sems, self.sent, self.got, self.local = dp_sems, sent, got, local
        self.ways = Owners(place)

    def shards(self, p):
        return self.terms.at[pl.ds(p * self.ways.each, self.ways.each)]

    def dp_copy(self, mask):
        at = self.at
        return remote(
            self.shards(at.masked(mask)), self.buf.at[mask], self.dp_sems.at[0, mask],
            self.dp_sems.at[1, mask], at.along_dp(at.masked(mask)),
        )

    def keep(self):
        return pltpu.make_async_copy(self.shards(self.at.p), self.buf.at[0], self.local.at[0])

    def start(self):
        for mask in range(1, self.at.dp):
            self.dp_copy(mask).start()
        self.keep().start()

    def shard_copy(self, i):
        at = self.at
        device, mine = self.ways.owner(i)
        return mine, remote(
            self.buf.at[0, i], self.out.at[at.seq], self.sent.at[i], self.got.at[at.seq], device
        )

    def back(self, i):
        return pltpu.make_async_copy(self.buf.at[0, i], self.out.at[self.at.seq], self.local.at[1])

    def add(self):
        at = self.at
        self.keep().wait()
        for mask in range(1, at.dp):
            self.dp_copy(mask).wait_recv()
        for i in range(self.ways.each):
            total = self.buf[0, i].astype(F32)
            for mask in range(1, at.dp):
                total = total + self.buf[mask, i].astype(F32)
            self.buf[0, i] = total.astype(BF16)
            mine, copy = self.shard_copy(i)
            pl.when(jnp.logical_not(mine))(copy.start)
            pl.when(mine)(lambda: self.back(i).start())

    def finish(self):
        at = self.at
        for mask in range(1, at.dp):
            self.dp_copy(mask).wait_send()
        for i in range(self.ways.each):
            mine, copy = self.shard_copy(i)
            pl.when(jnp.logical_not(mine))(copy.wait_send)
            pl.when(mine)(lambda: self.back(i).wait())
        for seq in range(at.seqs):
            _, mine = self.ways.holder(seq)

            @pl.when(jnp.logical_not(mine))
            def _():
                dst = self.out.at[seq]
                remote(dst, dst, self.sent.at[0], self.got.at[seq], at.along_sp(at.s)).wait_recv()


class SmallReduce:
    @staticmethod
    def scratch(dp, sp, seqs, shape):
        return [pltpu.VMEM((dp,) + shape, F32), dma(2, dp), dma(2, sp)]

    def __init__(self, place, x, out, buf, dp_sems, sp_sems):
        self.at, self.x, self.out, self.buf = place, x, out, buf
        self.dp_sems, self.sp_sems = dp_sems, sp_sems

    def dp_copy(self, mask):
        at = self.at
        return remote(
            self.x, self.buf.at[mask], self.dp_sems.at[0, mask], self.dp_sems.at[1, mask],
            at.along_dp(at.masked(mask)),
        )

    def sp_copy(self, i):
        at = self.at
        return remote(
            self.buf.at[0], self.out.at[at.s], self.sp_sems.at[0, i], self.sp_sems.at[1, i],
            at.along_sp(at.sp_peer(i)),
        )

    def start(self):
        for mask in range(1, self.at.dp):
            self.dp_copy(mask).start()

    def add(self):
        at = self.at
        total = self.x[...]
        for mask in range(1, at.dp):
            self.dp_copy(mask).wait_recv()
            total = total + self.buf[mask]
        self.buf[0] = total
        self.out[at.s] = total
        for i in range(1, at.sp):
            self.sp_copy(i).start()

    def finish(self):
        at = self.at
        for mask in range(1, at.dp):
            self.dp_copy(mask).wait_send()
        for i in range(1, at.sp):
            dst = self.out.at[lax.rem(at.s + at.sp - i, at.sp)]
            remote(dst, dst, self.sp_sems.at[0, i], self.sp_sems.at[1, i], at.along_sp(at.s)).wait_recv()
            self.sp_copy(i).wait_send()


def comm_params(number):
    return pltpu.CompilerParams(
        collective_id=number, has_side_effects=True, vmem_limit_bytes=VMEM_LIMIT
    )


class BlockGather:
    @staticmethod
    def scratch(dp, sp, seqs):
        return [dma(5, sp // 2)]

    def __init__(self, place, x, out, sems):
        self.at, self.x, self.out = place, x, out
        self.send, self.recv, self.cross_send, self.cross_recv, self.local = (
            sems.at[i] for i in range(5)
        )

    def chip_at(self, i):
        return lax.rem(self.at.chip + i, self.at.chips)

    def chip_copy(self, i):
        at = self.at
        chip = self.chip_at(i)
        return remote(
            self.x.at[chip // at.per], self.out.at[at.s], self.send.at[i], self.recv.at[at.chip],
            at.along_sp(chip * 2 + at.core),
        )

    def keep(self):
        return pltpu.make_async_copy(self.x.at[self.at.seq], self.out.at[self.at.s], self.local.at[0])

    def crossing(self, k, src):
        at = self.at
        return remote(
            src, self.out.at[k * 2 + at.core], self.cross_send.at[k], self.cross_recv.at[k],
            at.along_sp(at.chip * 2 + 1 - at.core),
        )

    def start(self):
        for i in range(1, self.at.chips):
            self.chip_copy(i).start()
        self.crossing(self.at.chip, self.x.at[self.at.seq]).start()
        self.keep().start()

    def arrive(self, i):
        at = self.at
        k = self.chip_at(i)
        dst = self.out.at[k * 2 + at.core]

        @pl.when(i == 0)
        def _():
            self.keep().wait()

        @pl.when(i != 0)
        def _():
            remote(dst, dst, self.send.at[0], self.recv.at[k], at.along_sp(at.s)).wait_recv()
            self.crossing(k, dst).start()

        return k * 2 + at.core

    def arrive_other(self, i):
        at = self.at
        k = self.chip_at(i)
        dst = self.out.at[k * 2 + 1 - at.core]
        remote(dst, dst, self.cross_send.at[0], self.cross_recv.at[k], at.along_sp(at.s)).wait_recv()
        return k * 2 + 1 - at.core

    def finish(self):
        for i in range(1, self.at.chips):
            self.chip_copy(i).wait_send()
        for k in range(self.at.chips):
            self.crossing(k, self.out.at[k * 2 + self.at.core]).wait_send()


class ColumnGather:
    @staticmethod
    def scratch(dp, sp, seqs):
        return [dma(2, sp), dma(1)] + DpTree.scratch(dp)

    def __init__(self, place, piece, out, along, local, *tree):
        self.at, self.piece, self.out = place, piece, out
        self.along, self.local = along, local.at[0]
        size = place.sp // 2
        self.tree = DpTree(place, lambda p, odd: out.at[p, pl.ds(odd * size, size)], *tree)

    def sp_copy(self, i):
        at = self.at
        target = at.sp_peer(i)
        return remote(
            self.piece(lax.rem(target, at.groups)), self.out.at[at.p, at.s],
            self.along.at[0, i], self.along.at[1, at.s], at.along_sp(target),
        )

    def keep(self):
        at = self.at
        return pltpu.make_async_copy(self.piece(at.group), self.out.at[at.p, at.s], self.local)

    def start(self):
        for i in range(1, self.at.sp):
            self.sp_copy(i).start()
        self.keep().start()

    def along_dp(self, odd):
        at = self.at
        size = at.sp // 2
        for slot in range(odd * size, (odd + 1) * size):

            @pl.when(at.s == slot)
            def _():
                self.keep().wait()

            @pl.when(at.s != slot)
            def _():
                dst = self.out.at[at.p, slot]
                remote(dst, dst, self.along.at[0, 0], self.along.at[1, slot], at.along_sp(at.s)).wait_recv()

        self.tree.start(odd)

    def forward(self, odd):
        self.tree.forward(odd)

    def finish(self):
        for i in range(1, self.at.sp):
            self.sp_copy(i).wait_send()
        self.tree.finish()


class CommonGather:
    @staticmethod
    def scratch(dp, sp, seqs):
        return [dma(2, sp // 2), dma(2, dp), dma(3)]

    def __init__(self, place, x, out, along, across, ends):
        self.at, self.x, self.out = place, x, out
        self.along, self.across, self.ends = along, across, ends

    def chip_copy(self, i):
        at = self.at
        chip = lax.rem(at.chip + i, at.chips)
        return remote(
            self.x, self.out.at[at.core, at.p, at.chip], self.along.at[0, i],
            self.along.at[1, at.chip], at.along_sp(chip * 2 + at.core),
        )

    def keep(self):
        at = self.at
        return pltpu.make_async_copy(self.x, self.out.at[at.core, at.p, at.chip], self.ends.at[0])

    def dp_copy(self, mask):
        at = self.at
        src = self.out.at[at.core, at.p]
        return remote(
            src, src, self.across.at[0, mask], self.across.at[1, mask], at.along_dp(at.masked(mask))
        )

    def crossing(self):
        at = self.at
        src = self.out.at[at.core]
        return remote(
            src, src, self.ends.at[1], self.ends.at[2], at.along_sp(at.chip * 2 + 1 - at.core)
        )

    def start(self):
        for i in range(1, self.at.chips):
            self.chip_copy(i).start()
        self.keep().start()

    def along_dp(self):
        at = self.at
        self.keep().wait()
        for i in range(1, at.chips):
            k = lax.rem(at.chip + i, at.chips)
            dst = self.out.at[at.core, at.p, k]
            remote(dst, dst, self.along.at[0, 0], self.along.at[1, k], at.along_sp(at.s)).wait_recv()
        for mask in range(1, at.dp):
            self.dp_copy(mask).start()

    def cross(self):
        at = self.at
        for mask in range(1, at.dp):
            dst = self.out.at[at.core, at.masked(mask)]
            remote(dst, dst, self.across.at[0, 0], self.across.at[1, mask], at.along_dp(at.p)).wait_recv()
        self.crossing().start()

    def finish(self):
        at = self.at
        dst = self.out.at[1 - at.core]
        remote(dst, dst, self.ends.at[1], self.ends.at[2], at.along_sp(at.s)).wait_recv()
        self.crossing().wait_send()
        for mask in range(1, at.dp):
            self.dp_copy(mask).wait_send()
        for i in range(1, at.chips):
            self.chip_copy(i).wait_send()


def first_kernel(dp, sp, seqs, chans, w_ref, misc_ref, hid_ref, wx_out, misc_out, hid_out, *sems):
    place = Place(dp, sp, seqs)
    inner = w_ref.shape[1] // 2
    columns = lambda g: w_ref.at[:, pl.ds(pl.multiple_of(inner + g * chans, LANES), chans)]
    wx = ColumnGather(place, columns, wx_out, *sems[:4])
    misc = CommonGather(place, misc_ref, misc_out, *sems[4:7])
    hid = BlockGather(place, hid_ref, hid_out, *sems[7:])
    place.meet()
    misc.start()
    wx.start()
    hid.start()
    misc.along_dp()
    wx.along_dp(0)
    wx.along_dp(1)
    misc.cross()
    hid.arrive(0)
    hid.arrive(1)
    wx.forward(0)
    wx.forward(1)
    for i in range(2, place.chips):
        hid.arrive(i)
    for i in range(place.chips):
        hid.arrive_other(i)
    misc.finish()
    wx.finish()
    hid.finish()


def run_first(dp, sp, seqs, chans, w_zx, misc, hidden):
    share = w_zx.shape[0]
    _, rows, cols = hidden.shape
    return pl.pallas_call(
        functools.partial(first_kernel, dp, sp, seqs, chans),
        in_specs=[ANY] * 3,
        out_specs=[ANY] * 3,
        out_shape=[
            jax.ShapeDtypeStruct((dp, sp, share, chans), BF16),
            jax.ShapeDtypeStruct((2, dp, sp // 2) + misc.shape, BF16),
            jax.ShapeDtypeStruct((sp, rows, cols), BF16),
        ],
        scratch_shapes=ColumnGather.scratch(dp, sp, seqs)
        + CommonGather.scratch(dp, sp, seqs)
        + BlockGather.scratch(dp, sp, seqs),
        compiler_params=comm_params(1),
        name="first_gather",
    )(w_zx, misc, hidden)


def scan_block(wide, chans, x, bd, taps, heads, skip, mixed, enter, ext, halo, state):
    rows = x.shape[0]
    pairs = chans // LANES
    low_half = iota((rows, LANES), 1) < P_SIZE
    ext[0:8, :] = halo[...]
    ext[8 : 8 + rows, :chans] = x.astype(F32)
    ext[8 : 8 + rows, chans:] = bd[:, :wide].astype(F32)
    halo[...] = ext[rows : rows + 8, :]
    pre = conv_pre(ext, rows, taps)
    act = (pre * jax.nn.sigmoid(pre)).astype(BF16)
    half = wide // 2
    bmat = act[:, chans : chans + half]
    cmat = act[:, chans + half :]
    _, steps, logs = steps_of(bd[:, wide:], heads)
    earlier = iota((rows, rows), 0) >= iota((rows, rows), 1)
    cumul = dot(earlier.astype(F32), logs, precision=HIGH)
    cumul_t = cumul.T
    last = cumul[rows - 1 :, :]
    scores = dot(cmat, bmat, ((1,), (1,)))
    grown = jnp.exp(cumul)
    to_end = steps * jnp.exp(last - cumul)
    final = jnp.exp(last)
    entering = state[...]
    entering_half = entering.astype(BF16)
    enter[...] = entering_half
    across = dot(cmat, entering_half)
    for pair in range(pairs):
        lanes = slice(pair * LANES, (pair + 1) * LANES)
        weights = []
        for head in (2 * pair, 2 * pair + 1):
            differ = cumul[:, head : head + 1] - cumul_t[head : head + 1, :]
            decay = jnp.where(earlier, jnp.exp(jnp.minimum(differ, 0.0)), 0.0)
            weights.append((decay * scores).astype(BF16))
        values = act[:, lanes].astype(F32)
        scaled = (values * spread(steps, pair, low_half)).astype(BF16)
        total = dot(jnp.concatenate(weights, axis=1), stack_heads(scaled, low_half))
        total = total + spread(grown, pair, low_half) * across[:, lanes]
        total = total + skip[0:1, lanes] * values
        mixed[:, lanes] = total.astype(BF16)
        ending = (values * spread(to_end, pair, low_half)).astype(BF16)
        state[:, lanes] = entering[:, lanes] * spread(final, pair, low_half[0:1, :]) + dot(
            bmat, ending, ((0,), (0,))
        )


def forward_kernel(
    dp, sp, seqs, wide, inner,
    w_ref, o_ref, cot_ref, hid_ref, wx_ref, wb_ref, norm, taps, heads, skip, gain,
    wg_out, o_out, cot_out, normed_out, x_out, bd_out, enter_out, gated_out, dgate_out, dy_out,
    hid, wx, wb, wg, rows_out, cot, normed, x, bd, mixed, enter, gate, d_gated, gated, dgate, dy,
    ext, halo, state, sums, got, saves, sum_sems, *sems,
):
    place = Place(dp, sp, seqs)
    chans = wx.shape[1]
    blocks, rows, width = hid.shape
    columns = lambda g: w_ref.at[:, pl.ds(pl.multiple_of(g * chans, LANES), chans)]
    wg_comm = ColumnGather(place, columns, wg, *sems[:4])
    out_comm = OutGather(place, o_ref, rows_out, *sems[4:9])
    cot_comm = BlockGather(place, cot_ref, cot, *sems[9:])
    loads = [
        pltpu.make_async_copy(src, dst, saves.at[7, i])
        for i, (src, dst) in enumerate(((hid_ref, hid), (wx_ref, wx), (wb_ref, wb)))
    ]
    for load in loads:
        load.start()
    place.meet(more=out_comm.ways.meet(True))
    out_comm.start()
    wg_comm.start()
    cot_comm.start()
    halo[...] = jnp.zeros(halo.shape, F32)
    state[...] = jnp.zeros(state.shape, F32)
    sums[...] = jnp.zeros(sums.shape, F32)
    for load in loads:
        load.wait()

    def save(src, dst, index, b):
        return pltpu.make_async_copy(src.at[b], dst.at[b], saves.at[index, b])

    early = ((normed, normed_out), (x, x_out), (bd, bd_out), (enter, enter_out))
    late = ((gated, gated_out), (dgate, dgate_out), (dy, dy_out))

    def first(b, carry):
        @pl.when(b == blocks // 2 - 1)
        def _():
            for odd in range(2):
                out_comm.along_dp(odd)

        @pl.when(b == blocks // 2)
        def _():
            for odd in range(2):
                wg_comm.along_dp(odd)

        @pl.when(b == blocks - 1)
        def _():
            for odd in range(2):
                out_comm.forward(odd)

        hidden = hid[b].astype(F32)
        scale = lax.rsqrt(jnp.mean(hidden * hidden, axis=-1, keepdims=True) + EPS)
        normed[b] = (hidden * scale * norm[0:1, :]).astype(BF16)
        x[b] = dot(normed[b], wx[...]).astype(BF16)
        bd[b] = dot(normed[b], wb[...]).astype(BF16)
        scan_block(
            wide, chans, x[b], bd[b], taps, heads, skip, mixed.at[b], enter.at[b], ext, halo, state
        )
        for index, (src, dst) in enumerate(early):
            save(src, dst, index, b).start()
        return carry

    lax.fori_loop(0, blocks, first, 0)
    wg_comm.forward(0)
    wg_comm.forward(1)
    lane = iota((rows, LANES), 1)

    def gates(b):
        gate[b] = dot(normed[b], wg[...].reshape(width, chans)).astype(BF16)

    def second(b):
        d_gated[b] = dot(cot[b], rows_out[...].reshape(chans, width), ((1,), (1,)))
        gate_f = gate[b].astype(F32)
        value = mixed[b].astype(F32) * gate_f * jax.nn.sigmoid(gate_f)
        square = jnp.sum(value * value, axis=1, keepdims=True)
        cross = jnp.sum(value * d_gated[b] * gain[0:1, :], axis=1, keepdims=True)
        sums[...] = sums[...] + jnp.where(lane == 2 * b, square, 0.0) + jnp.where(
            lane == 2 * b + 1, cross, 0.0
        )

    def gates_loop(b, carry):
        gates(b)
        return carry

    lax.fori_loop(0, blocks, gates_loop, 0)

    def own_core(i, carry):
        second(cot_comm.arrive(i))
        return carry

    def other_core(i, carry):
        second(cot_comm.arrive_other(i))
        return carry

    lax.fori_loop(0, place.chips, own_core, 0)
    lax.fori_loop(0, place.chips, other_core, 0)

    copies = [
        remote(sums, got.at[i], sum_sems.at[0, i], sum_sems.at[1, i], place.along_sp(place.group_peer(i)))
        for i in range(1, place.groups)
    ]
    for copy in copies:
        copy.start()
    keep_cot = pltpu.make_async_copy(cot, cot_out, saves.at[7, 0])
    keep_wg = pltpu.make_async_copy(wg, wg_out, saves.at[7, 1])
    keep_out = pltpu.make_async_copy(rows_out, o_out, saves.at[7, 2])
    for keep in (keep_cot, keep_wg, keep_out):
        keep.start()
    total = sums[...]
    for i, copy in enumerate(copies):
        copy.wait_recv()
        total = total + got[i + 1]
    got[0] = total

    def third(b, carry):
        total = got[0]
        square = jnp.sum(jnp.where(lane == 2 * b, total, 0.0), axis=1, keepdims=True)
        cross = jnp.sum(jnp.where(lane == 2 * b + 1, total, 0.0), axis=1, keepdims=True)
        scale = lax.rsqrt(square * (1.0 / inner) + EPS)
        mean = cross * scale * (1.0 / inner)
        gate_f = gate[b].astype(F32)
        sig = jax.nn.sigmoid(gate_f)
        silu = gate_f * sig
        mix = mixed[b].astype(F32)
        unit = mix * silu * scale
        gated[b] = (unit * gain[0:1, :]).astype(BF16)
        back = scale * (d_gated[b] * gain[0:1, :] - unit * mean)
        dy[b] = (back * silu).astype(BF16)
        dgate[b] = (back * mix * sig * (1.0 + gate_f * (1.0 - sig))).astype(BF16)
        for index, (src, dst) in enumerate(late):
            save(src, dst, 4 + index, b).start()
        return carry

    lax.fori_loop(0, blocks, third, 0)
    for copy in copies:
        copy.wait_send()
    cot_comm.finish()
    out_comm.finish()
    wg_comm.finish()
    for keep in (keep_cot, keep_wg, keep_out):
        keep.wait()
    for index, (src, dst) in enumerate(early + late):
        for b in range(blocks):
            save(src, dst, index, b).wait()


def run_middle(dp, sp, seqs, wide, inner, w_zx, w_out, cotangent, hidden, wx, wb, norm, taps, heads, skip, gain):
    share = w_zx.shape[0]
    blocks, rows, width = hidden.shape
    chans, cols = wx.shape[1], wb.shape[1]
    states = wide // 2
    shapes = [
        (dp, sp, share, chans), (sp,) + w_out.shape, hidden.shape, hidden.shape,
        (blocks, rows, chans), (blocks, rows, cols), (blocks, states, chans),
        (blocks, rows, chans), (blocks, rows, chans), (blocks, rows, chans),
    ]
    block = lambda n, kind: pltpu.VMEM((blocks, rows, n), kind)
    vmem = pl.BlockSpec(memory_space=pltpu.VMEM)
    return pl.pallas_call(
        functools.partial(forward_kernel, dp, sp, seqs, wide, inner),
        in_specs=[ANY] * 6 + [vmem] * 5,
        out_specs=[ANY] * len(shapes),
        out_shape=[jax.ShapeDtypeStruct(shape, BF16) for shape in shapes],
        scratch_shapes=[
            pltpu.VMEM(hidden.shape, BF16),
            pltpu.VMEM(wx.shape, BF16),
            pltpu.VMEM(wb.shape, BF16),
            pltpu.VMEM(shapes[0], BF16),
            pltpu.VMEM(shapes[1], BF16),
            pltpu.VMEM(shapes[2], BF16),
            block(width, BF16), block(chans, BF16), block(cols, BF16), block(chans, BF16),
            pltpu.VMEM(shapes[6], BF16),
            block(chans, BF16), block(chans, F32), block(chans, BF16), block(chans, BF16),
            block(chans, BF16),
            pltpu.VMEM((rows + 8, chans + wide), F32),
            pltpu.VMEM((8, chans + wide), F32),
            pltpu.VMEM((states, chans), F32),
            pltpu.VMEM((rows, LANES), F32),
            pltpu.VMEM((sp // seqs, rows, LANES), F32),
            dma(8, max(blocks, 3)),
            dma(2, sp // seqs),
        ]
        + ColumnGather.scratch(dp, sp, seqs)
        + OutGather.scratch(dp, sp, seqs)
        + BlockGather.scratch(dp, sp, seqs),
        compiler_params=comm_params(2),
        name="forward",
    )(w_zx, w_out, cotangent, hidden, wx, wb, norm, taps, heads, skip, gain)


def backward_kernel(
    dp, sp, seqs, wide, chans,
    dy, x, x_before, bd, bd_before, dgate, enter, taps, heads, skip, wg, wx, wb,
    normed_ref, out_part, terms_out, terms_gate,
    out_total, dn_total, og, ox, ob, oo, osmall,
    ext, gext, halo, dstate, dtaps, dheads, dskip, dx, dbd, normed, part, loads,
    tx, tb, small, landed, *scratch,
):
    step, steps = pl.program_id(0), pl.num_programs(0)
    chunk = steps - 1 - step
    place = Place(dp, sp, seqs)
    chips = place.chips
    blocks, rows, width = part.shape
    rest = list(scratch)

    def take(n):
        taken = rest[:n]
        del rest[:n]
        return taken

    out_red = BlockReduce(place, out_part, *take(6))
    dn_red = BlockReduce(place, part, None, *take(5))
    gate_red = ShardReduce(place, terms_gate, og, *take(4))
    x_red = ShardReduce(place, tx, ox, *take(4))
    b_red = ShardReduce(place, tb, ob, *take(4))
    out_grads = OutReduce(place, terms_out, oo, *take(5))
    few = SmallReduce(place, small, landed, *take(3))
    load = pltpu.make_async_copy(normed_ref, normed, loads.at[0])

    @pl.when(step == 0)
    def _():
        place.meet(more=out_grads.ways.meet(False))
        for k in range(chips):
            out_red.start(k)
        gate_red.start()
        out_grads.start()
        load.start()

    scan_backward(
        wide, chans, dy, x, x_before, bd, bd_before, taps, heads, skip, enter,
        dx.at[chunk], dbd.at[chunk], dtaps, dheads, dskip, ext, gext, halo, dstate,
    )
    across = ((1,), (1,))
    total = dot(dgate[...], wg[...], across) + dot(dx[chunk], wx[...], across)
    part[chunk] = (total + dot(dbd[chunk], wb[...], across)).astype(BF16)

    def both_ways(i, fn):
        for k in (place.chip + i, place.chip - i):
            pl.when((k >= 0) & (k < chips))(functools.partial(fn, k))

    @pl.when(step == 0)
    def _():
        for i in range(chips - 1, 0, -1):
            both_ways(i, out_red.collect)
        out_red.collect(place.chip)

    for i in range(chips - 1, -1, -1):

        @pl.when(step == steps - 1 - max(i, 0) * (steps - 3) // chips)
        def _():
            if i:
                both_ways(i, out_red.settle)
            else:
                out_red.settle(place.chip)

    @pl.when(lax.rem(step, 2) == 1)
    def _():
        dn_red.start(chunk // 2)

    @pl.when((lax.rem(step, 2) == 0) & (step >= 2))
    def _():
        dn_red.collect(chunk // 2 + 1)

    wait = 6

    @pl.when((lax.rem(step, 2) == 0) & (step >= wait))
    def _():
        dn_red.settle(chunk // 2 + wait // 2)

    @pl.when(step == steps - 1)
    def _():
        dn_red.collect(jnp.int32(0))
        load.wait()
        share_rows = tx.shape[1] * tx.shape[2]
        rows_all = blocks * rows
        small[:, : chans + wide] = dtaps[...]
        small[5:6, :chans] = dskip[0:1, :]
        small[:, chans + wide :] = dheads[...]
        few.start()
        turned = dx[...].reshape(rows_all, -1)
        turned_b = dbd[...].reshape(rows_all, -1)
        for mask in list(range(1, dp)) + [0]:
            other = place.masked(mask)
            first = pl.multiple_of(other * share_rows, LANES)
            columns = normed[:, :, pl.ds(first, share_rows)].reshape(rows_all, share_rows)
            for red, values in ((x_red, turned), (b_red, turned_b)):
                value = dot(columns, values, ((0,), (0,))).astype(BF16)
                value = value.reshape(red.terms.shape[1:])
                if mask:
                    red.terms[other] = value
                    red.dp_copy(mask).start()
                else:
                    red.buf[0] = value
        gate_red.add()
        out_grads.add()
        for k in range(chips - 1 - (steps - 1 - wait) // 2 - 1, -1, -1):
            dn_red.settle(jnp.int32(k))
        few.add()
        x_red.add(kept=False)
        b_red.add(kept=False)
        out_red.finish()
        out_total[...] = out_red.total[...]
        dn_red.finish()
        dn_total[...] = dn_red.total[...]
        gate_red.finish()
        out_grads.finish()
        few.finish()
        osmall[...] = landed[...]
        x_red.finish()
        b_red.finish()


def run_backward(
    dp, sp, seqs, dy, x, bd, dgate, enter, taps, heads, skip, wg, wx, wb,
    normed, out_part, terms_out, terms_gate, wide,
):
    blocks, rows, chans = x.shape
    states = wide // 2
    cols, width = bd.shape[2], normed.shape[2]
    share = terms_gate.shape[2]
    back = lambda i: blocks - 1 - i
    block = lambda n: pl.BlockSpec((None, rows, n), lambda i: (back(i), 0, 0))
    whole = lambda a: pl.BlockSpec(a.shape, lambda i: (0,) * a.ndim)
    before = lambda n: pl.BlockSpec(
        (None, 16, n), lambda i: (jnp.maximum(back(i) - 1, 0), rows // 16 - 1, 0)
    )
    fixed = lambda *shape: pl.BlockSpec(shape, lambda i: (0,) * len(shape))
    tokens = (seqs, rows, width)
    small = (8, chans + wide + LANES)
    reduce = lambda n: ShardReduce.scratch(dp, sp, (share, n))
    return pl.pallas_call(
        functools.partial(backward_kernel, dp, sp, seqs, wide, chans),
        grid=(blocks,),
        in_specs=[
            block(chans), block(chans), before(chans), block(cols), before(cols), block(chans),
            pl.BlockSpec((None, states, chans), lambda i: (back(i), 0, 0)),
            whole(taps), whole(heads), whole(skip), whole(wg), whole(wx), whole(wb),
        ]
        + [ANY] * 4,
        out_specs=[fixed(*tokens), fixed(*tokens)] + [ANY] * 3
        + [ANY, fixed(sp, *small)],
        out_shape=[
            jax.ShapeDtypeStruct(tokens, BF16),
            jax.ShapeDtypeStruct(tokens, BF16),
            jax.ShapeDtypeStruct((sp, share, chans), BF16),
            jax.ShapeDtypeStruct((sp, share, chans), BF16),
            jax.ShapeDtypeStruct((sp, share, cols), BF16),
            jax.ShapeDtypeStruct((seqs,) + terms_out.shape[1:], BF16),
            jax.ShapeDtypeStruct((sp,) + small, F32),
        ],
        scratch_shapes=[
            pltpu.VMEM((rows + 8, chans + wide), F32),
            pltpu.VMEM((rows + 8, chans + wide), F32),
            pltpu.VMEM((8, chans + wide), F32),
            pltpu.VMEM((states, chans), F32),
            pltpu.VMEM((8, chans + wide), F32),
            pltpu.VMEM((8, LANES), F32),
            pltpu.VMEM((8, chans), F32),
            pltpu.VMEM((blocks, rows, chans), BF16),
            pltpu.VMEM((blocks, rows, cols), BF16),
            pltpu.VMEM(normed.shape, BF16),
            pltpu.VMEM((blocks, rows, width), BF16),
            dma(1),
            pltpu.VMEM((dp, sp, share, chans), BF16),
            pltpu.VMEM((dp, sp, share, cols), BF16),
            pltpu.VMEM(small, F32),
            pltpu.VMEM((sp,) + small, F32),
        ]
        + BlockReduce.scratch(dp, sp, seqs, rows, width, True)
        + BlockReduce.scratch(dp, sp, seqs, rows, width, False)
        + reduce(chans) + reduce(chans) + reduce(cols)
        + OutReduce.scratch(dp, sp, seqs, terms_out.shape[1:])
        + SmallReduce.scratch(dp, sp, seqs, small),
        compiler_params=comm_params(4),
        name="backward",
    )(
        dy, x, x, bd, bd, dgate, enter, taps, heads, skip, wg, wx, wb,
        normed, out_part, terms_out, terms_gate,
    )


def pad_last(value, size):
    return jnp.pad(value, [(0, 0)] * (value.ndim - 1) + [(0, size - value.shape[-1])])


def eight_rows(*rows):
    stacked = jnp.stack(rows, axis=0)
    return jnp.pad(stacked, ((0, 8 - stacked.shape[0]), (0, 0)))


def on_device(
    dp, sp,
    hidden_in, w_zx, w_bc, w_dt, norm_gain, conv_bc_weight, conv_bc_bias,
    conv_x_weight, conv_x_bias, dt_bias, a_log, d_skip, gate_gain, w_out, cotangent,
):
    me_dp, me_sp = lax.axis_index("dp"), lax.axis_index("sp")
    seqs, block, width = hidden_in.shape
    groups = sp // seqs
    group = lax.rem(me_sp, groups)
    rows = sp * block
    wide, heads = w_bc.shape[1], w_dt.shape[1]
    share, taps_n = w_zx.shape[0], conv_x_weight.shape[1]
    inner = heads * P_SIZE
    chans = inner // groups
    own_heads = heads // groups
    gate_share, bc_share = gate_gain.shape[0], conv_bc_bias.shape[0]
    x_share, head_share = conv_x_bias.shape[0], dt_bias.shape[0]
    cols = wide + LANES

    small = jnp.concatenate(
        [
            norm_gain,
            gate_gain,
            jnp.concatenate([conv_bc_weight, conv_bc_bias[:, None]], axis=1).reshape(-1),
            jnp.concatenate([conv_x_weight, conv_x_bias[:, None]], axis=1).reshape(-1),
            dt_bias,
            a_log,
            d_skip,
        ]
    )
    spare = cols - wide - heads
    high = -(-max(share, -(-small.shape[0] // spare)) // 16) * 16
    tall = lambda v: jnp.pad(v, ((0, high - share), (0, 0)))
    misc = jnp.concatenate(
        [tall(w_bc), tall(w_dt), pad_last(small, high * spare).reshape(high, spare)], axis=1
    )
    wx, misc_all, hidden_all = run_first(dp, sp, seqs, chans, w_zx, misc, hidden_in)
    misc_all = jnp.transpose(misc_all, (1, 2, 0, 3, 4)).reshape((dp, sp) + misc.shape)

    wx = wx.reshape(width, chans)
    bd_all = misc_all[:, :, :share, :].reshape(width, cols)
    dt_cols = lax.dynamic_slice_in_dim(bd_all[:, wide : wide + heads], group * own_heads, own_heads, axis=1)
    wb = jnp.concatenate([bd_all[:, :wide], pad_last(dt_cols, LANES)], axis=1)
    few = misc_all[:, :, :, wide + heads :].reshape(dp, sp, high * spare)
    ends = []
    for size in (share, gate_share, bc_share * (taps_n + 1), x_share * (taps_n + 1)) + (head_share,) * 3:
        ends.append(size + (ends[-1] if ends else 0))
    piece = lambda i: few[:, :, (ends[i - 1] if i else 0) : ends[i]]
    mine = lambda i: lax.dynamic_slice_in_dim(piece(i)[0], group * seqs, seqs, axis=0).astype(F32)
    norm_all = piece(0).reshape(width).astype(F32)
    gate_mine = lax.dynamic_slice_in_dim(
        piece(1).reshape(inner), group * chans, chans
    ).astype(F32)
    bc_all = piece(2).reshape(wide, taps_n + 1).astype(F32)
    x_all = mine(3).reshape(chans, taps_n + 1)
    taps = jnp.concatenate([x_all, bc_all], axis=0).T
    taps = jnp.pad(taps, ((0, 8 - taps.shape[0]), (0, 0)))
    head_rows = eight_rows(
        pad_last(mine(4).reshape(own_heads), LANES),
        pad_last(jnp.exp(mine(5).reshape(own_heads)), LANES),
    )
    skip = eight_rows(jnp.repeat(mine(6).reshape(own_heads), P_SIZE))
    gain = eight_rows(gate_mine)

    wg, out_mine, cot_all, normed, x_blocks, bd_blocks, entering, gated, dgate, dy = run_middle(
        dp, sp, seqs, wide, inner, w_zx, w_out, cotangent, hidden_all, wx, wb,
        eight_rows(norm_all), taps, head_rows, skip, gain,
    )
    normed, gated, cot_rows = (v.reshape(rows, -1) for v in (normed, gated, cot_all))
    out_rows = out_mine.reshape(chans, width)
    out_part = dot(gated, out_rows).astype(BF16).reshape(sp, block, width)
    terms_out = dot(gated, cot_rows, ((0,), (0,))).astype(BF16).reshape(sp, gate_share, width)
    terms_gate = dot(normed, dgate.reshape(rows, chans), ((0,), (0,))).astype(BF16)
    out_sum, d_normed, og, ox, ob, oo, osmall = run_backward(
        dp, sp, seqs, dy, x_blocks, bd_blocks, dgate, entering, taps, head_rows, skip,
        wg.reshape(width, chans), wx, wb, normed.reshape(sp, block, width), out_part, terms_out,
        terms_gate.reshape(dp, sp, share, chans), wide,
    )
    hidden_out = (hidden_in.astype(F32) + out_sum.astype(F32)).astype(BF16)
    spread_cols = lambda v: jnp.transpose(
        jnp.sum(v.astype(F32).reshape(seqs, groups, share, -1), axis=0), (1, 0, 2)
    ).reshape(share, -1)
    grad_w_zx = jnp.concatenate([spread_cols(og), spread_cols(ox)], axis=1)
    ob = ob.astype(F32)
    grad_w_bc = jnp.sum(ob[:, :, :wide], axis=0)
    grad_w_dt = spread_cols(ob[:, :, wide : wide + own_heads])
    grad_norm_gain = (
        jnp.sum(grad_w_zx * w_zx.astype(F32), axis=1)
        + jnp.sum(grad_w_bc * w_bc.astype(F32), axis=1)
        + jnp.sum(grad_w_dt * w_dt.astype(F32), axis=1)
    ) / norm_gain.astype(F32)
    grad_w_out = jnp.sum(oo.astype(F32), axis=0)
    grad_gate_gain = jnp.sum(grad_w_out * w_out.astype(F32), axis=1) / gate_gain.astype(F32)

    hid = hidden_in.reshape(seqs * block, width).astype(F32)
    scale_own = lax.rsqrt(jnp.mean(hid * hid, axis=-1, keepdims=True) + EPS)
    unit_own = hid * scale_own
    weighted = d_normed.reshape(seqs * block, width).astype(F32) * norm_all
    grad_rows = cotangent.reshape(seqs * block, width).astype(F32) + scale_own * (
        weighted - unit_own * jnp.mean(weighted * unit_own, axis=-1, keepdims=True)
    )
    grad_hidden = grad_rows.astype(BF16).reshape(hidden_in.shape)

    by_group = jnp.sum(osmall.reshape(seqs, groups, 8, -1), axis=0)
    from_group = lax.dynamic_index_in_dim(by_group, me_sp // seqs, axis=0, keepdims=False)
    part = lax.rem(me_sp, seqs)
    g_x = lax.dynamic_slice_in_dim(from_group[:, :chans], part * x_share, x_share, axis=1)
    g_heads = lax.dynamic_slice_in_dim(
        from_group[:, chans + wide :], part * head_share, head_share, axis=1
    )
    g_skip = jnp.sum(g_x[5].reshape(head_share, P_SIZE), axis=1)
    g_bc = jnp.sum(by_group[:, :, chans : chans + wide], axis=0)
    first = (me_dp * sp + me_sp) * bc_share
    g_bc = lax.dynamic_slice_in_dim(g_bc, first, bc_share, axis=1)
    return (
        hidden_out,
        grad_hidden,
        grad_w_zx,
        grad_w_bc,
        grad_w_dt,
        grad_norm_gain,
        g_bc[:taps_n].T,
        g_bc[taps_n],
        g_x[:taps_n].T,
        g_x[taps_n],
        g_heads[0],
        g_heads[1],
        g_skip,
        grad_gate_gain,
        grad_w_out,
    )


def solution(mesh):
    both = P(("dp", "sp"))
    rows = P(("dp", "sp"), None)
    tokens = P("dp", "sp", None)
    return jax.shard_map(
        functools.partial(on_device, mesh.shape["dp"], mesh.shape["sp"]),
        mesh=mesh,
        in_specs=(
            tokens, rows, rows, rows, both, rows, both, P("sp", None), P("sp"), P("sp"),
            P("sp"), P("sp"), both, rows, tokens,
        ),
        out_specs=(
            tokens, tokens, rows, rows, rows, both, rows, both, P("sp", None), P("sp"),
            P("sp"), P("sp"), P("sp"), both, rows,
        ),
        check_vma=False,
    )
```

time: 591 us -> 379 us (0.64); the launches traced: 584 us -> 379 us
  Pallas kernels: 54.6 us -> 335 us
  blocking collectives: 228 us -> 0 us
  waiting for transfers between devices: 167 us -> 0 us
  matrix products: 60.8 us -> 14.5 us
  between operations: 15.2 us -> 1.12 us
  local copies, waits for them, and re-layouts: 29.1 us -> 15.3 us
  other arithmetic: 21.5 us -> 12.9 us
  starting transfers between devices: 7.21 us -> 0 us
    pallas_call x2 -> x3, Pallas kernels: 54.6 us -> 335 us  [the longest x1 143 us: run_backward(): pl.pallas_call(functools.partial(backward_kernel, dp, sp, seqs, wide, cha...]
    reduce_scatter x4 -> x0, waiting for transfers between devices: 117 us -> none  [the longest x1 72 us: on_device(): out_sum = lax.psum_scatter(out_part, 'sp', scatter_dimension=0, tiled=False)]
    psum x3 -> x0, blocking collectives: 86.1 us -> none  [the longest x1 42.2 us: on_device(): g_bc = lax.psum(dtaps[:5, chans:], both)]
    unnamed x1 -> x0, blocking collectives: 62.3 us -> none
    all_gather x1 -> x0, blocking collectives: 56.9 us -> none  [on_device(): lax.all_gather(jnp.concatenate([w_bc, w_dt], axis=1), both, axis=0, tiled...]
    all_gather x4 -> x0, waiting for transfers between devices: 49.3 us -> none  [the longest x1 49.2 us: on_device(): cot_all = lax.all_gather(cotangent, 'sp', axis=0, tiled=False)]
    dot_general x6 -> x3, matrix products: 60.8 us -> 14.5 us  [dot(): lax.dot_general(left, right, (dims, ((), ())), precision=precision, prefe...]
    all_to_all x1 -> x0, blocking collectives: 22.9 us -> none  [on_device(): lax.all_to_all(zx_parts, 'sp', split_axis=0, concat_axis=0, tiled=True)]
  transfers between devices with their start and end apart: 11 -> 0, of which waited for: 4 -> 0; matrix products, arithmetic and copies ran while one was open for 12% -> 0% of each run, Pallas kernels for 3% -> 0%
where the time goes in v3:
time: 379 us
  Pallas kernels  335 us (88%)
  local copies, waits for them, and re-layouts  15.3 us (4%)
  matrix products  14.5 us (4%)
  other arithmetic  12.9 us (3%)
    pallas_call x1, Pallas kernels, run_backward(): pl.pallas_call(functools.partial(backward_kernel, dp, sp, seqs, wide, cha...  143 us
    pallas_call x1, Pallas kernels, run_middle(): pl.pallas_call(functools.partial(forward_kernel, dp, sp, seqs, wide, inne...  135 us
    pallas_call x1, Pallas kernels, run_first(): pl.pallas_call(functools.partial(first_kernel, dp, sp, seqs, chans), in_s...  56.3 us
    dot_general x3, matrix products, dot(): lax.dot_general(left, right, (dims, ((), ())), precision=precision, prefe...  14.5 us

profile of v3, /device:TPU:0, one launch (start us, length us, event | category | flops | bytes accessed | tf_op | source)
XLA Modules:
  0.0 378.5 jit_solution(17828689203969954957)
XLA Ops:
  0.6 0.7 pad_maximum_fusion.2
  1.4 0.1 copy.55
  1.4 0.1 reshape.190
  1.5 0.7 broadcast_in_dim.13
  2.2 0.7 pad_maximum_fusion.1
  2.9 0.2 copy.56
  3.1 0.2 reshape.191
  3.3 3.4 concatenate.24
  6.8 0.1 reshape.192
  6.8 1.5 pad_maximum_fusion.misc_ref
  8.3 56.3 %first_gather.1 = (bf16[4,8,48,768]{3,2,1,0:T(8,128)(2,1)}, bf16[2,4,4,48,384]{4,3,2,1,0:T(8,128)(2,1)}, bf16[8,128,1536]{2,1,0:T(8,128)(2,1)}) custom-call(bf16[48,6144]{1,0:T(8,128)(2,1)} %w_ref.3, bf16[48,384]{1,0:T(8,128)(2,1)} %pad_maximum_fusion.misc_ref, bf16[2,128,1536]{2,1,0:T(8,128)(2,1)} %hid_ref.1), custom_call_target="tpu_custom_call" | custom-call | tf_op jit(solution)/shard_map/first_gather/pallas_call | solution.py:905
  64.6 1.4 copy.57
  66.0 0.2 constant_dynamic-slice_fusion.6
  66.3 1.1 fusion.10.wb_ref.wb
  67.4 0.2 slice.98
  67.6 0.4 reshape.195
  67.9 0.1 convert_element_type.122
  68.0 0.6 pad_convert_fusion.norm
  68.7 0.1 slice.101
  68.7 0.1 convert_element_type.124
  68.8 0.1 copy.60
  68.9 0.1 slice.100
  69.0 0.3 convert_element_type.123
  69.4 0.1 copy.59
  69.5 0.6 pad_convert_fusion.1.taps
  70.2 0.1 exp.7
  70.3 0.1 convert_element_type.125
  70.4 0.6 select_maximum_fusion.heads
  71.0 0.1 reshape.213
  71.2 0.1 stack_reshape.3
  71.3 0.6 pad.50.skip
  71.9 0.1 slice.105
  72.0 0.1 reshape.196
  72.1 0.1 dynamic_slice.36
  72.2 0.6 pad_convert_fusion.2.gain
  72.8 135.1 %forward.1 = (bf16[4,8,48,768]{3,2,1,0:T(8,128)(2,1)}, bf16[8,96,1536]{2,1,0:T(8,128)(2,1)}, bf16[8,128,1536]{2,1,0:T(8,128)(2,1)}, bf16[8,128,1536]{2,1,0:T(8,1...) custom-call(bf16[48,6144]{1,0:T(8,128)(2,1)} %w_ref.3, ...), custom_call_target="tpu_custom_call" | custom-call | tf_op jit(solution)/shard_map/forward/pallas_call | solution.py:1127
  207.9 6.5 %convolution_convert_fusion = bf16[1024,1536]{1,0:T(8,128)(2,1)} fusion(bf16[1024,768]{1,0:T(8,128)(2,1)} %bitcast.78, bf16[768,1536]{1,0:T(8,128)(2,1)} %bitcast.77), kind=kOutput, calls=%fused_computation.2 | convolution fusion | flops 2417491968 | bytes 7077888 | tf_op jit(solution)/shard_map/dot_general | solution.py:20
  214.5 4.0 %bitcast_convert_fusion.1 = bf16[768,1536]{1,0:T(8,128)(2,1)} fusion(bf16[8,128,768]{2,1,0:T(8,128)(2,1)S(1)} %copy-done.21, bf16[8,128,1536]{2,1,0:T(8,128)(2,1)S(1)} %copy-done.20), kind=kOutput, calls=%fused_computation.1 | convolution fusion | flops 2417098752 | bytes 7077888 | tf_op jit(solution)/shard_map/dot_general | solution.py:20
  218.5 4.0 %bitcast_convert_fusion = bf16[1536,768]{1,0:T(8,128)(2,1)} fusion(bf16[8,128,1536]{2,1,0:T(8,128)(2,1)S(1)} %copy-done.3, bf16[8,128,768]{2,1,0:T(8,128)(2,1)S(1)} %copy-done.7), kind=kOutput, calls=%fused_computation | convolution fusion | flops 2417098752 | bytes 7077888 | tf_op jit(solution)/shard_map/dot_general | solution.py:20
  222.5 143.3 %backward.1 = (bf16[2,128,1536]{2,1,0:T(8,128)(2,1)}, bf16[2,128,1536]{2,1,0:T(8,128)(2,1)}, bf16[8,48,768]{2,1,0:T(8,128)(2,1)}, bf16[8,48,768]{2,1,0:T(8,128)(...) custom-call(bf16[8,128,768]{2,1,0:T(8,128)(2,1)} %get-tuple-element.38.dy, ...), custom_call_target="tpu_custom_call" | custom-call | tf_op jit(solution)/shard_map/backward/pallas_call | solution.py:1299
  365.9 0.2 fusion.9
  366.1 1.7 fusion.3
  367.9 1.8 fusion.7
  369.8 0.1 convert_reduce_fusion.1
  369.9 0.9 copy-done.12
  370.8 0.1 convert_reduce_fusion
  371.0 0.7 copy-done.9
  372.0 0.1 copy.65
  372.1 0.7 copy.67
  372.8 0.1 copy.66
  372.9 0.2 multiply_reduce_fusion
  373.2 0.1 multiply_reduce_fusion.2
  373.3 0.5 convert_divide_fusion.1
  373.9 0.1 constant_dynamic-slice_fusion.1
  373.9 0.6 slice_bitcast_fusion
  374.5 0.5 slice_bitcast_fusion.3
  375.0 0.6 dynamic-slice_bitcast_fusion.1
  375.6 0.7 dynamic-slice_reduce_fusion
  376.4 0.5 slice_bitcast_fusion.1
  377.0 0.6 reduce_sum.137
  377.6 0.1 convert_reduce_fusion.2
  377.7 0.2 multiply_reduce_fusion.1
  377.9 0.5 convert_divide_fusion
  378.4 0.1 copy-done.6
  (74 shorter events, 1.0 us)
Async XLA Ops:
  207.9 6.6 %copy-start.20 = (bf16[8,128,1536]{2,1,0:T(8,128)(2,1)S(1)}, bf16[8,128,1536]{2,1,0:T(8,128)(2,1)}, u32[]{:S(2)}) copy-start(bf16[8,128,1536]{2,1,0:T(8,128)(2,1)} %get-tuple-element.47) | copy-start | bytes 9437188
  207.9 6.5 %copy-start.21 = (bf16[8,128,768]{2,1,0:T(8,128)(2,1)S(1)}, bf16[8,128,768]{2,1,0:T(8,128)(2,1)}, u32[]{:S(2)}) copy-start(bf16[8,128,768]{2,1,0:T(8,128)(2,1)} %get-tuple-element.45) | copy-start | bytes 4718596
  214.5 4.0 %copy-start.3 = (bf16[8,128,1536]{2,1,0:T(8,128)(2,1)S(1)}, bf16[8,128,1536]{2,1,0:T(8,128)(2,1)}, u32[]{:S(2)}) copy-start(bf16[8,128,1536]{2,1,0:T(8,128)(2,1)} %get-tuple-element.44.normed_ref) | copy-start | bytes 9437188
  214.5 4.0 %copy-start.7 = (bf16[8,128,768]{2,1,0:T(8,128)(2,1)S(1)}, bf16[8,128,768]{2,1,0:T(8,128)(2,1)}, u32[]{:S(2)}) copy-start(bf16[8,128,768]{2,1,0:T(8,128)(2,1)} %get-tuple-element.41.dgate) | copy-start | bytes 4718596
  222.5 143.4 %copy-start = (bf16[2,128,1536]{2,1,0:T(8,128)(2,1)S(1)}, bf16[2,128,1536]{2,1,0:T(8,128)(2,1)}, u32[]{:S(2)}) copy-start(bf16[2,128,1536]{2,1,0:T(8,128)(2,1)} %hid_ref.1) | copy-start | bytes 2359300
  365.8 2.1 copy-start.2
  365.8 2.1 copy-start.4
  365.8 2.1 copy-start.10
  367.9 1.8 copy-start.13
  369.8 1.1 copy-start.12
  370.8 1.0 copy-start.9
  371.0 1.8 copy-start.17
  371.0 1.9 copy-start.1
  371.0 2.1 copy-start.5
  371.8 1.3 copy-start.16
  371.8 1.4 copy-start.18
  371.9 2.0 copy-start.14
  371.9 1.9 copy-start.15
  371.9 5.7 %copy-start.11 = (bf16[2,96,1536]{2,1,0:T(8,128)(2,1)S(1)}, bf16[2,96,1536]{2,1,0:T(8,128)(2,1)}, u32[]{:S(2)}) copy-start(bf16[2,96,1536]{2,1,0:T(8,128)(2,1)} %get-tuple-element.54) | copy-start | bytes 1769476
  372.9 4.8 %copy-start.8 = (bf16[96,1536]{1,0:T(8,128)(2,1)S(1)}, bf16[96,1536]{1,0:T(8,128)(2,1)}, u32[]{:S(2)}) copy-start(bf16[96,1536]{1,0:T(8,128)(2,1)} %o_ref.1) | copy-start | bytes 884740
  373.2 4.7 %copy-start.19 = (bf16[96]{0:T(256)(128)(2,1)S(1)}, bf16[96]{0:T(256)(128)(2,1)}, u32[]{:S(2)}) copy-start(bf16[96]{0:T(256)(128)(2,1)} %param.27) | copy-start | bytes 580
  377.7 0.8 copy-start.6

commit v4 on v3

--- a/solution.py
+++ b/solution.py
@@ -273,13 +273,28 @@
         for copy in self.children(odd, 0):
             copy.start()
 
-    def forward(self, odd):
-        at = self.at
-        for mask in sorted(range(1, at.dp), key=lambda m: (bin(m).count("1"), m)):
-            dst = self.part(at.masked(mask), odd)
-            remote(dst, dst, self.send.at[odd, 0, 0], self.recv.at[odd, mask], at.along_dp(at.p)).wait_recv()
-            for copy in self.children(odd, mask):
-                copy.start()
+    def arrived(self, odd, mask):
+        at = self.at
+        dst = self.part(at.masked(mask), odd)
+        remote(dst, dst, self.send.at[odd, 0, 0], self.recv.at[odd, mask], at.along_dp(at.p)).wait_recv()
+
+    def passed(self, odd, mask):
+        order = self.at.bits if odd == 0 else self.at.bits[::-1]
+        return not mask & order[-1]
+
+    def forward(self):
+        for mask in sorted(range(1, self.at.dp), key=lambda m: (bin(m).count("1"), m)):
+            for odd in range(2):
+                if self.passed(odd, mask):
+                    self.arrived(odd, mask)
+                    for copy in self.children(odd, mask):
+                        copy.start()
+
+    def complete(self):
+        for mask in range(1, self.at.dp):
+            for odd in range(2):
+                if not self.passed(odd, mask):
+                    self.arrived(odd, mask)
 
     def finish(self):
         for odd in range(2):
@@ -294,12 +309,16 @@
 
     def holder(self, seq):
         at = self.at
-        p, s = at.s // self.each, seq * at.groups + at.p
+        p, s = lax.rem(at.s // self.each + at.p, at.dp), seq * at.groups + at.p
         return (p, s), (p == at.p) & (s == at.s)
 
+    def first(self, p):
+        at = self.at
+        return lax.rem(p + at.dp - at.group, at.dp) * self.each
+
     def owner(self, i):
         at = self.at
-        p, s = at.group, at.p * self.each + i
+        p, s = at.group, self.first(at.p) + i
         return (p, s), (p == at.p) & (s == at.s)
 
     def meet(self, spread):
@@ -330,7 +349,7 @@
         self.ways = Owners(place)
         each = self.ways.each
         size = each // 2
-        part = lambda p, odd: out.at[pl.ds(p * each + odd * size, size)]
+        part = lambda p, odd: out.at[pl.ds(self.ways.first(p) + odd * size, size)]
         self.tree = DpTree(place, part, *tree)
 
     def shard_copy(self, seq):
@@ -354,7 +373,7 @@
         at, each = self.at, self.ways.each
         for i in range(odd * each // 2, (odd + 1) * each // 2):
             _, mine = self.ways.owner(i)
-            slot = at.p * each + i
+            slot = self.ways.first(at.p) + i
             pl.when(mine)(lambda: self.keep().wait())
 
             @pl.when(jnp.logical_not(mine))
@@ -364,8 +383,11 @@
 
         self.tree.start(odd)
 
-    def forward(self, odd):
-        self.tree.forward(odd)
+    def forward(self):
+        self.tree.forward()
+
+    def complete(self):
+        self.tree.complete()
 
     def finish(self):
         for seq in range(self.at.seqs):
@@ -491,130 +513,159 @@
             pl.when((at.chip == out) & (at.chip != k))(lambda: self.ending(k).wait_send())
 
 
+class TreeReduce:
+    @staticmethod
+    def scratch(dp, half, kept):
+        own = [pltpu.VMEM((2, dp // 2) + half, BF16)] if kept else []
+        return own + [pltpu.VMEM((2, dp - 1) + half, BF16), dma(3, 2, dp)]
+
+    def __init__(self, place, source, kept, *scratch):
+        self.at, self.source = place, source
+        self.own = scratch[0] if kept else None
+        self.recv, sems = scratch[-2:]
+        self.send_sem, self.recv_sem, self.local = (sems.at[i] for i in range(3))
+        self.steps = len(place.bits)
+
+    def order(self, odd):
+        return self.at.bits if odd == 0 else self.at.bits[::-1]
+
+    def kept(self, odd):
+        return [m for m in range(self.at.dp) if not m & self.order(odd)[0]]
+
+    def block(self, odd, mask):
+        if self.own is None:
+            return self.source(self.at.masked(mask), odd)
+        return self.own.at[odd, self.kept(odd).index(mask)]
+
+    def sent(self, odd, i):
+        order = self.order(odd)
+        before = sum(order[:i])
+        masks = [m for m in range(self.at.dp) if m & order[i] and not m & before]
+        first = sum(self.at.dp >> (k + 1) for k in range(i))
+        return [(first + n, m) for n, m in enumerate(masks)]
+
+    def copy(self, odd, i, n, mask):
+        at = self.at
+        src = self.block(odd, mask) if i else self.source(at.masked(mask), odd)
+        return remote(
+            src, self.recv.at[odd, n], self.send_sem.at[odd, n], self.recv_sem.at[odd, n],
+            at.along_dp(at.flip(self.order(odd)[i])),
+        )
+
+    def load(self, odd, mask):
+        n = self.kept(odd).index(mask)
+        return pltpu.make_async_copy(
+            self.source(self.at.masked(mask), odd), self.own.at[odd, n], self.local.at[odd, n]
+        )
+
+    def start(self):
+        for odd in range(2):
+            for n, mask in self.sent(odd, 0):
+                self.copy(odd, 0, n, mask).start()
+            if self.own is not None:
+                for mask in self.kept(odd):
+                    self.load(odd, mask).start()
+
+    def step(self, i):
+        for odd in range(2):
+            if i == 0 and self.own is not None:
+                for mask in self.kept(odd):
+                    self.load(odd, mask).wait()
+            bit = self.order(odd)[i]
+            for n, mask in self.sent(odd, i):
+                self.copy(odd, i, n, mask).wait_recv()
+                block = self.block(odd, mask ^ bit)
+                block[...] = (block[...].astype(F32) + self.recv[odd, n].astype(F32)).astype(BF16)
+            if i + 1 < self.steps:
+                for n, mask in self.sent(odd, i + 1):
+                    self.copy(odd, i + 1, n, mask).start()
+
+    def total(self, odd):
+        return self.block(odd, 0)
+
+    def finish(self):
+        for odd in range(2):
+            for i in range(self.steps):
+                for n, mask in self.sent(odd, i):
+                    self.copy(odd, i, n, mask).wait_send()
+
+
 class ShardReduce:
     @staticmethod
-    def scratch(dp, sp, shape):
-        return [
-            pltpu.VMEM((dp, sp) + shape, BF16),
-            dma(2, dp), dma(2, sp), dma(1),
-        ]
-
-    def __init__(self, place, terms, out, buf, along_dp, along_sp, local):
-        self.at, self.terms, self.out, self.buf = place, terms, out, buf
-        self.dp_sems, self.sp_sems, self.local = along_dp, along_sp, local.at[0]
-
-    def dp_copy(self, mask):
-        at = self.at
+    def scratch(dp, sp, shape, kept):
+        return [dma(2, sp), dma(1)] + TreeReduce.scratch(dp, (sp // 2,) + shape, kept)
+
+    def __init__(self, place, terms, out, kept, sems, local, *tree):
+        self.at, self.out, self.sems, self.local = place, out, sems, local.at[0]
+        self.size = place.sp // 2
+        source = lambda p, odd: terms.at[p, pl.ds(odd * self.size, self.size)]
+        self.tree = TreeReduce(place, source, kept, *tree)
+
+    def sp_copy(self, slot):
+        at = self.at
+        src = self.tree.total(slot // self.size).at[slot % self.size]
         return remote(
-            self.terms.at[at.masked(mask)], self.buf.at[mask], self.dp_sems.at[0, mask],
-            self.dp_sems.at[1, mask], at.along_dp(at.masked(mask)),
-        )
-
-    def keep(self):
-        return pltpu.make_async_copy(self.terms.at[self.at.p], self.buf.at[0], self.local)
-
-    def sp_copy(self, i):
-        at = self.at
-        target = at.sp_peer(i)
-        return remote(
-            self.buf.at[0, target], self.out.at[at.s], self.sp_sems.at[0, i], self.sp_sems.at[1, i],
-            at.along_sp(target),
-        )
-
-    def back(self):
-        at = self.at
-        return pltpu.make_async_copy(self.buf.at[0, at.s], self.out.at[at.s], self.local)
-
-    def start(self):
-        for mask in range(1, self.at.dp):
-            self.dp_copy(mask).start()
-        self.keep().start()
-
-    def add(self, kept=True):
-        at = self.at
-        if kept:
-            self.keep().wait()
-        for mask in range(1, at.dp):
-            self.dp_copy(mask).wait_recv()
-        for i in list(range(1, at.sp)) + [0]:
-            slot = at.sp_peer(i)
-            total = self.buf[0, slot].astype(F32)
-            for mask in range(1, at.dp):
-                total = total + self.buf[mask, slot].astype(F32)
-            self.buf[0, slot] = total.astype(BF16)
-            if i:
-                self.sp_copy(i).start()
-            else:
-                self.back().start()
+            src, self.out.at[at.s], self.sems.at[0, slot], self.sems.at[1, at.s], at.along_sp(slot)
+        )
+
+    def back(self, slot):
+        src = self.tree.total(slot // self.size).at[slot % self.size]
+        return pltpu.make_async_copy(src, self.out.at[slot], self.local)
+
+    def spread(self):
+        for slot in range(self.at.sp):
+            pl.when(self.at.s == slot)(lambda: self.back(slot).start())
+            pl.when(self.at.s != slot)(lambda: self.sp_copy(slot).start())
 
     def finish(self):
         at = self.at
-        for mask in range(1, at.dp):
-            self.dp_copy(mask).wait_send()
-        for i in range(1, at.sp):
-            dst = self.out.at[lax.rem(at.s + at.sp - i, at.sp)]
-            remote(dst, dst, self.sp_sems.at[0, i], self.sp_sems.at[1, i], at.along_sp(at.s)).wait_recv()
-            self.sp_copy(i).wait_send()
-        self.back().wait()
+        self.tree.finish()
+        for slot in range(at.sp):
+
+            @pl.when(at.s == slot)
+            def _():
+                self.back(slot).wait()
+
+            @pl.when(at.s != slot)
+            def _():
+                dst = self.out.at[slot]
+                remote(dst, dst, self.sems.at[0, 0], self.sems.at[1, slot], at.along_sp(at.s)).wait_recv()
+                self.sp_copy(slot).wait_send()
 
 
 class OutReduce:
     @staticmethod
     def scratch(dp, sp, seqs, shape):
         each = sp // dp
-        return [pltpu.VMEM((dp, each) + shape, BF16), dma(2, dp), dma(each), dma(seqs), dma(2)]
-
-    def __init__(self, place, terms, out, buf, dp_sems, sent, got, local):
-        self.at, self.terms, self.out, self.buf = place, terms, out, buf
-        self.dp_sems, self.sent, self.got, self.local = dp_sems, sent, got, local
+        return [dma(each), dma(seqs), dma(1)] + TreeReduce.scratch(dp, (each // 2,) + shape, True)
+
+    def __init__(self, place, terms, out, sent, got, local, *tree):
+        self.at, self.out = place, out
+        self.sent, self.got, self.local = sent, got, local.at[0]
         self.ways = Owners(place)
-
-    def shards(self, p):
-        return self.terms.at[pl.ds(p * self.ways.each, self.ways.each)]
-
-    def dp_copy(self, mask):
-        at = self.at
-        return remote(
-            self.shards(at.masked(mask)), self.buf.at[mask], self.dp_sems.at[0, mask],
-            self.dp_sems.at[1, mask], at.along_dp(at.masked(mask)),
-        )
-
-    def keep(self):
-        return pltpu.make_async_copy(self.shards(self.at.p), self.buf.at[0], self.local.at[0])
-
-    def start(self):
-        for mask in range(1, self.at.dp):
-            self.dp_copy(mask).start()
-        self.keep().start()
+        self.size = self.ways.each // 2
+        source = lambda p, odd: terms.at[pl.ds(self.ways.first(p) + odd * self.size, self.size)]
+        self.tree = TreeReduce(place, source, True, *tree)
 
     def shard_copy(self, i):
         at = self.at
         device, mine = self.ways.owner(i)
-        return mine, remote(
-            self.buf.at[0, i], self.out.at[at.seq], self.sent.at[i], self.got.at[at.seq], device
-        )
+        src = self.tree.total(i // self.size).at[i % self.size]
+        return mine, remote(src, self.out.at[at.seq], self.sent.at[i], self.got.at[at.seq], device)
 
     def back(self, i):
-        return pltpu.make_async_copy(self.buf.at[0, i], self.out.at[self.at.seq], self.local.at[1])
-
-    def add(self):
-        at = self.at
-        self.keep().wait()
-        for mask in range(1, at.dp):
-            self.dp_copy(mask).wait_recv()
+        src = self.tree.total(i // self.size).at[i % self.size]
+        return pltpu.make_async_copy(src, self.out.at[self.at.seq], self.local)
+
+    def spread(self):
         for i in range(self.ways.each):
-            total = self.buf[0, i].astype(F32)
-            for mask in range(1, at.dp):
-                total = total + self.buf[mask, i].astype(F32)
-            self.buf[0, i] = total.astype(BF16)
             mine, copy = self.shard_copy(i)
             pl.when(jnp.logical_not(mine))(copy.start)
             pl.when(mine)(lambda: self.back(i).start())
 
     def finish(self):
         at = self.at
-        for mask in range(1, at.dp):
-            self.dp_copy(mask).wait_send()
+        self.tree.finish()
         for i in range(self.ways.each):
             mine, copy = self.shard_copy(i)
             pl.when(jnp.logical_not(mine))(copy.wait_send)
@@ -630,50 +681,88 @@
 
 class SmallReduce:
     @staticmethod
-    def scratch(dp, sp, seqs, shape):
-        return [pltpu.VMEM((dp,) + shape, F32), dma(2, dp), dma(2, sp)]
-
-    def __init__(self, place, x, out, buf, dp_sems, sp_sems):
-        self.at, self.x, self.out, self.buf = place, x, out, buf
-        self.dp_sems, self.sp_sems = dp_sems, sp_sems
-
-    def dp_copy(self, mask):
-        at = self.at
+    def scratch(dp, sp, seqs, own, common):
+        return [
+            pltpu.VMEM((dp,) + own, F32), pltpu.VMEM((dp,) + common, F32),
+            pltpu.VMEM((seqs,) + own, F32), pltpu.VMEM((sp,) + common, F32),
+            dma(4, dp), dma(2, sp), dma(2, seqs),
+        ]
+
+    def __init__(self, place, own, common, own_buf, common_buf, out_own, out_common, dp_sems, sp_sems, own_sems):
+        self.at = place
+        self.parts = ((own, own_buf), (common, common_buf))
+        self.out_own, self.out_common = out_own, out_common
+        self.dp_sems, self.sp_sems, self.own_sems = dp_sems, sp_sems, own_sems
+
+    def dp_copy(self, which, mask):
+        at = self.at
+        x, buf = self.parts[which]
         return remote(
-            self.x, self.buf.at[mask], self.dp_sems.at[0, mask], self.dp_sems.at[1, mask],
+            x, buf.at[mask], self.dp_sems.at[2 * which, mask], self.dp_sems.at[2 * which + 1, mask],
             at.along_dp(at.masked(mask)),
         )
 
-    def sp_copy(self, i):
+    def own_copy(self, i):
+        at = self.at
+        target = at.group * at.seqs + i
+        return target == at.s, remote(
+            self.parts[0][1].at[0], self.out_own.at[at.seq], self.own_sems.at[0, i],
+            self.own_sems.at[1, at.seq], at.along_sp(target),
+        )
+
+    def common_copy(self, i):
         at = self.at
         return remote(
-            self.buf.at[0], self.out.at[at.s], self.sp_sems.at[0, i], self.sp_sems.at[1, i],
-            at.along_sp(at.sp_peer(i)),
+            self.parts[1][1].at[0], self.out_common.at[at.s], self.sp_sems.at[0, i],
+            self.sp_sems.at[1, at.s], at.along_sp(at.sp_peer(i)),
         )
 
     def start(self):
-        for mask in range(1, self.at.dp):
-            self.dp_copy(mask).start()
+        for which in range(2):
+            for mask in range(1, self.at.dp):
+                self.dp_copy(which, mask).start()
 
     def add(self):
         at = self.at
-        total = self.x[...]
-        for mask in range(1, at.dp):
-            self.dp_copy(mask).wait_recv()
-            total = total + self.buf[mask]
-        self.buf[0] = total
-        self.out[at.s] = total
+        for which in range(2):
+            x, buf = self.parts[which]
+            total = x[...]
+            for mask in range(1, at.dp):
+                self.dp_copy(which, mask).wait_recv()
+                total = total + buf[mask]
+            buf[0] = total
+        for i in range(at.seqs):
+            mine, copy = self.own_copy(i)
+            pl.when(jnp.logical_not(mine))(copy.start)
+
+            @pl.when(mine)
+            def _():
+                self.out_own[at.seq] = self.parts[0][1][0]
+
+        self.out_common[at.s] = self.parts[1][1][0]
         for i in range(1, at.sp):
-            self.sp_copy(i).start()
+            self.common_copy(i).start()
 
     def finish(self):
         at = self.at
-        for mask in range(1, at.dp):
-            self.dp_copy(mask).wait_send()
+        for which in range(2):
+            for mask in range(1, at.dp):
+                self.dp_copy(which, mask).wait_send()
+        for i in range(at.seqs):
+            mine, copy = self.own_copy(i)
+            pl.when(jnp.logical_not(mine))(copy.wait_send)
+            sender = i * at.groups + at.s // at.seqs
+
+            @pl.when(sender != at.s)
+            def _():
+                dst = self.out_own.at[i]
+                remote(dst, dst, self.own_sems.at[0, 0], self.own_sems.at[1, i], at.along_sp(at.s)).wait_recv()
+
         for i in range(1, at.sp):
-            dst = self.out.at[lax.rem(at.s + at.sp - i, at.sp)]
-            remote(dst, dst, self.sp_sems.at[0, i], self.sp_sems.at[1, i], at.along_sp(at.s)).wait_recv()
-            self.sp_copy(i).wait_send()
+            slot = at.sp_peer(i)
+            dst = self.out_common.at[slot]
+            remote(dst, dst, self.sp_sems.at[0, 0], self.sp_sems.at[1, slot], at.along_sp(at.s)).wait_recv()
+            self.common_copy(i).wait_send()
 
 
 def comm_params(number):
@@ -794,8 +883,11 @@
 
         self.tree.start(odd)
 
-    def forward(self, odd):
-        self.tree.forward(odd)
+    def forward(self):
+        self.tree.forward()
+
+    def complete(self):
+        self.tree.complete()
 
     def finish(self):
         for i in range(1, self.at.sp):
@@ -871,52 +963,69 @@
             self.chip_copy(i).wait_send()
 
 
-def first_kernel(dp, sp, seqs, chans, w_ref, misc_ref, hid_ref, wx_out, misc_out, hid_out, *sems):
+def first_kernel(
+    dp, sp, seqs, chans, w_ref, misc_ref, hid_ref, o_ref, wx_out, misc_out, hid_out, o_out, *sems
+):
     place = Place(dp, sp, seqs)
     inner = w_ref.shape[1] // 2
     columns = lambda g: w_ref.at[:, pl.ds(pl.multiple_of(inner + g * chans, LANES), chans)]
-    wx = ColumnGather(place, columns, wx_out, *sems[:4])
-    misc = CommonGather(place, misc_ref, misc_out, *sems[4:7])
-    hid = BlockGather(place, hid_ref, hid_out, *sems[7:])
-    place.meet()
+    rest = list(sems)
+
+    def take(scratch):
+        taken = rest[: len(scratch)]
+        del rest[: len(scratch)]
+        return taken
+
+    wx = ColumnGather(place, columns, wx_out, *take(ColumnGather.scratch(dp, sp, seqs)))
+    misc = CommonGather(place, misc_ref, misc_out, *take(CommonGather.scratch(dp, sp, seqs)))
+    hid = BlockGather(place, hid_ref, hid_out, *take(BlockGather.scratch(dp, sp, seqs)))
+    out = OutGather(place, o_ref, o_out, *take(OutGather.scratch(dp, sp, seqs)))
+    place.meet(more=out.ways.meet(True))
     misc.start()
     wx.start()
+    out.start()
     hid.start()
     misc.along_dp()
-    wx.along_dp(0)
-    wx.along_dp(1)
+    for odd in range(2):
+        wx.along_dp(odd)
+    for odd in range(2):
+        out.along_dp(odd)
     misc.cross()
     hid.arrive(0)
-    hid.arrive(1)
-    wx.forward(0)
-    wx.forward(1)
-    for i in range(2, place.chips):
+    wx.forward()
+    out.forward()
+    for i in range(1, place.chips):
         hid.arrive(i)
     for i in range(place.chips):
         hid.arrive_other(i)
+    wx.complete()
+    out.complete()
     misc.finish()
     wx.finish()
     hid.finish()
-
-
-def run_first(dp, sp, seqs, chans, w_zx, misc, hidden):
+    out.finish()
+
+
+def run_first(dp, sp, seqs, chans, w_zx, misc, hidden, w_out):
     share = w_zx.shape[0]
     _, rows, cols = hidden.shape
     return pl.pallas_call(
         functools.partial(first_kernel, dp, sp, seqs, chans),
-        in_specs=[ANY] * 3,
-        out_specs=[ANY] * 3,
+        in_specs=[ANY] * 4,
+        out_specs=[ANY] * 4,
         out_shape=[
             jax.ShapeDtypeStruct((dp, sp, share, chans), BF16),
             jax.ShapeDtypeStruct((2, dp, sp // 2) + misc.shape, BF16),
             jax.ShapeDtypeStruct((sp, rows, cols), BF16),
+            jax.ShapeDtypeStruct((sp,) + w_out.shape, BF16),
         ],
         scratch_shapes=ColumnGather.scratch(dp, sp, seqs)
         + CommonGather.scratch(dp, sp, seqs)
-        + BlockGather.scratch(dp, sp, seqs),
+        + BlockGather.scratch(dp, sp, seqs)
+        + OutGather.scratch(dp, sp, seqs),
         compiler_params=comm_params(1),
         name="first_gather",
-    )(w_zx, misc, hidden)
+    )(w_zx, misc, hidden, w_out)
 
 
 def scan_block(wide, chans, x, bd, taps, heads, skip, mixed, enter, ext, halo, state):
@@ -966,55 +1075,45 @@
 
 def forward_kernel(
     dp, sp, seqs, wide, inner,
-    w_ref, o_ref, cot_ref, hid_ref, wx_ref, wb_ref, norm, taps, heads, skip, gain,
-    wg_out, o_out, cot_out, normed_out, x_out, bd_out, enter_out, gated_out, dgate_out, dy_out,
-    hid, wx, wb, wg, rows_out, cot, normed, x, bd, mixed, enter, gate, d_gated, gated, dgate, dy,
-    ext, halo, state, sums, got, saves, sum_sems, *sems,
+    w_ref, cot_ref, hid_ref, wx_ref, wb_ref, o_ref, norm, taps, heads, skip, gain,
+    wg_out, normed_out, x_out, bd_out, enter_out, dgate_out, dy_out, part_out, tg_out, to_out,
+    hid, wx, wb, rows_out, wg, cot, normed, x, bd, mixed, enter, gate, d_gated, gated, dgate, dy,
+    part, tg, to, ext, halo, state, sums, got, saves, sum_sems, *sems,
 ):
     place = Place(dp, sp, seqs)
     chans = wx.shape[1]
     blocks, rows, width = hid.shape
     columns = lambda g: w_ref.at[:, pl.ds(pl.multiple_of(g * chans, LANES), chans)]
-    wg_comm = ColumnGather(place, columns, wg, *sems[:4])
-    out_comm = OutGather(place, o_ref, rows_out, *sems[4:9])
-    cot_comm = BlockGather(place, cot_ref, cot, *sems[9:])
+    wg_comm = ColumnGather(place, columns, wg, *sems[:-1])
+    cot_comm = BlockGather(place, cot_ref, cot, sems[-1])
     loads = [
         pltpu.make_async_copy(src, dst, saves.at[7, i])
-        for i, (src, dst) in enumerate(((hid_ref, hid), (wx_ref, wx), (wb_ref, wb)))
+        for i, (src, dst) in enumerate(
+            ((hid_ref, hid), (wx_ref, wx), (wb_ref, wb), (o_ref, rows_out))
+        )
     ]
     for load in loads:
         load.start()
-    place.meet(more=out_comm.ways.meet(True))
-    out_comm.start()
+    place.meet()
     wg_comm.start()
     cot_comm.start()
     halo[...] = jnp.zeros(halo.shape, F32)
     state[...] = jnp.zeros(state.shape, F32)
     sums[...] = jnp.zeros(sums.shape, F32)
-    for load in loads:
+    for load in loads[:3]:
         load.wait()
 
     def save(src, dst, index, b):
         return pltpu.make_async_copy(src.at[b], dst.at[b], saves.at[index, b])
 
     early = ((normed, normed_out), (x, x_out), (bd, bd_out), (enter, enter_out))
-    late = ((gated, gated_out), (dgate, dgate_out), (dy, dy_out))
+    late = ((dgate, dgate_out), (dy, dy_out), (part, part_out))
 
     def first(b, carry):
-        @pl.when(b == blocks // 2 - 1)
-        def _():
-            for odd in range(2):
-                out_comm.along_dp(odd)
-
-        @pl.when(b == blocks // 2)
+        @pl.when(b == blocks - 3)
         def _():
             for odd in range(2):
                 wg_comm.along_dp(odd)
-
-        @pl.when(b == blocks - 1)
-        def _():
-            for odd in range(2):
-                out_comm.forward(odd)
 
         hidden = hid[b].astype(F32)
         scale = lax.rsqrt(jnp.mean(hidden * hidden, axis=-1, keepdims=True) + EPS)
@@ -1029,8 +1128,9 @@
         return carry
 
     lax.fori_loop(0, blocks, first, 0)
-    wg_comm.forward(0)
-    wg_comm.forward(1)
+    wg_comm.forward()
+    wg_comm.complete()
+    loads[3].wait()
     lane = iota((rows, LANES), 1)
 
     def gates(b):
@@ -1069,11 +1169,8 @@
     ]
     for copy in copies:
         copy.start()
-    keep_cot = pltpu.make_async_copy(cot, cot_out, saves.at[7, 0])
-    keep_wg = pltpu.make_async_copy(wg, wg_out, saves.at[7, 1])
-    keep_out = pltpu.make_async_copy(rows_out, o_out, saves.at[7, 2])
-    for keep in (keep_cot, keep_wg, keep_out):
-        keep.start()
+    keep_wg = pltpu.make_async_copy(wg, wg_out, saves.at[7, 0])
+    keep_wg.start()
     total = sums[...]
     for i, copy in enumerate(copies):
         copy.wait_recv()
@@ -1095,32 +1192,52 @@
         back = scale * (d_gated[b] * gain[0:1, :] - unit * mean)
         dy[b] = (back * silu).astype(BF16)
         dgate[b] = (back * mix * sig * (1.0 + gate_f * (1.0 - sig))).astype(BF16)
+        part[b] = dot(gated[b], rows_out[...].reshape(chans, width)).astype(BF16)
         for index, (src, dst) in enumerate(late):
             save(src, dst, 4 + index, b).start()
         return carry
 
     lax.fori_loop(0, blocks, third, 0)
+    everything = blocks * rows
+    tile = width // dp
+    keep_tg, keep_to = [], []
+    for p in range(dp):
+        columns = normed[:, :, p * tile : (p + 1) * tile].reshape(everything, tile)
+        value = dot(columns, dgate[...].reshape(everything, chans), ((0,), (0,)))
+        tg[p] = value.astype(BF16).reshape(tg.shape[1:])
+        keep_tg.append(pltpu.make_async_copy(tg.at[p], tg_out.at[p], saves.at[7, 1 + p]))
+        keep_tg[-1].start()
+    slots = sp // 2
+    for half in range(2):
+        size = chans // 2
+        columns = gated[:, :, half * size : (half + 1) * size].reshape(everything, size)
+        value = dot(columns, cot[...].reshape(everything, width), ((0,), (0,)))
+        span = pl.ds(half * slots, slots)
+        to[span] = value.astype(BF16).reshape((slots,) + to.shape[1:])
+        keep_to.append(
+            pltpu.make_async_copy(to.at[span], to_out.at[span], saves.at[8, half])
+        )
+        keep_to[-1].start()
     for copy in copies:
         copy.wait_send()
     cot_comm.finish()
-    out_comm.finish()
     wg_comm.finish()
-    for keep in (keep_cot, keep_wg, keep_out):
+    for keep in [keep_wg] + keep_tg + keep_to:
         keep.wait()
     for index, (src, dst) in enumerate(early + late):
         for b in range(blocks):
             save(src, dst, index, b).wait()
 
 
-def run_middle(dp, sp, seqs, wide, inner, w_zx, w_out, cotangent, hidden, wx, wb, norm, taps, heads, skip, gain):
+def run_middle(dp, sp, seqs, wide, inner, w_zx, cotangent, hidden, wx, wb, w_rows, norm, taps, heads, skip, gain):
     share = w_zx.shape[0]
     blocks, rows, width = hidden.shape
     chans, cols = wx.shape[1], wb.shape[1]
     states = wide // 2
     shapes = [
-        (dp, sp, share, chans), (sp,) + w_out.shape, hidden.shape, hidden.shape,
-        (blocks, rows, chans), (blocks, rows, cols), (blocks, states, chans),
-        (blocks, rows, chans), (blocks, rows, chans), (blocks, rows, chans),
+        (dp, sp, share, chans), hidden.shape, (blocks, rows, chans), (blocks, rows, cols),
+        (blocks, states, chans), (blocks, rows, chans), (blocks, rows, chans), hidden.shape,
+        (dp, sp, share, chans), w_rows.shape,
     ]
     block = lambda n, kind: pltpu.VMEM((blocks, rows, n), kind)
     vmem = pl.BlockSpec(memory_space=pltpu.VMEM)
@@ -1133,36 +1250,37 @@
             pltpu.VMEM(hidden.shape, BF16),
             pltpu.VMEM(wx.shape, BF16),
             pltpu.VMEM(wb.shape, BF16),
+            pltpu.VMEM(w_rows.shape, BF16),
             pltpu.VMEM(shapes[0], BF16),
-            pltpu.VMEM(shapes[1], BF16),
-            pltpu.VMEM(shapes[2], BF16),
+            pltpu.VMEM(hidden.shape, BF16),
             block(width, BF16), block(chans, BF16), block(cols, BF16), block(chans, BF16),
-            pltpu.VMEM(shapes[6], BF16),
+            pltpu.VMEM(shapes[4], BF16),
             block(chans, BF16), block(chans, F32), block(chans, BF16), block(chans, BF16),
-            block(chans, BF16),
+            block(chans, BF16), block(width, BF16),
+            pltpu.VMEM(shapes[0], BF16),
+            pltpu.VMEM(w_rows.shape, BF16),
             pltpu.VMEM((rows + 8, chans + wide), F32),
             pltpu.VMEM((8, chans + wide), F32),
             pltpu.VMEM((states, chans), F32),
             pltpu.VMEM((rows, LANES), F32),
             pltpu.VMEM((sp // seqs, rows, LANES), F32),
-            dma(8, max(blocks, 3)),
+            dma(9, max(blocks, dp + 1, 4)),
             dma(2, sp // seqs),
         ]
         + ColumnGather.scratch(dp, sp, seqs)
-        + OutGather.scratch(dp, sp, seqs)
         + BlockGather.scratch(dp, sp, seqs),
         compiler_params=comm_params(2),
         name="forward",
-    )(w_zx, w_out, cotangent, hidden, wx, wb, norm, taps, heads, skip, gain)
+    )(w_zx, cotangent, hidden, wx, wb, w_rows, norm, taps, heads, skip, gain)
 
 
 def backward_kernel(
     dp, sp, seqs, wide, chans,
-    dy, x, x_before, bd, bd_before, dgate, enter, taps, heads, skip, wg, wx, wb,
-    normed_ref, out_part, terms_out, terms_gate,
-    out_total, dn_total, og, ox, ob, oo, osmall,
-    ext, gext, halo, dstate, dtaps, dheads, dskip, dx, dbd, normed, part, loads,
-    tx, tb, small, landed, *scratch,
+    dy, x, x_before, bd, bd_before, dgate, enter, taps, heads, skip, norm, wg, wx, wb,
+    normed_ref, out_part, terms_out, terms_gate, hid_ref, cot_ref, w_zx_ref, w_bc_ref, w_out_ref,
+    hidden_out, grad_hidden, grad_zx, grad_bc, grad_dt, norm_sum, grad_out, gate_sum, own_small, common_small,
+    ext, gext, halo, dstate, dtaps, dheads, dskip, dx, dbd, normed, part,
+    hid, cot, w_zx, w_bc, w_out, loads, tb, og, ob, oo, own, *scratch,
 ):
     step, steps = pl.program_id(0), pl.num_programs(0)
     chunk = steps - 1 - step
@@ -1178,21 +1296,33 @@
 
     out_red = BlockReduce(place, out_part, *take(6))
     dn_red = BlockReduce(place, part, None, *take(5))
-    gate_red = ShardReduce(place, terms_gate, og, *take(4))
-    x_red = ShardReduce(place, tx, ox, *take(4))
-    b_red = ShardReduce(place, tb, ob, *take(4))
-    out_grads = OutReduce(place, terms_out, oo, *take(5))
-    few = SmallReduce(place, small, landed, *take(3))
-    load = pltpu.make_async_copy(normed_ref, normed, loads.at[0])
+    gate_red = ShardReduce(place, terms_gate, og, True, *take(5))
+    b_red = ShardReduce(place, tb, ob, False, *take(4))
+    out_grads = OutReduce(place, terms_out, oo, *take(6))
+    few = SmallReduce(place, own, dtaps.at[:, pl.ds(chans, wide)], *take(7))
+    x_reds, x_parts = [], []
+    while rest:
+        tx, landed = take(2)
+        x_reds.append((tx, ShardReduce(place, tx, landed, False, *take(4))))
+        x_parts.append(landed)
+    last_loads = [
+        pltpu.make_async_copy(src, dst, loads.at[i])
+        for i, (src, dst) in enumerate(
+            (
+                (normed_ref, normed), (hid_ref, hid), (cot_ref, cot), (w_zx_ref, w_zx),
+                (w_bc_ref, w_bc), (w_out_ref, w_out),
+            )
+        )
+    ]
 
     @pl.when(step == 0)
     def _():
         place.meet(more=out_grads.ways.meet(False))
         for k in range(chips):
             out_red.start(k)
-        gate_red.start()
-        out_grads.start()
-        load.start()
+        gate_red.tree.start()
+        for load in last_loads:
+            load.start()
 
     scan_backward(
         wide, chans, dy, x, x_before, bd, bd_before, taps, heads, skip, enter,
@@ -1214,13 +1344,25 @@
 
     for i in range(chips - 1, -1, -1):
 
-        @pl.when(step == steps - 1 - max(i, 0) * (steps - 3) // chips)
+        @pl.when(step == steps - 1 - i * (steps - 3) // chips)
         def _():
             if i:
                 both_ways(i, out_red.settle)
             else:
                 out_red.settle(place.chip)
 
+    levels = len(place.bits)
+
+    def at_step(when, fn):
+        pl.when(step == min(when, steps - 1))(fn)
+
+    at_step(1, out_grads.tree.start)
+    for i in range(levels):
+        at_step(3 + 2 * i, functools.partial(gate_red.tree.step, i))
+        at_step(5 + i, functools.partial(out_grads.tree.step, i))
+    at_step(1 + 2 * levels, gate_red.spread)
+    at_step(4 + levels, out_grads.spread)
+
     @pl.when(lax.rem(step, 2) == 1)
     def _():
         dn_red.start(chunk // 2)
@@ -1237,113 +1379,165 @@
 
     @pl.when(step == steps - 1)
     def _():
+        for load in last_loads:
+            load.wait()
+        rows_all = blocks * rows
+        share_rows = tb.shape[1] * tb.shape[2]
+        size = chans // len(x_reds)
+        own[:, :chans] = dtaps[:, :chans]
+        own[5:6, :chans] = dskip[0:1, :]
+        own[:, chans:] = dheads[...]
+        few.start()
+
+        def terms(red, out, values):
+            for p in range(dp):
+                columns = normed[:, :, p * share_rows : (p + 1) * share_rows]
+                value = dot(columns.reshape(rows_all, share_rows), values, ((0,), (0,)))
+                out[p] = value.astype(BF16).reshape(out.shape[1:])
+            red.tree.start()
+
+        for n, (tx, red) in enumerate(x_reds):
+            terms(red, tx, dx[:, :, n * size : (n + 1) * size].reshape(rows_all, size))
         dn_red.collect(jnp.int32(0))
-        load.wait()
-        share_rows = tx.shape[1] * tx.shape[2]
-        rows_all = blocks * rows
-        small[:, : chans + wide] = dtaps[...]
-        small[5:6, :chans] = dskip[0:1, :]
-        small[:, chans + wide :] = dheads[...]
-        few.start()
-        turned = dx[...].reshape(rows_all, -1)
-        turned_b = dbd[...].reshape(rows_all, -1)
-        for mask in list(range(1, dp)) + [0]:
-            other = place.masked(mask)
-            first = pl.multiple_of(other * share_rows, LANES)
-            columns = normed[:, :, pl.ds(first, share_rows)].reshape(rows_all, share_rows)
-            for red, values in ((x_red, turned), (b_red, turned_b)):
-                value = dot(columns, values, ((0,), (0,))).astype(BF16)
-                value = value.reshape(red.terms.shape[1:])
-                if mask:
-                    red.terms[other] = value
-                    red.dp_copy(mask).start()
-                else:
-                    red.buf[0] = value
-        gate_red.add()
-        out_grads.add()
-        for k in range(chips - 1 - (steps - 1 - wait) // 2 - 1, -1, -1):
+        terms(b_red, tb, dbd[...].reshape(rows_all, -1))
+        for k in range(chips - 1 - (steps - 1 - wait) // 2 - 1, 0, -1):
             dn_red.settle(jnp.int32(k))
         few.add()
-        x_red.add(kept=False)
-        b_red.add(kept=False)
+        late = [red for _, red in x_reds] + [b_red]
+        for i in range(levels):
+            for red in late:
+                red.tree.step(i)
+                if i == levels - 1:
+                    red.spread()
+            if i == 0:
+                dn_red.settle(jnp.int32(0))
         out_red.finish()
-        out_total[...] = out_red.total[...]
+        hidden_out[...] = (hid[...].astype(F32) + out_red.total[...].astype(F32)).astype(BF16)
+        out_grads.finish()
+        value = oo[0].astype(F32)
+        for seq in range(1, seqs):
+            value = value + oo[seq].astype(F32)
+        grad_out[...] = value
+        gate_sum[...] = jnp.broadcast_to(
+            jnp.sum(value * w_out[...].astype(F32), axis=1, keepdims=True), gate_sum.shape
+        )
+        gate_red.finish()
+        by_seq = lambda ref, g: functools.reduce(
+            jnp.add, [ref[seq * place.groups + g].astype(F32) for seq in range(seqs)]
+        )
+        inner = grad_zx.shape[1] // 2
+        norm_total = jnp.zeros((grad_zx.shape[0], 1), F32)
+
+        def write(first, value):
+            lanes = slice(first, first + value.shape[1])
+            grad_zx[:, lanes] = value
+            return jnp.sum(value * w_zx[:, lanes].astype(F32), axis=1, keepdims=True)
+
+        for g in range(place.groups):
+            norm_total = norm_total + write(g * chans, by_seq(og, g))
         dn_red.finish()
-        dn_total[...] = dn_red.total[...]
-        gate_red.finish()
-        out_grads.finish()
+        for seq in range(seqs):
+            value = hid[seq].astype(F32)
+            scale = lax.rsqrt(jnp.mean(value * value, axis=-1, keepdims=True) + EPS)
+            unit = value * scale
+            weighted = dn_red.total[seq].astype(F32) * norm[0:1, :]
+            weighted = weighted - unit * jnp.mean(weighted * unit, axis=-1, keepdims=True)
+            grad_hidden[seq] = (cot[seq].astype(F32) + scale * weighted).astype(BF16)
         few.finish()
-        osmall[...] = landed[...]
-        x_red.finish()
+        own_small[...] = functools.reduce(jnp.add, [few.out_own[seq] for seq in range(seqs)])
+        common_small[...] = functools.reduce(jnp.add, [few.out_common[slot] for slot in range(sp)])
+        for n, landed in enumerate(x_parts):
+            x_reds[n][1].finish()
+            for g in range(place.groups):
+                norm_total = norm_total + write(inner + g * chans + n * size, by_seq(landed, g))
         b_red.finish()
+        value = functools.reduce(jnp.add, [ob[slot, :, :wide].astype(F32) for slot in range(sp)])
+        grad_bc[...] = value
+        norm_total = norm_total + jnp.sum(value * w_bc[...].astype(F32), axis=1, keepdims=True)
+        norm_sum[...] = jnp.broadcast_to(norm_total, norm_sum.shape)
+        for g in range(place.groups):
+            grad_dt[g] = functools.reduce(
+                jnp.add,
+                [ob[seq * place.groups + g, :, wide:].astype(F32) for seq in range(seqs)],
+            )
 
 
 def run_backward(
-    dp, sp, seqs, dy, x, bd, dgate, enter, taps, heads, skip, wg, wx, wb,
-    normed, out_part, terms_out, terms_gate, wide,
+    dp, sp, seqs, dy, x, bd, dgate, enter, taps, heads, skip, norm, wg, wx, wb,
+    normed, out_part, terms_out, terms_gate, hidden, cotangent, w_zx, w_bc, w_out, wide,
 ):
     blocks, rows, chans = x.shape
     states = wide // 2
     cols, width = bd.shape[2], normed.shape[2]
     share = terms_gate.shape[2]
+    groups = sp // seqs
+    pieces = 2 if chans % (2 * LANES) == 0 else 1
     back = lambda i: blocks - 1 - i
     block = lambda n: pl.BlockSpec((None, rows, n), lambda i: (back(i), 0, 0))
     whole = lambda a: pl.BlockSpec(a.shape, lambda i: (0,) * a.ndim)
     before = lambda n: pl.BlockSpec(
         (None, 16, n), lambda i: (jnp.maximum(back(i) - 1, 0), rows // 16 - 1, 0)
     )
-    fixed = lambda *shape: pl.BlockSpec(shape, lambda i: (0,) * len(shape))
-    tokens = (seqs, rows, width)
-    small = (8, chans + wide + LANES)
-    reduce = lambda n: ShardReduce.scratch(dp, sp, (share, n))
+    outs = [
+        jax.ShapeDtypeStruct(hidden.shape, BF16),
+        jax.ShapeDtypeStruct(hidden.shape, BF16),
+        jax.ShapeDtypeStruct(w_zx.shape, F32),
+        jax.ShapeDtypeStruct(w_bc.shape, F32),
+        jax.ShapeDtypeStruct((groups, share, LANES), F32),
+        jax.ShapeDtypeStruct((share, LANES), F32),
+        jax.ShapeDtypeStruct(w_out.shape, F32),
+        jax.ShapeDtypeStruct((w_out.shape[0], LANES), F32),
+        jax.ShapeDtypeStruct((8, chans + LANES), F32),
+        jax.ShapeDtypeStruct((8, wide), F32),
+    ]
+    vmem = lambda a: pltpu.VMEM(a.shape, a.dtype)
+    scratch = [
+        pltpu.VMEM((rows + 8, chans + wide), F32),
+        pltpu.VMEM((rows + 8, chans + wide), F32),
+        pltpu.VMEM((8, chans + wide), F32),
+        pltpu.VMEM((states, chans), F32),
+        pltpu.VMEM((8, chans + wide), F32),
+        pltpu.VMEM((8, LANES), F32),
+        pltpu.VMEM((8, chans), F32),
+        pltpu.VMEM((blocks, rows, chans), BF16),
+        pltpu.VMEM((blocks, rows, cols), BF16),
+        vmem(normed),
+        pltpu.VMEM((blocks, rows, width), BF16),
+        vmem(hidden), vmem(cotangent), vmem(w_zx), vmem(w_bc), vmem(w_out),
+        dma(6),
+        pltpu.VMEM((dp, sp, share, cols), BF16),
+        pltpu.VMEM((sp, share, chans), BF16),
+        pltpu.VMEM((sp, share, cols), BF16),
+        pltpu.VMEM((seqs,) + w_out.shape, BF16),
+        pltpu.VMEM((8, chans + LANES), F32),
+    ]
+    scratch += BlockReduce.scratch(dp, sp, seqs, rows, width, True)
+    scratch += BlockReduce.scratch(dp, sp, seqs, rows, width, False)
+    scratch += ShardReduce.scratch(dp, sp, (share, chans), True)
+    scratch += ShardReduce.scratch(dp, sp, (share, cols), False)
+    scratch += OutReduce.scratch(dp, sp, seqs, w_out.shape)
+    scratch += SmallReduce.scratch(dp, sp, seqs, (8, chans + LANES), (8, wide))
+    for _ in range(pieces):
+        shape = (share, chans // pieces)
+        scratch += [pltpu.VMEM((dp, sp) + shape, BF16), pltpu.VMEM((sp,) + shape, BF16)]
+        scratch += ShardReduce.scratch(dp, sp, shape, False)
     return pl.pallas_call(
         functools.partial(backward_kernel, dp, sp, seqs, wide, chans),
         grid=(blocks,),
         in_specs=[
             block(chans), block(chans), before(chans), block(cols), before(cols), block(chans),
             pl.BlockSpec((None, states, chans), lambda i: (back(i), 0, 0)),
-            whole(taps), whole(heads), whole(skip), whole(wg), whole(wx), whole(wb),
+            whole(taps), whole(heads), whole(skip), whole(norm), whole(wg), whole(wx), whole(wb),
         ]
-        + [ANY] * 4,
-        out_specs=[fixed(*tokens), fixed(*tokens)] + [ANY] * 3
-        + [ANY, fixed(sp, *small)],
-        out_shape=[
-            jax.ShapeDtypeStruct(tokens, BF16),
-            jax.ShapeDtypeStruct(tokens, BF16),
-            jax.ShapeDtypeStruct((sp, share, chans), BF16),
-            jax.ShapeDtypeStruct((sp, share, chans), BF16),
-            jax.ShapeDtypeStruct((sp, share, cols), BF16),
-            jax.ShapeDtypeStruct((seqs,) + terms_out.shape[1:], BF16),
-            jax.ShapeDtypeStruct((sp,) + small, F32),
-        ],
-        scratch_shapes=[
-            pltpu.VMEM((rows + 8, chans + wide), F32),
-            pltpu.VMEM((rows + 8, chans + wide), F32),
-            pltpu.VMEM((8, chans + wide), F32),
-            pltpu.VMEM((states, chans), F32),
-            pltpu.VMEM((8, chans + wide), F32),
-            pltpu.VMEM((8, LANES), F32),
-            pltpu.VMEM((8, chans), F32),
-            pltpu.VMEM((blocks, rows, chans), BF16),
-            pltpu.VMEM((blocks, rows, cols), BF16),
-            pltpu.VMEM(normed.shape, BF16),
-            pltpu.VMEM((blocks, rows, width), BF16),
-            dma(1),
-            pltpu.VMEM((dp, sp, share, chans), BF16),
-            pltpu.VMEM((dp, sp, share, cols), BF16),
-            pltpu.VMEM(small, F32),
-            pltpu.VMEM((sp,) + small, F32),
-        ]
-        + BlockReduce.scratch(dp, sp, seqs, rows, width, True)
-        + BlockReduce.scratch(dp, sp, seqs, rows, width, False)
-        + reduce(chans) + reduce(chans) + reduce(cols)
-        + OutReduce.scratch(dp, sp, seqs, terms_out.shape[1:])
-        + SmallReduce.scratch(dp, sp, seqs, small),
+        + [ANY] * 9,
+        out_specs=[whole(out) for out in outs],
+        out_shape=outs,
+        scratch_shapes=scratch,
         compiler_params=comm_params(4),
         name="backward",
     )(
-        dy, x, x, bd, bd, dgate, enter, taps, heads, skip, wg, wx, wb,
-        normed, out_part, terms_out, terms_gate,
+        dy, x, x, bd, bd, dgate, enter, taps, heads, skip, norm, wg, wx, wb,
+        normed, out_part, terms_out, terms_gate, hidden, cotangent, w_zx, w_bc, w_out,
     )
 
 
@@ -1365,7 +1559,6 @@
     seqs, block, width = hidden_in.shape
     groups = sp // seqs
     group = lax.rem(me_sp, groups)
-    rows = sp * block
     wide, heads = w_bc.shape[1], w_dt.shape[1]
     share, taps_n = w_zx.shape[0], conv_x_weight.shape[1]
     inner = heads * P_SIZE
@@ -1392,7 +1585,7 @@
     misc = jnp.concatenate(
         [tall(w_bc), tall(w_dt), pad_last(small, high * spare).reshape(high, spare)], axis=1
     )
-    wx, misc_all, hidden_all = run_first(dp, sp, seqs, chans, w_zx, misc, hidden_in)
+    wx, misc_all, hidden_all, w_rows = run_first(dp, sp, seqs, chans, w_zx, misc, hidden_in, w_out)
     misc_all = jnp.transpose(misc_all, (1, 2, 0, 3, 4)).reshape((dp, sp) + misc.shape)
 
     wx = wx.reshape(width, chans)
@@ -1420,56 +1613,29 @@
     skip = eight_rows(jnp.repeat(mine(6).reshape(own_heads), P_SIZE))
     gain = eight_rows(gate_mine)
 
-    wg, out_mine, cot_all, normed, x_blocks, bd_blocks, entering, gated, dgate, dy = run_middle(
-        dp, sp, seqs, wide, inner, w_zx, w_out, cotangent, hidden_all, wx, wb,
-        eight_rows(norm_all), taps, head_rows, skip, gain,
+    norm = eight_rows(norm_all)
+    wg, normed, x_blocks, bd_blocks, entering, dgate, dy, out_part, terms_gate, terms_out = run_middle(
+        dp, sp, seqs, wide, inner, w_zx, cotangent, hidden_all, wx, wb, w_rows,
+        norm, taps, head_rows, skip, gain,
     )
-    normed, gated, cot_rows = (v.reshape(rows, -1) for v in (normed, gated, cot_all))
-    out_rows = out_mine.reshape(chans, width)
-    out_part = dot(gated, out_rows).astype(BF16).reshape(sp, block, width)
-    terms_out = dot(gated, cot_rows, ((0,), (0,))).astype(BF16).reshape(sp, gate_share, width)
-    terms_gate = dot(normed, dgate.reshape(rows, chans), ((0,), (0,))).astype(BF16)
-    out_sum, d_normed, og, ox, ob, oo, osmall = run_backward(
-        dp, sp, seqs, dy, x_blocks, bd_blocks, dgate, entering, taps, head_rows, skip,
-        wg.reshape(width, chans), wx, wb, normed.reshape(sp, block, width), out_part, terms_out,
-        terms_gate.reshape(dp, sp, share, chans), wide,
+    (hidden_out, grad_hidden, grad_w_zx, grad_w_bc, dt_parts, norm_sum, grad_w_out, gate_sum,
+     own_small, common_small) = run_backward(
+        dp, sp, seqs, dy, x_blocks, bd_blocks, dgate, entering, taps, head_rows, skip, norm,
+        wg.reshape(width, chans), wx, wb, normed, out_part, terms_out, terms_gate,
+        hidden_in, cotangent, w_zx, w_bc, w_out, wide,
     )
-    hidden_out = (hidden_in.astype(F32) + out_sum.astype(F32)).astype(BF16)
-    spread_cols = lambda v: jnp.transpose(
-        jnp.sum(v.astype(F32).reshape(seqs, groups, share, -1), axis=0), (1, 0, 2)
-    ).reshape(share, -1)
-    grad_w_zx = jnp.concatenate([spread_cols(og), spread_cols(ox)], axis=1)
-    ob = ob.astype(F32)
-    grad_w_bc = jnp.sum(ob[:, :, :wide], axis=0)
-    grad_w_dt = spread_cols(ob[:, :, wide : wide + own_heads])
+    grad_w_dt = jnp.transpose(dt_parts[:, :, :own_heads], (1, 0, 2)).reshape(share, heads)
     grad_norm_gain = (
-        jnp.sum(grad_w_zx * w_zx.astype(F32), axis=1)
-        + jnp.sum(grad_w_bc * w_bc.astype(F32), axis=1)
-        + jnp.sum(grad_w_dt * w_dt.astype(F32), axis=1)
+        norm_sum[:, 0] + jnp.sum(grad_w_dt * w_dt.astype(F32), axis=1)
     ) / norm_gain.astype(F32)
-    grad_w_out = jnp.sum(oo.astype(F32), axis=0)
-    grad_gate_gain = jnp.sum(grad_w_out * w_out.astype(F32), axis=1) / gate_gain.astype(F32)
-
-    hid = hidden_in.reshape(seqs * block, width).astype(F32)
-    scale_own = lax.rsqrt(jnp.mean(hid * hid, axis=-1, keepdims=True) + EPS)
-    unit_own = hid * scale_own
-    weighted = d_normed.reshape(seqs * block, width).astype(F32) * norm_all
-    grad_rows = cotangent.reshape(seqs * block, width).astype(F32) + scale_own * (
-        weighted - unit_own * jnp.mean(weighted * unit_own, axis=-1, keepdims=True)
-    )
-    grad_hidden = grad_rows.astype(BF16).reshape(hidden_in.shape)
-
-    by_group = jnp.sum(osmall.reshape(seqs, groups, 8, -1), axis=0)
-    from_group = lax.dynamic_index_in_dim(by_group, me_sp // seqs, axis=0, keepdims=False)
+    grad_gate_gain = gate_sum[:, 0] / gate_gain.astype(F32)
+
     part = lax.rem(me_sp, seqs)
-    g_x = lax.dynamic_slice_in_dim(from_group[:, :chans], part * x_share, x_share, axis=1)
-    g_heads = lax.dynamic_slice_in_dim(
-        from_group[:, chans + wide :], part * head_share, head_share, axis=1
-    )
+    g_x = lax.dynamic_slice_in_dim(own_small[:, :chans], part * x_share, x_share, axis=1)
+    g_heads = lax.dynamic_slice_in_dim(own_small[:, chans:], part * head_share, head_share, axis=1)
     g_skip = jnp.sum(g_x[5].reshape(head_share, P_SIZE), axis=1)
-    g_bc = jnp.sum(by_group[:, :, chans : chans + wide], axis=0)
     first = (me_dp * sp + me_sp) * bc_share
-    g_bc = lax.dynamic_slice_in_dim(g_bc, first, bc_share, axis=1)
+    g_bc = lax.dynamic_slice_in_dim(common_small, first, bc_share, axis=1)
     return (
         hidden_out,
         grad_hidden,

time: 379 us -> 324 us (0.85)
  Pallas kernels: 335 us -> 290 us
  matrix products: 14.5 us -> 0 us
  local copies, waits for them, and re-layouts: 15.3 us -> 23.6 us
  other arithmetic: 12.9 us -> 8.21 us
    pallas_call x1, Pallas kernels: 135 us -> 86.4 us  [run_middle(): pl.pallas_call(functools.partial(forward_kernel, dp, sp, seqs, wide, inne...]
    pallas_call x1, Pallas kernels: 56.3 us -> 76.1 us  [run_first(): pl.pallas_call(functools.partial(first_kernel, dp, sp, seqs, chans), in_s...]
    pallas_call x1, Pallas kernels: 143 us -> 128 us  [run_backward(): pl.pallas_call(functools.partial(backward_kernel, dp, sp, seqs, wide, cha...]
    dot_general x3 -> x0, matrix products: 14.5 us -> none  [dot(): lax.dot_general(left, right, (dims, ((), ())), precision=precision, prefe...]
where the time goes in v4:
time: 324 us; the launch traced here: 323 us
  Pallas kernels  290 us (90%)
  local copies, waits for them, and re-layouts  23.6 us (7%)
  other arithmetic  8.21 us (3%)
    pallas_call x1, Pallas kernels, run_backward(): pl.pallas_call(functools.partial(backward_kernel, dp, sp, seqs, wide, cha...  128 us
    pallas_call x1, Pallas kernels, run_middle(): pl.pallas_call(functools.partial(forward_kernel, dp, sp, seqs, wide, inne...  86.4 us
    pallas_call x1, Pallas kernels, run_first(): pl.pallas_call(functools.partial(first_kernel, dp, sp, seqs, chans), in_s...  76.1 us

profile of v4, /device:TPU:0, one launch (start us, length us, event | category | flops | bytes accessed | tf_op | source)
XLA Modules:
  0.0 323.0 jit_solution(15084038470838891494)
XLA Ops:
  0.7 0.7 broadcast_in_dim.10
  1.3 0.7 pad_maximum_fusion.1
  2.0 0.2 copy.33
  2.2 0.2 reshape.94
  2.4 0.7 pad_maximum_fusion.2
  3.1 0.1 copy.32
  3.2 0.1 reshape.93
  3.3 3.4 %concatenate.21 = bf16[2122]{0:T(1024)(128)(2,1)S(1)} concatenate(bf16[48]{0:T(256)(128)(2,1)} %param.19, bf16[96]{0:T(256)(128)(2,1)} %param.27, bf16[40]{0:T(256)(128)(2,1)S(1)} %reshape.93, bf16[1920]{0:T(1024)(128)(2,1)S(1)} %reshape.94, bf16[6]{0:T(256)(128)(2,1)} %param.24, bf16[6]{0:T(256)(128)(2,1)} %param.25, bf16[6]{0:T(256)(128)(2,1)} %param.26), dimensions={0} | concatenate | bytes 8488 | tf_op jit(solution)/shard_map/concatenate | solution.py:1571
  6.8 0.1 reshape.95
  6.9 1.5 pad_maximum_fusion.misc_ref
  8.3 76.1 %first_gather.1 = (bf16[4,8,48,768]{3,2,1,0:T(8,128)(2,1)}, bf16[2,4,4,48,384]{4,3,2,1,0:T(8,128)(2,1)}, bf16[8,128,1536]{2,1,0:T(8,128)(2,1)}, bf16[8,96,1536]{2,1,0:T(8,128)(2,1)}) custom-call(bf16[48,6144]{1,0:T(8,128)(2,1)} %w_zx_ref.1, bf16[48,384]{1,0:T(8,128)(2,1)} %pad_maximum_fusion.misc_ref, bf16[2,128,1536]{2,1,0:T(8,128)(2,1)} %hid_ref.3, ...), custom_call_target="tpu_custom_call" | custom-call | tf_op jit(solution)/shard_map/first_gather/pallas_call | solution.py:1012
  84.4 1.4 copy.34
  85.8 0.2 slice.98
  86.0 0.4 reshape.98
  86.4 0.1 fusion.3
  86.5 0.1 convert_element_type.66
  86.6 0.1 exp.7
  86.7 0.6 select_maximum_fusion.heads
  87.3 0.1 reshape.103
  87.4 0.1 broadcast_in_dim.11
  87.4 0.1 stack_reshape.3
  87.5 0.6 pad.50.skip
  88.1 0.1 slice.100
  88.2 0.3 convert_element_type.64
  88.6 0.1 copy.36
  88.7 0.1 slice.101
  88.8 0.1 convert_element_type.65
  88.9 0.1 copy.37
  89.0 0.6 pad_convert_fusion.1.taps
  89.6 0.2 constant_dynamic-slice_fusion.6
  89.8 0.1 slice.96
  89.9 1.1 fusion.1.wb_ref.wb
  91.0 0.1 slice.105
  91.1 0.1 reshape.99
  91.2 0.1 dynamic_slice.32
  91.3 0.6 pad_convert_fusion.2.gain
  91.9 0.1 convert_element_type.63
  92.0 0.6 pad_convert_fusion.norm
  92.6 86.4 %forward.1 = (bf16[4,8,48,768]{3,2,1,0:T(8,128)(2,1)}, bf16[8,128,1536]{2,1,0:T(8,128)(2,1)}, bf16[8,128,768]{2,1,0:T(8,128)(2,1)}, bf16[8,128,384]{2,1,0:T(8,12...) custom-call(bf16[48,6144]{1,0:T(8,128)(2,1)} %w_zx_ref.1, ...), custom_call_target="tpu_custom_call" | custom-call | tf_op jit(solution)/shard_map/forward/pallas_call | solution.py:1244
  179.1 127.9 %backward.1 = (bf16[2,128,1536]{2,1,0:T(8,128)(2,1)}, bf16[2,128,1536]{2,1,0:T(8,128)(2,1)}, f32[48,6144]{1,0:T(8,128)}, f32[48,256]{1,0:T(8,128)}, f32[4,48,128...) custom-call(bf16[8,128,768]{2,1,0:T(8,128)(2,1)} %get-tuple-element., ...), custom_call_target="tpu_custom_call" | custom-call | tf_op jit(solution)/shard_map/backward/pallas_call | solution.py:1524
  307.0 1.0 slice_bitcast_fusion
  307.9 0.1 copy.38
  308.1 0.1 copy.39
  308.2 0.9 slice_reduce_fusion.1
  309.0 0.5 convert_divide_fusion.1
  309.6 0.7 copy.40
  310.3 0.7 slice.88
  311.0 0.7 dynamic-slice_reduce_fusion
  311.7 0.1 reshape_squeeze.3
  311.7 0.6 reduce_sum.19
  312.4 0.6 dynamic-slice_bitcast_fusion
  313.0 0.7 slice.91
  313.6 0.1 constant_dynamic-slice_fusion
  313.7 0.5 slice_bitcast_fusion.2
  314.2 0.8 constant_dynamic-slice_fusion.1
  315.0 0.6 slice_bitcast_fusion.1
  315.6 0.5 slice_bitcast_fusion.4
  316.1 0.9 slice_reduce_fusion
  317.0 0.5 convert_divide_fusion
  317.5 2.2 copy.46
  319.7 0.9 copy.47
  320.6 1.0 copy.48
  321.6 0.6 copy.49
  322.2 0.8 copy.50
  (26 shorter events, 0.2 us)
Async XLA Ops:
  179.0 129.0 %copy-start.4 = (bf16[48,48]{1,0:T(8,128)(2,1)S(1)}, bf16[48,48]{1,0:T(8,128)(2,1)}, u32[]{:S(2)}) copy-start(bf16[48,48]{1,0:T(8,128)(2,1)} %param.18) | copy-start | bytes 13828
  179.1 130.0 %copy-start.5 = (bf16[48]{0:T(256)(128)(2,1)S(1)}, bf16[48]{0:T(256)(128)(2,1)}, u32[]{:S(2)}) copy-start(bf16[48]{0:T(256)(128)(2,1)} %param.19) | copy-start | bytes 292
  179.1 137.9 %copy-start.6 = (bf16[96]{0:T(256)(128)(2,1)S(1)}, bf16[96]{0:T(256)(128)(2,1)}, u32[]{:S(2)}) copy-start(bf16[96]{0:T(256)(128)(2,1)} %param.27) | copy-start | bytes 580
  307.0 12.7 %copy-start.1 = (bf16[2,128,1536]{2,1,0:T(8,128)(2,1)S(1)}, bf16[2,128,1536]{2,1,0:T(8,128)(2,1)}, u32[]{:S(2)}) copy-start(bf16[2,128,1536]{2,1,0:T(8,128)(2,1)} %get-tuple-element.103) | copy-start | bytes 2359300
  317.5 3.0 copy-start
  320.6 1.0 copy-start.3
  320.6 1.6 copy-start.2

commit v5 on v4

--- a/solution.py
+++ b/solution.py
@@ -952,10 +952,13 @@
             remote(dst, dst, self.across.at[0, 0], self.across.at[1, mask], at.along_dp(at.p)).wait_recv()
         self.crossing().start()
 
-    def finish(self):
+    def complete(self):
         at = self.at
         dst = self.out.at[1 - at.core]
         remote(dst, dst, self.ends.at[1], self.ends.at[2], at.along_sp(at.s)).wait_recv()
+
+    def finish(self):
+        at = self.at
         self.crossing().wait_send()
         for mask in range(1, at.dp):
             self.dp_copy(mask).wait_send()
@@ -963,69 +966,88 @@
             self.chip_copy(i).wait_send()
 
 
-def first_kernel(
-    dp, sp, seqs, chans, w_ref, misc_ref, hid_ref, o_ref, wx_out, misc_out, hid_out, o_out, *sems
+def pack_kernel(
+    w_bc, w_dt, norm, gate, bc_taps, bc_bias, x_taps, x_bias, dt_bias, a_log, d_skip, out, rows
 ):
-    place = Place(dp, sp, seqs)
-    inner = w_ref.shape[1] // 2
-    columns = lambda g: w_ref.at[:, pl.ds(pl.multiple_of(inner + g * chans, LANES), chans)]
-    rest = list(sems)
-
-    def take(scratch):
-        taken = rest[: len(scratch)]
-        del rest[: len(scratch)]
-        return taken
-
-    wx = ColumnGather(place, columns, wx_out, *take(ColumnGather.scratch(dp, sp, seqs)))
-    misc = CommonGather(place, misc_ref, misc_out, *take(CommonGather.scratch(dp, sp, seqs)))
-    hid = BlockGather(place, hid_ref, hid_out, *take(BlockGather.scratch(dp, sp, seqs)))
-    out = OutGather(place, o_ref, o_out, *take(OutGather.scratch(dp, sp, seqs)))
-    place.meet(more=out.ways.meet(True))
-    misc.start()
-    wx.start()
-    out.start()
-    hid.start()
-    misc.along_dp()
-    for odd in range(2):
-        wx.along_dp(odd)
-    for odd in range(2):
-        out.along_dp(odd)
-    misc.cross()
-    hid.arrive(0)
-    wx.forward()
-    out.forward()
-    for i in range(1, place.chips):
-        hid.arrive(i)
-    for i in range(place.chips):
-        hid.arrive_other(i)
-    wx.complete()
-    out.complete()
-    misc.finish()
-    wx.finish()
-    hid.finish()
-    out.finish()
-
-
-def run_first(dp, sp, seqs, chans, w_zx, misc, hidden, w_out):
-    share = w_zx.shape[0]
-    _, rows, cols = hidden.shape
+    share, wide = w_bc.shape
+    high = out.shape[0] - 16
+    out[...] = jnp.zeros(out.shape, BF16)
+    out[:share, :wide] = w_bc[...]
+    out[:share, wide : wide + w_dt.shape[1]] = w_dt[...]
+    rows[...] = jnp.zeros(rows.shape, F32)
+    lines = ((0, norm), (1, gate), (6, bc_bias), (7, dt_bias), (8, a_log), (9, d_skip), (14, x_bias))
+    for line, ref in lines:
+        size = ref.shape[0]
+        rows[line : line + 1, :size] = ref[...].astype(F32).reshape(1, size)
+    for line, ref in ((2, bc_taps), (10, x_taps)):
+        rows[line : line + 4, : ref.shape[1]] = ref[...].astype(F32)
+    out[high:, :] = rows[...].astype(BF16)
+
+
+def run_pack(w_bc, *args):
+    share, wide = w_bc.shape
+    shape = (-(-share // 16) * 16 + 16, wide + LANES)
+    vmem = pl.BlockSpec(memory_space=pltpu.VMEM)
     return pl.pallas_call(
-        functools.partial(first_kernel, dp, sp, seqs, chans),
-        in_specs=[ANY] * 4,
-        out_specs=[ANY] * 4,
-        out_shape=[
-            jax.ShapeDtypeStruct((dp, sp, share, chans), BF16),
-            jax.ShapeDtypeStruct((2, dp, sp // 2) + misc.shape, BF16),
-            jax.ShapeDtypeStruct((sp, rows, cols), BF16),
-            jax.ShapeDtypeStruct((sp,) + w_out.shape, BF16),
-        ],
-        scratch_shapes=ColumnGather.scratch(dp, sp, seqs)
-        + CommonGather.scratch(dp, sp, seqs)
-        + BlockGather.scratch(dp, sp, seqs)
-        + OutGather.scratch(dp, sp, seqs),
-        compiler_params=comm_params(1),
-        name="first_gather",
-    )(w_zx, misc, hidden, w_out)
+        pack_kernel,
+        in_specs=[vmem] * (1 + len(args)),
+        out_specs=vmem,
+        out_shape=jax.ShapeDtypeStruct(shape, BF16),
+        scratch_shapes=[pltpu.VMEM((16, shape[1]), F32)],
+        name="pack",
+    )(w_bc, *args)
+
+
+def flatten(values, each, total):
+    count, size = values.shape
+    lane = iota((size, total), 1)
+    place = (iota((size, total), 0) == lane - lane // each * each).astype(BF16)
+    wide = dot(values.astype(BF16), place)
+    keep = iota((count, total), 0) == iota((count, total), 1) // each
+    return jnp.sum(jnp.where(keep, wide, 0.0), axis=0, keepdims=True)
+
+
+def unpack(place, shards, misc, wb, dt_all, lines, norm, taps, heads, skip, gain):
+    share, gate_share, bc_share, x_share, head_share = shards
+    high = misc.shape[3] - 16
+    wide = misc.shape[4] - LANES
+    chans = gain.shape[1]
+    count = place.dp * place.sp
+    for index in range(count):
+        p, s = index // place.sp, index % place.sp
+        tile = misc[s % 2, p, s // 2]
+        span = slice(index * share, (index + 1) * share)
+        wb[span, :wide] = tile[:share, :wide]
+        dt_all[span, :] = tile[:share, wide:].astype(F32)
+        below = tile[high:, :].astype(F32)
+        for line in range(7):
+            lines[line, index : index + 1, :] = below[line : line + 1, :]
+    own_heads = head_share * place.seqs
+    turned = pltpu.roll(dt_all[...], lax.rem(LANES - place.group * own_heads, LANES), 1)
+    wb[:, wide:] = jnp.where(iota(turned.shape, 1) < own_heads, turned, 0.0).astype(BF16)
+    norm[0:1, :] = flatten(lines[0], share, norm.shape[1])
+    mine = lines[1, pl.ds(place.group * place.sp, place.sp), :]
+    gain[0:1, :] = flatten(mine, gate_share, chans)
+    taps[...] = jnp.zeros(taps.shape, F32)
+    for tap in range(5):
+        taps[tap : tap + 1, chans:] = flatten(lines[2 + tap], bc_share, wide)
+    found = []
+    for i in range(place.seqs):
+        holder = place.group * place.seqs + i
+        tile = misc[lax.rem(holder, 2), place.p, holder // 2]
+        below = tile[high:, :].astype(F32)
+        taps[0:5, i * x_share : (i + 1) * x_share] = below[10:15, :x_share]
+        found.append(below)
+    rows = [
+        flatten(jnp.concatenate([f[line : line + 1, :LANES] for f in found], axis=0), head_share, LANES)
+        for line in (7, 8, 9)
+    ]
+    rows = [jnp.where(iota((1, LANES), 1) < own_heads, row, 0.0) for row in rows]
+    heads[...] = jnp.zeros(heads.shape, F32)
+    heads[0:1, :] = rows[0]
+    heads[1:2, :] = jnp.exp(rows[1])
+    owner = iota((LANES, chans), 0) == iota((LANES, chans), 1) // P_SIZE
+    skip[...] = jnp.broadcast_to(dot(rows[2].astype(BF16), owner.astype(BF16)), skip.shape)
 
 
 def scan_block(wide, chans, x, bd, taps, heads, skip, mixed, enter, ext, halo, state):
@@ -1075,33 +1097,69 @@
 
 def forward_kernel(
     dp, sp, seqs, wide, inner,
-    w_ref, cot_ref, hid_ref, wx_ref, wb_ref, o_ref, norm, taps, heads, skip, gain,
-    wg_out, normed_out, x_out, bd_out, enter_out, dgate_out, dy_out, part_out, tg_out, to_out,
-    hid, wx, wb, rows_out, wg, cot, normed, x, bd, mixed, enter, gate, d_gated, gated, dgate, dy,
-    part, tg, to, ext, halo, state, sums, got, saves, sum_sems, *sems,
+    shards, w_ref, misc_ref, hid_ref, o_ref, cot_ref,
+    normed_out, x_out, bd_out, enter_out, dgate_out, dy_out, part_out, tg_out, to_out,
+    wx_out, wg_out, wb_out, norm, taps, heads, skip,
+    misc, dt_all, lines, gain, hid, wx_all, wb, rows_out, wg, cot, normed, x, bd, mixed, enter, gate, d_gated, gated, dgate, dy,
+    part, tg, to, ext, halo, state, sums, mine, got, saves, sum_sems, *sems,
 ):
     place = Place(dp, sp, seqs)
-    chans = wx.shape[1]
+    chans = gain.shape[1]
+    chips = place.chips
     blocks, rows, width = hid.shape
-    columns = lambda g: w_ref.at[:, pl.ds(pl.multiple_of(g * chans, LANES), chans)]
-    wg_comm = ColumnGather(place, columns, wg, *sems[:-1])
-    cot_comm = BlockGather(place, cot_ref, cot, sems[-1])
-    loads = [
-        pltpu.make_async_copy(src, dst, saves.at[7, i])
-        for i, (src, dst) in enumerate(
-            ((hid_ref, hid), (wx_ref, wx), (wb_ref, wb), (o_ref, rows_out))
-        )
-    ]
-    for load in loads:
-        load.start()
-    place.meet()
-    wg_comm.start()
-    cot_comm.start()
+    rest = list(sems)
+
+    def take(scratch):
+        taken = rest[: len(scratch)]
+        del rest[: len(scratch)]
+        return taken
+
+    def columns(first):
+        return lambda g: w_ref.at[:, pl.ds(pl.multiple_of(first + g * chans, LANES), chans)]
+
+    half = ColumnGather.scratch(dp, sp, seqs)
+    wx_comm = ColumnGather(place, columns(inner), wx_all, *take(half))
+    wg_comm = ColumnGather(place, columns(0), wg, *take(half))
+    misc_comm = CommonGather(place, misc_ref, misc, *take(CommonGather.scratch(dp, sp, seqs)))
+    out_comm = OutGather(place, o_ref, rows_out, *take(OutGather.scratch(dp, sp, seqs)))
+    hid_comm = BlockGather(place, hid_ref, hid, *take(BlockGather.scratch(dp, sp, seqs)))
+    cot_comm = BlockGather(place, cot_ref, cot, *take(BlockGather.scratch(dp, sp, seqs)))
+    place.meet(more=out_comm.ways.meet(True))
+    misc_comm.start()
+    wx_comm.start()
     halo[...] = jnp.zeros(halo.shape, F32)
     state[...] = jnp.zeros(state.shape, F32)
     sums[...] = jnp.zeros(sums.shape, F32)
-    for load in loads[:3]:
-        load.wait()
+    for odd in range(2):
+        wx_comm.along_dp(odd)
+    wg_comm.start()
+    out_comm.start()
+    misc_comm.along_dp()
+    wx_comm.forward()
+    misc_comm.cross()
+    for odd in range(2):
+        wg_comm.along_dp(odd)
+    hid_comm.start()
+    for odd in range(2):
+        out_comm.along_dp(odd)
+    hid_comm.arrive(0)
+    misc_comm.complete()
+    unpack(place, shards, misc, wb, dt_all, lines, norm, taps, heads, skip, gain)
+    wg_comm.forward()
+    hid_comm.arrive(1)
+    cot_comm.start()
+    for i in range(2, chips):
+        hid_comm.arrive(i)
+    out_comm.forward()
+    for i in range(chips):
+        hid_comm.arrive_other(i)
+    wx_comm.complete()
+    keeps = [
+        pltpu.make_async_copy(src, dst, saves.at[7, i])
+        for i, (src, dst) in enumerate(((wx_all, wx_out), (wb, wb_out)))
+    ]
+    for keep in keeps:
+        keep.start()
 
     def save(src, dst, index, b):
         return pltpu.make_async_copy(src.at[b], dst.at[b], saves.at[index, b])
@@ -1110,15 +1168,10 @@
     late = ((dgate, dgate_out), (dy, dy_out), (part, part_out))
 
     def first(b, carry):
-        @pl.when(b == blocks - 3)
-        def _():
-            for odd in range(2):
-                wg_comm.along_dp(odd)
-
         hidden = hid[b].astype(F32)
         scale = lax.rsqrt(jnp.mean(hidden * hidden, axis=-1, keepdims=True) + EPS)
         normed[b] = (hidden * scale * norm[0:1, :]).astype(BF16)
-        x[b] = dot(normed[b], wx[...]).astype(BF16)
+        x[b] = dot(normed[b], wx_all[...].reshape(width, chans)).astype(BF16)
         bd[b] = dot(normed[b], wb[...]).astype(BF16)
         scan_block(
             wide, chans, x[b], bd[b], taps, heads, skip, mixed.at[b], enter.at[b], ext, halo, state
@@ -1128,150 +1181,186 @@
         return carry
 
     lax.fori_loop(0, blocks, first, 0)
-    wg_comm.forward()
     wg_comm.complete()
-    loads[3].wait()
+    keeps.append(pltpu.make_async_copy(wg, wg_out, saves.at[7, 2]))
+    keeps[-1].start()
     lane = iota((rows, LANES), 1)
 
-    def gates(b):
-        gate[b] = dot(normed[b], wg[...].reshape(width, chans)).astype(BF16)
-
-    def second(b):
-        d_gated[b] = dot(cot[b], rows_out[...].reshape(chans, width), ((1,), (1,)))
-        gate_f = gate[b].astype(F32)
-        value = mixed[b].astype(F32) * gate_f * jax.nn.sigmoid(gate_f)
-        square = jnp.sum(value * value, axis=1, keepdims=True)
-        cross = jnp.sum(value * d_gated[b] * gain[0:1, :], axis=1, keepdims=True)
-        sums[...] = sums[...] + jnp.where(lane == 2 * b, square, 0.0) + jnp.where(
-            lane == 2 * b + 1, cross, 0.0
-        )
-
-    def gates_loop(b, carry):
-        gates(b)
-        return carry
-
-    lax.fori_loop(0, blocks, gates_loop, 0)
-
-    def own_core(i, carry):
-        second(cot_comm.arrive(i))
-        return carry
-
-    def other_core(i, carry):
-        second(cot_comm.arrive_other(i))
-        return carry
-
-    lax.fori_loop(0, place.chips, own_core, 0)
-    lax.fori_loop(0, place.chips, other_core, 0)
-
-    copies = [
-        remote(sums, got.at[i], sum_sems.at[0, i], sum_sems.at[1, i], place.along_sp(place.group_peer(i)))
-        for i in range(1, place.groups)
-    ]
-    for copy in copies:
-        copy.start()
-    keep_wg = pltpu.make_async_copy(wg, wg_out, saves.at[7, 0])
-    keep_wg.start()
-    total = sums[...]
-    for i, copy in enumerate(copies):
-        copy.wait_recv()
-        total = total + got[i + 1]
-    got[0] = total
-
-    def third(b, carry):
-        total = got[0]
-        square = jnp.sum(jnp.where(lane == 2 * b, total, 0.0), axis=1, keepdims=True)
-        cross = jnp.sum(jnp.where(lane == 2 * b + 1, total, 0.0), axis=1, keepdims=True)
-        scale = lax.rsqrt(square * (1.0 / inner) + EPS)
-        mean = cross * scale * (1.0 / inner)
+    def sum_copies(n):
+        return [
+            remote(
+                mine.at[n], got.at[n, i], sum_sems.at[2 * n, i], sum_sems.at[2 * n + 1, i],
+                place.along_sp(place.group_peer(i)),
+            )
+            for i in range(1, place.groups)
+        ]
+
+    def send_sums(n):
+        mine[n] = sums[...].T[:blocks]
+        for copy in sum_copies(n):
+            copy.start()
+
+    def take_sums(n):
+        total = mine[n]
+        for i, copy in enumerate(sum_copies(n)):
+            copy.wait_recv()
+            total = total + got[n, i + 1]
+        sums[...] = jnp.concatenate([total, jnp.zeros((LANES - blocks, rows), F32)], axis=0).T
+
+    def column(b):
+        return jnp.sum(jnp.where(lane == b, sums[...], 0.0), axis=1, keepdims=True)
+
+    def activated(b):
         gate_f = gate[b].astype(F32)
         sig = jax.nn.sigmoid(gate_f)
-        silu = gate_f * sig
-        mix = mixed[b].astype(F32)
-        unit = mix * silu * scale
-        gated[b] = (unit * gain[0:1, :]).astype(BF16)
+        return gate_f, sig, mixed[b].astype(F32) * gate_f * sig
+
+    def second(b, carry):
+        gate[b] = dot(normed[b], wg[...].reshape(width, chans)).astype(BF16)
+        _, _, value = activated(b)
+        square = jnp.sum(value * value, axis=1, keepdims=True)
+        sums[...] = jnp.where(lane == b, square, sums[...])
+        return carry
+
+    lax.fori_loop(0, blocks, second, 0)
+    send_sums(0)
+    out_comm.complete()
+    take_sums(0)
+    scales = lax.rsqrt(sums[...] * (1.0 / inner) + EPS)
+    sums[...] = scales
+
+    def third(b, carry):
+        _, _, value = activated(b)
+        gated[b] = (value * column(b) * gain[0:1, :]).astype(BF16)
+        part[b] = dot(gated[b], rows_out[...].reshape(chans, width)).astype(BF16)
+        save(part, part_out, 6, b).start()
+        return carry
+
+    lax.fori_loop(0, blocks, third, 0)
+    got[0, 0] = sums[...].T[:blocks]
+
+    def fourth(b):
+        d_gated[b] = dot(cot[b], rows_out[...].reshape(chans, width), ((1,), (1,)))
+        _, _, value = activated(b)
+        cross = jnp.sum(value * d_gated[b] * gain[0:1, :], axis=1, keepdims=True)
+        sums[...] = jnp.where(lane == b, cross, sums[...])
+
+    def own_core(i, carry):
+        fourth(cot_comm.arrive(i))
+        return carry
+
+    def other_core(i, carry):
+        fourth(cot_comm.arrive_other(i))
+        return carry
+
+    lax.fori_loop(0, chips, own_core, 0)
+    lax.fori_loop(0, chips, other_core, 0)
+    send_sums(1)
+    everything = blocks * rows
+    slots = sp // 2
+    keep_to = []
+    for half in range(2):
+        size = chans // 2
+        lanes = gated[:, :, half * size : (half + 1) * size].reshape(everything, size)
+        value = dot(lanes, cot[...].reshape(everything, width), ((0,), (0,)))
+        span = pl.ds(half * slots, slots)
+        to[span] = value.astype(BF16).reshape((slots,) + to.shape[1:])
+        keep_to.append(pltpu.make_async_copy(to.at[span], to_out.at[span], saves.at[8, half]))
+        keep_to[-1].start()
+    take_sums(1)
+    crosses = sums[...]
+    scales = jnp.concatenate([got[0, 0], jnp.zeros((LANES - blocks, rows), F32)], axis=0).T
+
+    def fifth(b, carry):
+        scale = jnp.sum(jnp.where(lane == b, scales, 0.0), axis=1, keepdims=True)
+        mean = column(b) * scale * (1.0 / inner)
+        gate_f, sig, value = activated(b)
+        unit = value * scale
         back = scale * (d_gated[b] * gain[0:1, :] - unit * mean)
-        dy[b] = (back * silu).astype(BF16)
-        dgate[b] = (back * mix * sig * (1.0 + gate_f * (1.0 - sig))).astype(BF16)
-        part[b] = dot(gated[b], rows_out[...].reshape(chans, width)).astype(BF16)
-        for index, (src, dst) in enumerate(late):
+        dy[b] = (back * gate_f * sig).astype(BF16)
+        dgate[b] = (
+            back * mixed[b].astype(F32) * sig * (1.0 + gate_f * (1.0 - sig))
+        ).astype(BF16)
+        for index, (src, dst) in enumerate(late[:2]):
             save(src, dst, 4 + index, b).start()
         return carry
 
-    lax.fori_loop(0, blocks, third, 0)
-    everything = blocks * rows
+    lax.fori_loop(0, blocks, fifth, 0)
     tile = width // dp
-    keep_tg, keep_to = [], []
+    keep_tg = []
     for p in range(dp):
-        columns = normed[:, :, p * tile : (p + 1) * tile].reshape(everything, tile)
-        value = dot(columns, dgate[...].reshape(everything, chans), ((0,), (0,)))
+        lanes = normed[:, :, p * tile : (p + 1) * tile].reshape(everything, tile)
+        value = dot(lanes, dgate[...].reshape(everything, chans), ((0,), (0,)))
         tg[p] = value.astype(BF16).reshape(tg.shape[1:])
-        keep_tg.append(pltpu.make_async_copy(tg.at[p], tg_out.at[p], saves.at[7, 1 + p]))
+        keep_tg.append(pltpu.make_async_copy(tg.at[p], tg_out.at[p], saves.at[7, 3 + p]))
         keep_tg[-1].start()
-    slots = sp // 2
-    for half in range(2):
-        size = chans // 2
-        columns = gated[:, :, half * size : (half + 1) * size].reshape(everything, size)
-        value = dot(columns, cot[...].reshape(everything, width), ((0,), (0,)))
-        span = pl.ds(half * slots, slots)
-        to[span] = value.astype(BF16).reshape((slots,) + to.shape[1:])
-        keep_to.append(
-            pltpu.make_async_copy(to.at[span], to_out.at[span], saves.at[8, half])
-        )
-        keep_to[-1].start()
-    for copy in copies:
-        copy.wait_send()
-    cot_comm.finish()
-    wg_comm.finish()
-    for keep in [keep_wg] + keep_tg + keep_to:
+    for n in range(2):
+        for copy in sum_copies(n):
+            copy.wait_send()
+    for comm in (misc_comm, wx_comm, wg_comm, out_comm, hid_comm, cot_comm):
+        comm.finish()
+    for keep in keeps + keep_tg + keep_to:
         keep.wait()
     for index, (src, dst) in enumerate(early + late):
         for b in range(blocks):
             save(src, dst, index, b).wait()
 
 
-def run_middle(dp, sp, seqs, wide, inner, w_zx, cotangent, hidden, wx, wb, w_rows, norm, taps, heads, skip, gain):
+def run_forward(dp, sp, seqs, wide, inner, shards, w_zx, misc, hidden, w_out, cotangent):
     share = w_zx.shape[0]
-    blocks, rows, width = hidden.shape
-    chans, cols = wx.shape[1], wb.shape[1]
+    _, rows, width = hidden.shape
+    blocks, chans, cols = sp, inner * seqs // sp, misc.shape[1]
     states = wide // 2
+    columns = (dp, sp, share, chans)
+    w_rows = (sp,) + w_out.shape
+    tokens = lambda n: (blocks, rows, n)
     shapes = [
-        (dp, sp, share, chans), hidden.shape, (blocks, rows, chans), (blocks, rows, cols),
-        (blocks, states, chans), (blocks, rows, chans), (blocks, rows, chans), hidden.shape,
-        (dp, sp, share, chans), w_rows.shape,
+        tokens(width), tokens(chans), tokens(cols), (blocks, states, chans), tokens(chans),
+        tokens(chans), tokens(width), columns, w_rows, columns, columns, (width, cols),
     ]
-    block = lambda n, kind: pltpu.VMEM((blocks, rows, n), kind)
+    params = [(8, width), (8, chans + wide), (8, LANES), (8, chans)]
+    half = lambda shape: pltpu.VMEM(shape, BF16)
+    full = lambda *shape: pltpu.VMEM(shape, F32)
     vmem = pl.BlockSpec(memory_space=pltpu.VMEM)
     return pl.pallas_call(
-        functools.partial(forward_kernel, dp, sp, seqs, wide, inner),
-        in_specs=[ANY] * 6 + [vmem] * 5,
-        out_specs=[ANY] * len(shapes),
-        out_shape=[jax.ShapeDtypeStruct(shape, BF16) for shape in shapes],
+        functools.partial(forward_kernel, dp, sp, seqs, wide, inner, shards),
+        in_specs=[ANY] * 5,
+        out_specs=[ANY] * len(shapes) + [vmem] * len(params),
+        out_shape=[jax.ShapeDtypeStruct(shape, BF16) for shape in shapes]
+        + [jax.ShapeDtypeStruct(shape, F32) for shape in params],
         scratch_shapes=[
-            pltpu.VMEM(hidden.shape, BF16),
-            pltpu.VMEM(wx.shape, BF16),
-            pltpu.VMEM(wb.shape, BF16),
-            pltpu.VMEM(w_rows.shape, BF16),
-            pltpu.VMEM(shapes[0], BF16),
-            pltpu.VMEM(hidden.shape, BF16),
-            block(width, BF16), block(chans, BF16), block(cols, BF16), block(chans, BF16),
-            pltpu.VMEM(shapes[4], BF16),
-            block(chans, BF16), block(chans, F32), block(chans, BF16), block(chans, BF16),
-            block(chans, BF16), block(width, BF16),
-            pltpu.VMEM(shapes[0], BF16),
-            pltpu.VMEM(w_rows.shape, BF16),
-            pltpu.VMEM((rows + 8, chans + wide), F32),
-            pltpu.VMEM((8, chans + wide), F32),
-            pltpu.VMEM((states, chans), F32),
-            pltpu.VMEM((rows, LANES), F32),
-            pltpu.VMEM((sp // seqs, rows, LANES), F32),
-            dma(9, max(blocks, dp + 1, 4)),
-            dma(2, sp // seqs),
+            half((2, dp, sp // 2) + misc.shape),
+            full(width, LANES),
+            full(7, dp * sp, cols),
+            full(8, chans),
+            half(tokens(width)),
+            half(columns),
+            half((width, cols)),
+            half(w_rows),
+            half(columns),
+            half(tokens(width)),
+            half(tokens(width)), half(tokens(chans)), half(tokens(cols)), half(tokens(chans)),
+            half((blocks, states, chans)),
+            half(tokens(chans)), full(*tokens(chans)), half(tokens(chans)), half(tokens(chans)),
+            half(tokens(chans)), half(tokens(width)),
+            half(columns),
+            half(w_rows),
+            full(rows + 8, chans + wide),
+            full(8, chans + wide),
+            full(states, chans),
+            full(rows, LANES),
+            full(2, blocks, rows),
+            full(2, sp // seqs, blocks, rows),
+            dma(9, max(blocks, dp + 3)),
+            dma(4, sp // seqs),
         ]
-        + ColumnGather.scratch(dp, sp, seqs)
-        + BlockGather.scratch(dp, sp, seqs),
+        + ColumnGather.scratch(dp, sp, seqs) * 2
+        + CommonGather.scratch(dp, sp, seqs)
+        + OutGather.scratch(dp, sp, seqs)
+        + BlockGather.scratch(dp, sp, seqs) * 2,
         compiler_params=comm_params(2),
         name="forward",
-    )(w_zx, cotangent, hidden, wx, wb, w_rows, norm, taps, heads, skip, gain)
+    )(w_zx, misc, hidden, w_out, cotangent)
 
 
 def backward_kernel(
@@ -1541,13 +1630,81 @@
     )
 
 
-def pad_last(value, size):
-    return jnp.pad(value, [(0, 0)] * (value.ndim - 1) + [(0, size - value.shape[-1])])
-
-
-def eight_rows(*rows):
-    stacked = jnp.stack(rows, axis=0)
-    return jnp.pad(stacked, ((0, 8 - stacked.shape[0]), (0, 0)))
+def finish_kernel(
+    dp, sp, seqs,
+    hidden, grad, zx, bc, dt_parts, norm_sum, out, gate_sum, own, common, w_dt, norm_gain, gate_gain,
+    hidden_to, grad_to, zx_to, bc_to, dt_to, norm_to, bc_taps, bc_bias, x_taps, x_bias, g_dt, g_log,
+    g_skip, gate_to, out_to, tall,
+):
+    place = Place(dp, sp, seqs)
+    for src, dst in ((hidden, hidden_to), (grad, grad_to), (zx, zx_to), (bc, bc_to), (out, out_to)):
+        dst[...] = src[...]
+    share, heads = w_dt.shape
+    each = heads // place.groups
+    lane = iota((share, LANES), 1)
+    value = jnp.zeros((share, LANES), F32)
+    for g in range(place.groups):
+        part = jnp.where(lane < each, dt_parts[g], 0.0)
+        value = value + (pltpu.roll(part, g * each, 1) if g else part)
+    value = value[:, :heads]
+    dt_to[...] = value
+    dt_sum = jnp.sum(value * w_dt[...].astype(F32), axis=1, keepdims=True)
+
+    def row(column):
+        size = column.shape[0]
+        wide = -(-size // LANES) * LANES
+        tall[:size, :] = jnp.broadcast_to(column, (size, LANES))
+        return tall[:wide, :].T[0:1, :size]
+
+    share_sum = row(norm_sum[:, 0:1] + dt_sum)
+    norm_to[...] = (share_sum / norm_gain[...].astype(F32).reshape(1, share)).reshape(share)
+    size = gate_gain.shape[0]
+    gate_to[...] = (row(gate_sum[:, 0:1]) / gate_gain[...].astype(F32).reshape(1, size)).reshape(size)
+    x_share, bc_share = x_bias.shape[0], bc_bias.shape[0]
+    chans = own.shape[1] - LANES
+    place_in = lax.rem(place.s, place.seqs)
+    mine = jnp.zeros((8, x_share), F32)
+    for i in range(place.seqs):
+        mine = mine + jnp.where(place_in == i, own[:, i * x_share : (i + 1) * x_share], 0.0)
+    x_taps[...] = mine[0:4]
+    x_bias[...] = mine[4:5].reshape(x_share)
+    head_share = g_dt.shape[0]
+    owner = (iota((x_share, LANES), 0) // P_SIZE == iota((x_share, LANES), 1)).astype(F32)
+    skips = dot(mine, owner, precision=HIGH)[5:6, :head_share]
+    g_skip[...] = skips.reshape(head_share)
+    per_head = own[:, chans:]
+    turned = per_head
+    for i in range(1, place.seqs):
+        turned = jnp.where(place_in == i, pltpu.roll(per_head, LANES - i * head_share, 1), turned)
+    g_dt[...] = turned[0:1, :head_share].reshape(head_share)
+    g_log[...] = turned[1:2, :head_share].reshape(head_share)
+    wide = common.shape[1]
+    index = place.p * sp + place.s
+    pick = (iota((wide, LANES), 0) == iota((wide, LANES), 1) + index * bc_share).astype(F32)
+    mine = dot(common[...], pick, precision=HIGH)[:, :bc_share]
+    bc_taps[...] = mine[0:4]
+    bc_bias[...] = mine[4:5].reshape(bc_share)
+
+
+def run_finish(dp, sp, seqs, x_share, head_share, bc_share, *args):
+    hidden, grad, zx, bc, _, _, out, _, _, _, w_dt, norm_gain, gate_gain = args
+    vmem = pl.BlockSpec(memory_space=pltpu.VMEM)
+    shapes = [
+        hidden.shape, grad.shape, zx.shape, bc.shape, w_dt.shape, norm_gain.shape, (4, bc_share),
+        (bc_share,), (4, x_share), (x_share,), (head_share,), (head_share,), (head_share,),
+        gate_gain.shape, out.shape,
+    ]
+    kinds = [BF16, BF16] + [F32] * 13
+    tall = max(-(-n // LANES) * LANES for n in (norm_gain.shape[0], gate_gain.shape[0]))
+    return pl.pallas_call(
+        functools.partial(finish_kernel, dp, sp, seqs),
+        in_specs=[vmem] * len(args),
+        out_specs=[vmem] * len(shapes),
+        out_shape=[jax.ShapeDtypeStruct(s, k) for s, k in zip(shapes, kinds)],
+        scratch_shapes=[pltpu.VMEM((tall, LANES), F32)],
+        compiler_params=pltpu.CompilerParams(vmem_limit_bytes=VMEM_LIMIT),
+        name="finish",
+    )(*args)
 
 
 def on_device(
@@ -1555,104 +1712,31 @@
     hidden_in, w_zx, w_bc, w_dt, norm_gain, conv_bc_weight, conv_bc_bias,
     conv_x_weight, conv_x_bias, dt_bias, a_log, d_skip, gate_gain, w_out, cotangent,
 ):
-    me_dp, me_sp = lax.axis_index("dp"), lax.axis_index("sp")
-    seqs, block, width = hidden_in.shape
-    groups = sp // seqs
-    group = lax.rem(me_sp, groups)
+    seqs, width = hidden_in.shape[0], hidden_in.shape[2]
     wide, heads = w_bc.shape[1], w_dt.shape[1]
-    share, taps_n = w_zx.shape[0], conv_x_weight.shape[1]
     inner = heads * P_SIZE
-    chans = inner // groups
-    own_heads = heads // groups
-    gate_share, bc_share = gate_gain.shape[0], conv_bc_bias.shape[0]
-    x_share, head_share = conv_x_bias.shape[0], dt_bias.shape[0]
-    cols = wide + LANES
-
-    small = jnp.concatenate(
-        [
-            norm_gain,
-            gate_gain,
-            jnp.concatenate([conv_bc_weight, conv_bc_bias[:, None]], axis=1).reshape(-1),
-            jnp.concatenate([conv_x_weight, conv_x_bias[:, None]], axis=1).reshape(-1),
-            dt_bias,
-            a_log,
-            d_skip,
-        ]
+    chans = inner * seqs // sp
+    x_share, head_share, bc_share = conv_x_bias.shape[0], dt_bias.shape[0], conv_bc_bias.shape[0]
+    misc = run_pack(
+        w_bc, w_dt, norm_gain, gate_gain, conv_bc_weight.T, conv_bc_bias, conv_x_weight.T,
+        conv_x_bias, dt_bias, a_log, d_skip,
     )
-    spare = cols - wide - heads
-    high = -(-max(share, -(-small.shape[0] // spare)) // 16) * 16
-    tall = lambda v: jnp.pad(v, ((0, high - share), (0, 0)))
-    misc = jnp.concatenate(
-        [tall(w_bc), tall(w_dt), pad_last(small, high * spare).reshape(high, spare)], axis=1
+    shards = (w_zx.shape[0], gate_gain.shape[0], bc_share, x_share, head_share)
+    (normed, x, bd, entering, dgate, dy, out_part, terms_gate, terms_out, wx, wg, wb,
+     norm, taps, head_rows, skip) = run_forward(
+        dp, sp, seqs, wide, inner, shards, w_zx, misc, hidden_in, w_out, cotangent
     )
-    wx, misc_all, hidden_all, w_rows = run_first(dp, sp, seqs, chans, w_zx, misc, hidden_in, w_out)
-    misc_all = jnp.transpose(misc_all, (1, 2, 0, 3, 4)).reshape((dp, sp) + misc.shape)
-
-    wx = wx.reshape(width, chans)
-    bd_all = misc_all[:, :, :share, :].reshape(width, cols)
-    dt_cols = lax.dynamic_slice_in_dim(bd_all[:, wide : wide + heads], group * own_heads, own_heads, axis=1)
-    wb = jnp.concatenate([bd_all[:, :wide], pad_last(dt_cols, LANES)], axis=1)
-    few = misc_all[:, :, :, wide + heads :].reshape(dp, sp, high * spare)
-    ends = []
-    for size in (share, gate_share, bc_share * (taps_n + 1), x_share * (taps_n + 1)) + (head_share,) * 3:
-        ends.append(size + (ends[-1] if ends else 0))
-    piece = lambda i: few[:, :, (ends[i - 1] if i else 0) : ends[i]]
-    mine = lambda i: lax.dynamic_slice_in_dim(piece(i)[0], group * seqs, seqs, axis=0).astype(F32)
-    norm_all = piece(0).reshape(width).astype(F32)
-    gate_mine = lax.dynamic_slice_in_dim(
-        piece(1).reshape(inner), group * chans, chans
-    ).astype(F32)
-    bc_all = piece(2).reshape(wide, taps_n + 1).astype(F32)
-    x_all = mine(3).reshape(chans, taps_n + 1)
-    taps = jnp.concatenate([x_all, bc_all], axis=0).T
-    taps = jnp.pad(taps, ((0, 8 - taps.shape[0]), (0, 0)))
-    head_rows = eight_rows(
-        pad_last(mine(4).reshape(own_heads), LANES),
-        pad_last(jnp.exp(mine(5).reshape(own_heads)), LANES),
+    grads = run_backward(
+        dp, sp, seqs, dy, x, bd, dgate, entering, taps, head_rows, skip, norm,
+        wg.reshape(width, chans), wx.reshape(width, chans), wb, normed, out_part, terms_out,
+        terms_gate, hidden_in, cotangent, w_zx, w_bc, w_out, wide,
     )
-    skip = eight_rows(jnp.repeat(mine(6).reshape(own_heads), P_SIZE))
-    gain = eight_rows(gate_mine)
-
-    norm = eight_rows(norm_all)
-    wg, normed, x_blocks, bd_blocks, entering, dgate, dy, out_part, terms_gate, terms_out = run_middle(
-        dp, sp, seqs, wide, inner, w_zx, cotangent, hidden_all, wx, wb, w_rows,
-        norm, taps, head_rows, skip, gain,
+    results = list(
+        run_finish(dp, sp, seqs, x_share, head_share, bc_share, *grads, w_dt, norm_gain, gate_gain)
     )
-    (hidden_out, grad_hidden, grad_w_zx, grad_w_bc, dt_parts, norm_sum, grad_w_out, gate_sum,
-     own_small, common_small) = run_backward(
-        dp, sp, seqs, dy, x_blocks, bd_blocks, dgate, entering, taps, head_rows, skip, norm,
-        wg.reshape(width, chans), wx, wb, normed, out_part, terms_out, terms_gate,
-        hidden_in, cotangent, w_zx, w_bc, w_out, wide,
-    )
-    grad_w_dt = jnp.transpose(dt_parts[:, :, :own_heads], (1, 0, 2)).reshape(share, heads)
-    grad_norm_gain = (
-        norm_sum[:, 0] + jnp.sum(grad_w_dt * w_dt.astype(F32), axis=1)
-    ) / norm_gain.astype(F32)
-    grad_gate_gain = gate_sum[:, 0] / gate_gain.astype(F32)
-
-    part = lax.rem(me_sp, seqs)
-    g_x = lax.dynamic_slice_in_dim(own_small[:, :chans], part * x_share, x_share, axis=1)
-    g_heads = lax.dynamic_slice_in_dim(own_small[:, chans:], part * head_share, head_share, axis=1)
-    g_skip = jnp.sum(g_x[5].reshape(head_share, P_SIZE), axis=1)
-    first = (me_dp * sp + me_sp) * bc_share
-    g_bc = lax.dynamic_slice_in_dim(common_small, first, bc_share, axis=1)
-    return (
-        hidden_out,
-        grad_hidden,
-        grad_w_zx,
-        grad_w_bc,
-        grad_w_dt,
-        grad_norm_gain,
-        g_bc[:taps_n].T,
-        g_bc[taps_n],
-        g_x[:taps_n].T,
-        g_x[taps_n],
-        g_heads[0],
-        g_heads[1],
-        g_skip,
-        grad_gate_gain,
-        grad_w_out,
-    )
+    for taps_at in (6, 8):
+        results[taps_at] = results[taps_at].T
+    return tuple(results)
 
 
 def solution(mesh):

time: 324 us -> 292 us (0.901)
  local copies, waits for them, and re-layouts: 23.6 us -> 0 us
  other arithmetic: 8.21 us -> 0 us
    pallas_call x1, Pallas kernels: 128 us -> 144 us  [run_backward(): pl.pallas_call(functools.partial(backward_kernel, dp, sp, seqs, wide, cha...]
    pallas_call x2 -> x3, Pallas kernels: 163 us -> 147 us  [the longest x1 142 us: run_forward(): pl.pallas_call(functools.partial(forward_kernel, dp, sp, seqs, wide, inne...]
    unnamed x21 -> x0, local copies, waits for them, and re-layouts: 6.3 us -> none
    slice x13 -> x0, local copies, waits for them, and re-layouts: 4.41 us -> none  [the longest x1 0.9 us: on_device(): grad_gate_gain = gate_sum[:, 0] / gate_gain.astype(F32)]
    concatenate x4 -> x0, other arithmetic: 3.98 us -> none  [the longest x1 1.45 us: on_device(): jnp.concatenate([tall(w_bc), tall(w_dt), pad_last(small, high * spare).re...]
    concatenate x3 -> x0, local copies, waits for them, and re-layouts: 3.69 us -> none  [the longest x1 3.42 us: on_device(): jnp.concatenate([norm_gain, gate_gain, jnp.concatenate([conv_bc_weight, c...]
    transpose x5 -> x0, local copies, waits for them, and re-layouts: 3.63 us -> none  [the longest x1 1.39 us: on_device(): jnp.transpose(misc_all, (1, 2, 0, 3, 4)).reshape((dp, sp) + misc.shape)]
where the time goes in v5:
time: 292 us
  Pallas kernels  291 us (100%)
    pallas_call x1, Pallas kernels, run_backward(): pl.pallas_call(functools.partial(backward_kernel, dp, sp, seqs, wide, cha...  144 us
    pallas_call x1, Pallas kernels, run_forward(): pl.pallas_call(functools.partial(forward_kernel, dp, sp, seqs, wide, inne...  142 us

profile of v5, /device:TPU:0, one launch (start us, length us, event | category | flops | bytes accessed | tf_op | source)
XLA Modules:
  0.0 292.0 jit_solution(13103868055775445156)
XLA Ops:
  0.6 1.5 pack.1.misc_ref
  2.1 141.5 %forward.1 = (bf16[8,128,1536]{2,1,0:T(8,128)(2,1)}, bf16[8,128,768]{2,1,0:T(8,128)(2,1)}, bf16[8,128,384]{2,1,0:T(8,128)(2,1)}, bf16[8,128,768]{2,1,0:T(8,128)(...) custom-call(bf16[48,6144]{1,0:T(8,128)(2,1)} %w_zx_ref.1, ...), custom_call_target="tpu_custom_call" | custom-call | tf_op jit(solution)/shard_map/forward/pallas_call | solution.py:1325
  143.6 144.2 %backward.1 = (bf16[2,128,1536]{2,1,0:T(8,128)(2,1)}, bf16[2,128,1536]{2,1,0:T(8,128)(2,1)}, f32[48,6144]{1,0:T(8,128)}, f32[48,256]{1,0:T(8,128)}, f32[4,48,128...) custom-call(bf16[8,128,768]{2,1,0:T(8,128)(2,1)} %get-tuple-element., ...), custom_call_target="tpu_custom_call" | custom-call | tf_op jit(solution)/shard_map/backward/pallas_call | solution.py:1613
  287.8 4.1 %finish.1 = (bf16[2,128,1536]{2,1,0:T(8,128)(2,1)}, bf16[2,128,1536]{2,1,0:T(8,128)(2,1)}, f32[48,6144]{1,0:T(8,128)}, f32[48,256]{1,0:T(8,128)}, f32[48,48]{1,0...) custom-call(bf16[2,128,1536]{2,1,0:T(8,128)(2,1)} %get-tuple-element, ...), custom_call_target="tpu_custom_call" | custom-call | tf_op jit(solution)/shard_map/finish/pallas_call | solution.py:1699

commit v6 on v5

--- a/solution.py
+++ b/solution.py
@@ -13,6 +13,7 @@
 BF16 = jnp.bfloat16
 HIGH = lax.Precision.HIGHEST
 LANES = 128
+PIECES = 3
 VMEM_LIMIT = 58 * 1024 * 1024
 
 
@@ -20,6 +21,24 @@
     return lax.dot_general(
         left, right, (dims, ((), ())), precision=precision, preferred_element_type=F32
     )
+
+
+def parts_of(value, count):
+    found = []
+    for _ in range(count):
+        found.append(value.astype(BF16))
+        value = value - found[-1].astype(F32)
+    return found
+
+
+def select_rows(chosen, value):
+    size = value.shape[1]
+    wide = dot(chosen.astype(BF16), jnp.concatenate(parts_of(value, 3), axis=1))
+    return wide[:, :size] + wide[:, size : 2 * size] + wide[:, 2 * size :]
+
+
+def head_sums(value, owner):
+    return dot(jnp.concatenate(parts_of(value, 2), axis=1), jnp.concatenate([owner, owner], axis=0))
 
 
 def iota(shape, axis):
@@ -99,7 +118,7 @@
     xval = xmat.astype(F32)
     dt_pre, steps, logs = steps_of(bd[:, wide:], heads)
     row, col = iota((rows, rows), 0), iota((rows, rows), 1)
-    cumul = dot((row >= col).astype(F32), logs, precision=HIGH)
+    cumul = select_rows(row >= col, logs)
     cumul_t = cumul.T
     last = cumul[rows - 1 :, :]
     later = row <= col
@@ -119,11 +138,17 @@
     dstate[...] = dleave * spread_all(final, pairs, low_half[0:1, :]) + dot(
         cmat, dy_grown, ((0,), (0,))
     )
-    owner = (iota((chans, LANES), 0) // P_SIZE == iota((chans, LANES), 1)).astype(F32)
-    near = dot(xval * from_state, owner, precision=HIGH) * shrunk
-    reach = dot(dy * across, owner, precision=HIGH) * grown
+    owner = (iota((chans, LANES), 0) // P_SIZE == iota((chans, LANES), 1)).astype(BF16)
     kept = jnp.sum(entering.astype(F32) * dleave, axis=0, keepdims=True)
-    kept = dot(jnp.broadcast_to(kept, (8, chans)), owner, precision=HIGH)[0:1, :] * final
+    found = head_sums(
+        jnp.concatenate(
+            [xval * from_state, dy * across, jnp.broadcast_to(kept, (8, chans))], axis=0
+        ),
+        owner,
+    )
+    near = found[:rows] * shrunk
+    reach = found[rows : 2 * rows] * grown
+    kept = found[2 * rows : 2 * rows + 1] * final
     pairs_sum = jnp.zeros((rows, rows), F32)
     head_lane = iota((rows, LANES), 1)
     col_sum = jnp.zeros((rows, LANES), F32)
@@ -160,8 +185,8 @@
     row_sum = jnp.concatenate(
         row_sums + [jnp.zeros((LANES - 2 * pairs, rows), F32)], axis=0
     ).T
-    d_logs = dot((row <= col).astype(F32), row_sum - steps * col_sum + reach, precision=HIGH)
-    d_logs = d_logs + dot((row > col).astype(F32), steps * near, precision=HIGH) + kept
+    d_logs = select_rows(row <= col, row_sum - steps * col_sum + reach)
+    d_logs = d_logs + select_rows(row > col, steps * near) + kept
     d_steps = col_sum + near - heads[1:2, :] * d_logs
     d_pre = d_steps * jax.nn.sigmoid(dt_pre)
     dbd[:, wide:] = d_pre.astype(BF16)
@@ -1065,7 +1090,7 @@
     cmat = act[:, chans + half :]
     _, steps, logs = steps_of(bd[:, wide:], heads)
     earlier = iota((rows, rows), 0) >= iota((rows, rows), 1)
-    cumul = dot(earlier.astype(F32), logs, precision=HIGH)
+    cumul = select_rows(earlier, logs)
     cumul_t = cumul.T
     last = cumul[rows - 1 :, :]
     scores = dot(cmat, bmat, ((1,), (1,)))
@@ -1138,10 +1163,10 @@
     wx_comm.forward()
     misc_comm.cross()
     for odd in range(2):
-        wg_comm.along_dp(odd)
+        out_comm.along_dp(odd)
     hid_comm.start()
     for odd in range(2):
-        out_comm.along_dp(odd)
+        wg_comm.along_dp(odd)
     hid_comm.arrive(0)
     misc_comm.complete()
     unpack(place, shards, misc, wb, dt_all, lines, norm, taps, heads, skip, gain)
@@ -1365,11 +1390,11 @@
 
 def backward_kernel(
     dp, sp, seqs, wide, chans,
-    dy, x, x_before, bd, bd_before, dgate, enter, taps, heads, skip, norm, wg, wx, wb,
+    dy, x, x_before, bd, bd_before, dgate, enter, taps, heads, skip, norm, wg_ref, wx_ref, wb_ref,
     normed_ref, out_part, terms_out, terms_gate, hid_ref, cot_ref, w_zx_ref, w_bc_ref, w_out_ref,
     hidden_out, grad_hidden, grad_zx, grad_bc, grad_dt, norm_sum, grad_out, gate_sum, own_small, common_small,
     ext, gext, halo, dstate, dtaps, dheads, dskip, dx, dbd, normed, part,
-    hid, cot, w_zx, w_bc, w_out, loads, tb, og, ob, oo, own, *scratch,
+    hid, cot, w_zx, w_bc, w_out, wg, wx, wb, loads, tb, og, ob, oo, own, *scratch,
 ):
     step, steps = pl.program_id(0), pl.num_programs(0)
     chunk = steps - 1 - step
@@ -1394,6 +1419,10 @@
         tx, landed = take(2)
         x_reds.append((tx, ShardReduce(place, tx, landed, False, *take(4))))
         x_parts.append(landed)
+    weight_loads = [
+        pltpu.make_async_copy(src, dst, loads.at[6 + i])
+        for i, (src, dst) in enumerate(((wg_ref, wg), (wx_ref, wx), (wb_ref, wb)))
+    ]
     last_loads = [
         pltpu.make_async_copy(src, dst, loads.at[i])
         for i, (src, dst) in enumerate(
@@ -1406,6 +1435,8 @@
 
     @pl.when(step == 0)
     def _():
+        for load in weight_loads:
+            load.start()
         place.meet(more=out_grads.ways.meet(False))
         for k in range(chips):
             out_red.start(k)
@@ -1417,6 +1448,12 @@
         wide, chans, dy, x, x_before, bd, bd_before, taps, heads, skip, enter,
         dx.at[chunk], dbd.at[chunk], dtaps, dheads, dskip, ext, gext, halo, dstate,
     )
+
+    @pl.when(step == 0)
+    def _():
+        for load in weight_loads:
+            load.wait()
+
     across = ((1,), (1,))
     total = dot(dgate[...], wg[...], across) + dot(dx[chunk], wx[...], across)
     part[chunk] = (total + dot(dbd[chunk], wb[...], across)).astype(BF16)
@@ -1425,15 +1462,16 @@
         for k in (place.chip + i, place.chip - i):
             pl.when((k >= 0) & (k < chips))(functools.partial(fn, k))
 
-    @pl.when(step == 0)
-    def _():
-        for i in range(chips - 1, 0, -1):
-            both_ways(i, out_red.collect)
-        out_red.collect(place.chip)
-
     for i in range(chips - 1, -1, -1):
 
-        @pl.when(step == steps - 1 - i * (steps - 3) // chips)
+        @pl.when(step == min(chips - 1 - i, chips - 2))
+        def _():
+            if i:
+                both_ways(i, out_red.collect)
+            else:
+                out_red.collect(place.chip)
+
+        @pl.when(step == min(chips + 2 - i, steps - 1))
         def _():
             if i:
                 both_ways(i, out_red.settle)
@@ -1485,21 +1523,30 @@
                 out[p] = value.astype(BF16).reshape(out.shape[1:])
             red.tree.start()
 
-        for n, (tx, red) in enumerate(x_reds):
-            terms(red, tx, dx[:, :, n * size : (n + 1) * size].reshape(rows_all, size))
-        dn_red.collect(jnp.int32(0))
-        terms(b_red, tb, dbd[...].reshape(rows_all, -1))
-        for k in range(chips - 1 - (steps - 1 - wait) // 2 - 1, 0, -1):
+        late = [
+            (red, tx, lambda n=n: dx[:, :, n * size : (n + 1) * size].reshape(rows_all, size))
+            for n, (tx, red) in enumerate(x_reds)
+        ]
+        late.append((b_red, tb, lambda: dbd[...].reshape(rows_all, -1)))
+        settles = list(range(chips - 1 - (steps - 1 - wait) // 2 - 1, -1, -1))
+        for turn in range(len(late) + levels):
+            for place_in, (red, out, values) in enumerate(late):
+                stage = turn - place_in
+                if stage == 0:
+                    terms(red, out, values())
+                elif 0 < stage <= levels:
+                    red.tree.step(stage - 1)
+                    if stage == levels:
+                        red.spread()
+            if turn == 0:
+                dn_red.collect(jnp.int32(0))
+                dn_red.settle(jnp.int32(settles.pop(0)))
+            elif turn == 2:
+                few.add()
+            if turn and settles:
+                dn_red.settle(jnp.int32(settles.pop(0)))
+        for k in settles:
             dn_red.settle(jnp.int32(k))
-        few.add()
-        late = [red for _, red in x_reds] + [b_red]
-        for i in range(levels):
-            for red in late:
-                red.tree.step(i)
-                if i == levels - 1:
-                    red.spread()
-            if i == 0:
-                dn_red.settle(jnp.int32(0))
         out_red.finish()
         hidden_out[...] = (hid[...].astype(F32) + out_red.total[...].astype(F32)).astype(BF16)
         out_grads.finish()
@@ -1560,7 +1607,7 @@
     cols, width = bd.shape[2], normed.shape[2]
     share = terms_gate.shape[2]
     groups = sp // seqs
-    pieces = 2 if chans % (2 * LANES) == 0 else 1
+    pieces = max(n for n in (1, 2, PIECES) if chans % (n * LANES) == 0)
     back = lambda i: blocks - 1 - i
     block = lambda n: pl.BlockSpec((None, rows, n), lambda i: (back(i), 0, 0))
     whole = lambda a: pl.BlockSpec(a.shape, lambda i: (0,) * a.ndim)
@@ -1593,7 +1640,8 @@
         vmem(normed),
         pltpu.VMEM((blocks, rows, width), BF16),
         vmem(hidden), vmem(cotangent), vmem(w_zx), vmem(w_bc), vmem(w_out),
-        dma(6),
+        vmem(wg), vmem(wx), vmem(wb),
+        dma(9),
         pltpu.VMEM((dp, sp, share, cols), BF16),
         pltpu.VMEM((sp, share, chans), BF16),
         pltpu.VMEM((sp, share, cols), BF16),
@@ -1616,9 +1664,9 @@
         in_specs=[
             block(chans), block(chans), before(chans), block(cols), before(cols), block(chans),
             pl.BlockSpec((None, states, chans), lambda i: (back(i), 0, 0)),
-            whole(taps), whole(heads), whole(skip), whole(norm), whole(wg), whole(wx), whole(wb),
+            whole(taps), whole(heads), whole(skip), whole(norm),
         ]
-        + [ANY] * 9,
+        + [ANY] * 12,
         out_specs=[whole(out) for out in outs],
         out_shape=outs,
         scratch_shapes=scratch,

time: 292 us -> 271 us (0.928)
  Pallas kernels: 291 us -> 270 us
    pallas_call x1, Pallas kernels: 144 us -> 121 us  [run_backward(): pl.pallas_call(functools.partial(backward_kernel, dp, sp, seqs, wide, cha...]
where the time goes in v6:
time: 271 us
  Pallas kernels  270 us (100%)
    pallas_call x1, Pallas kernels, run_forward(): pl.pallas_call(functools.partial(forward_kernel, dp, sp, seqs, wide, inne...  143 us
    pallas_call x1, Pallas kernels, run_backward(): pl.pallas_call(functools.partial(backward_kernel, dp, sp, seqs, wide, cha...  121 us

profile of v6, /device:TPU:0, one launch (start us, length us, event | category | flops | bytes accessed | tf_op | source)
XLA Modules:
  0.0 270.7 jit_solution(156867596932494457)
XLA Ops:
  0.6 1.5 pack.1.misc_ref
  2.1 143.1 %forward.1 = (bf16[8,128,1536]{2,1,0:T(8,128)(2,1)}, bf16[8,128,768]{2,1,0:T(8,128)(2,1)}, bf16[8,128,384]{2,1,0:T(8,128)(2,1)}, bf16[8,128,768]{2,1,0:T(8,128)(...) custom-call(bf16[48,6144]{1,0:T(8,128)(2,1)} %w_zx_ref.1, ...), custom_call_target="tpu_custom_call" | custom-call | tf_op jit(solution)/shard_map/forward/pallas_call | solution.py:1350
  145.2 121.3 %backward.1 = (bf16[2,128,1536]{2,1,0:T(8,128)(2,1)}, bf16[2,128,1536]{2,1,0:T(8,128)(2,1)}, f32[48,6144]{1,0:T(8,128)}, f32[48,256]{1,0:T(8,128)}, f32[4,48,128...) custom-call(bf16[8,128,768]{2,1,0:T(8,128)(2,1)} %get-tuple-element., ...), custom_call_target="tpu_custom_call" | custom-call | tf_op jit(solution)/shard_map/backward/pallas_call | solution.py:1661
  266.5 4.1 %finish.1 = (bf16[2,128,1536]{2,1,0:T(8,128)(2,1)}, bf16[2,128,1536]{2,1,0:T(8,128)(2,1)}, f32[48,6144]{1,0:T(8,128)}, f32[48,256]{1,0:T(8,128)}, f32[48,48]{1,0...) custom-call(bf16[2,128,1536]{2,1,0:T(8,128)(2,1)} %get-tuple-element, ...), custom_call_target="tpu_custom_call" | custom-call | tf_op jit(solution)/shard_map/finish/pallas_call | solution.py:1747
